TPU v7x, 32 devices: a whole 2x2x4 slice. The times are simulated.
32 devices in a mesh: freq: 2 (over core), tile: 16 (over z, y, x).
Axes of the slice: x: 2, y: 2, z: 4, core: 2. Of those that a mesh axis runs over, the one named last changes fastest.
Arguments:
- wave_in: bfloat16 [2, 4096, 2, 256], P(None, 'tile', None, 'freq'), may hold values from -6 to 6
- column_basis: bfloat16 [2, 32, 16, 256, 128], P('freq', None, 'tile'), may hold values from -0.25 to 0.25
- row_basis: bfloat16 [2, 32, 16, 256, 128], P('freq', 'tile'), may hold values from -0.1875 to 0.1875
- tile_scale: float32 [2, 32, 16], P('freq'), may hold values from 0.5 to 2
- tile_ranks: int32 [2, 32, 16], P('freq'), may hold values from 16 to 64, as said below
Outputs:
- forward_out: bfloat16 [2, 8192, 2, 256], P('freq', 'tile')
- adjoint_out: bfloat16 [2, 4096, 2, 256], P(None, 'tile', None, 'freq')
Inputs may be any that keep to these rules, and one draw needn't show every extreme that they name: `tile_ranks`: every entry is a multiple of 16. For each frequency, in each aligned group of 2 tile rows and 1 tile columns the ranks add up to at most 80, and some group reaches that sum.
All inputs are finite; a program needn't handle non-finite values.
Results may differ from a plain program's by a relative error of at most 0.005.
Values may be sent and summed in bfloat16 or wider, within the bound.
No kernel may reach another device: no remote copies, remote signals or barrier semaphores. Data moves between devices by JAX's collectives and lax.ppermute only.
A program may use at most 192 MiB of HBM per device.

v0:
```python
import jax
import jax.numpy as jnp
from jax import lax
from jax.sharding import PartitionSpec as P

NB = 256
RMAX = 64
MT_DEV = 2
NT_DEV = 1
NVS = 256
CAP = 5


def combine_conj(products):
    shaped = products.reshape(
        products.shape[:-3] + (products.shape[-3] // 32, 2, 16) + products.shape[-2:]
    )
    real_part = shaped[..., 0, :, 0, :] + shaped[..., 1, :, 1, :]
    imag_part = shaped[..., 0, :, 1, :] - shaped[..., 1, :, 0, :]
    return jnp.stack([real_part, imag_part], -3)


def combine_plain(summed):
    real_part = summed[..., 0, 0, :] - summed[..., 1, 1, :]
    imag_part = summed[..., 0, 1, :] + summed[..., 1, 0, :]
    return jnp.stack([real_part, imag_part], -2)


def pack_table(live_mask, capacity):
    counted = jnp.cumsum(live_mask.astype(jnp.int32), axis=1) - 1
    places = jnp.arange(capacity, dtype=jnp.int32)
    chosen = live_mask[:, None, :] & (counted[:, None, :] == places[None, :, None])
    return chosen.astype(jnp.bfloat16)


def per_device(wave_in, column_basis, row_basis, tile_scale, tile_ranks):
    tile_count = lax.axis_size("tile")
    my_index = lax.axis_index("tile")
    blocks = RMAX // 16
    base_width = 2 * RMAX
    slot_count = MT_DEV * NT_DEV * blocks
    wavefield = lax.all_to_all(wave_in, "freq", split_axis=0, concat_axis=3, tiled=True)
    column_bases = column_basis[0]
    row_bases = row_basis[0]
    scales = tile_scale[0]
    rank_table = tile_ranks[0]
    live_all = (16 * jnp.arange(blocks, dtype=jnp.int32))[None, None, :] < rank_table[:, :, None]
    weight_all = scales[:, :, None] * live_all.astype(jnp.float32)
    col_live = lax.dynamic_slice_in_dim(live_all, my_index * NT_DEV, NT_DEV, 1)
    col_weight = lax.dynamic_slice_in_dim(weight_all, my_index * NT_DEV, NT_DEV, 1)
    row_live = lax.dynamic_slice_in_dim(live_all, my_index * MT_DEV, MT_DEV, 0)
    row_weight = lax.dynamic_slice_in_dim(weight_all, my_index * MT_DEV, MT_DEV, 0)
    row_live = jnp.transpose(row_live.reshape(MT_DEV, tile_count, NT_DEV, blocks), (1, 0, 2, 3))
    row_weight = jnp.transpose(row_weight.reshape(MT_DEV, tile_count, NT_DEV, blocks), (1, 0, 2, 3))
    col_table = pack_table(col_live.reshape(tile_count, slot_count), CAP)
    row_table = pack_table(row_live.reshape(tile_count, slot_count), CAP)
    rows_split = row_bases.reshape(MT_DEV, tile_count, NT_DEV, NB, blocks, 2, 16)
    cols_split = column_bases.reshape(tile_count, MT_DEV, NT_DEV, NB, blocks, 2, 16)

    def pack_rows(sending, selector):
        flattened = sending.reshape(tile_count, slot_count, 32 * NVS)
        packed = jnp.einsum("aks,asf->akf", selector, flattened, preferred_element_type=jnp.float32)
        return packed.astype(jnp.bfloat16).reshape(tile_count, CAP, 2, 16, NVS)

    def unpack(received, selector):
        item_count = received.shape[-1]
        flattened = received.reshape(tile_count, received.shape[1], 32 * item_count)
        opened = jnp.einsum("aks,akf->asf", selector, flattened, preferred_element_type=jnp.float32)
        return opened.astype(jnp.bfloat16).reshape(
            tile_count, MT_DEV, NT_DEV, blocks, 2, 16, item_count
        )

    products = jnp.einsum(
        "mjbc,jbpn->mjcpn", column_bases, wavefield, preferred_element_type=jnp.float32
    )
    coded_rows = combine_conj(products) * col_weight[:, :, :, None, None, None]
    coded_rows = coded_rows.astype(jnp.bfloat16).reshape(tile_count, slot_count, 2, 16, NVS)
    summed = jnp.einsum(
        "isjbkqt,sijkptn->ibqpn",
        rows_split,
        unpack(
            lax.all_to_all(
                pack_rows(coded_rows, col_table), "tile", split_axis=0, concat_axis=0, tiled=True
            ),
            row_table,
        ),
        preferred_element_type=jnp.float32,
    )
    forward = combine_plain(summed).astype(jnp.bfloat16)
    back_products = jnp.einsum(
        "isjbc,ibpn->sijcpn",
        row_bases.reshape(MT_DEV, tile_count, NT_DEV, NB, base_width),
        forward,
        preferred_element_type=jnp.float32,
    )
    returned = combine_conj(back_products) * row_weight[:, :, :, :, None, None, None]
    returned = returned.astype(jnp.bfloat16).reshape(tile_count, slot_count, 2, 16, NVS)
    summed = jnp.einsum(
        "dijbkqt,dijkptn->jbqpn",
        cols_split,
        unpack(
            lax.all_to_all(
                pack_rows(returned, row_table), "tile", split_axis=0, concat_axis=0, tiled=True
            ),
            col_table,
        ),
        preferred_element_type=jnp.float32,
    )
    adjoint = combine_plain(summed).astype(jnp.bfloat16)
    adjoint_out = lax.all_to_all(adjoint, "freq", split_axis=3, concat_axis=0, tiled=True)
    forward_out = forward.reshape(1, MT_DEV * NB, 2, NVS)
    return (forward_out, adjoint_out)


def solution(mesh):
    return jax.shard_map(
        per_device,
        mesh=mesh,
        in_specs=(
            P(None, "tile", None, "freq"),
            P("freq", None, "tile", None, None),
            P("freq", "tile", None, None, None),
            P("freq", None, None),
            P("freq", None, None),
        ),
        out_specs=(P("freq", "tile", None, None), P(None, "tile", None, "freq")),
        check_vma=False,
    )
```

profile of v0, /device:TPU:9, one launch (start us, length us, event | category | flops | bytes accessed | tf_op | source)
XLA Modules:
  0.0 136.6 jit_solution(11709293905378083969)
XLA Ops:
  0.6 5.3 %all_to_all.43 = bf16[2,256,2,128]{3,2,1,0:T(2,128)(2,1)S(1)} all-to-all(bf16[2,256,2,128]{3,2,1,0:T(2,128)(2,1)} %param.5), channel_id=1, replica_groups=mesh['freq'=2,'tile'=16] {'freq'}, dimensions={0} | all-to-all | bytes 524288 | tf_op jit(solution)/shard_map/all_to_all | solution.py:42
  5.9 0.3 copy.78
  6.2 0.2 reshape.446
  6.4 2.9 %fusion.8 = f32[2,256,32,128]{1,3,2,0:T(8,128)S(1)} fusion(bf16[1,32,1,256,128]{4,3,2,1,0:T(8,128)(2,1)} %param.6, bf16[256,2,256,1]{2,0,1,3:T(8,128)(2,1)S(1)} %reshape.446), kind=kOutput, calls=%fused_computation.22 | convolution fusion | flops 1073741824 | bytes 10747904 | tf_op jit(solution)/shard_map/mjbc,jbpn->mjcpn/dot_general | solution.py:73
  9.3 0.5 fusion.3
  9.8 0.5 fusion.5
  10.3 0.5 pad_maximum_fusion
  10.7 2.6 %copy.82 = f32[32,1,4,2,16,256]{5,4,3,2,0,1:T(8,128)} copy(f32[32,1,4,2,16,256]{5,4,2,0,3,1:T(8,128)S(1)} %pad_maximum_fusion) | data formatting | bytes 8388608 | tf_op jit(solution)/shard_map/stack | solution.py:20
  13.4 5.0 %stack.36 = f32[16,8,8192]{2,1,0:T(8,128)} reshape(f32[32,1,4,2,16,256]{5,4,3,2,0,1:T(8,128)} %copy.82) | data formatting | bytes 8388608 | tf_op jit(solution)/shard_map/stack | solution.py:20
  18.3 0.0 copy-done.7
  18.4 0.1 copy.83
  18.4 0.0 copy-done.8
  18.4 0.1 copy.73
  18.5 0.1 broadcast_select_fusion
  18.6 0.2 dynamic-slice_reduce_fusion
  18.8 0.1 mul.52
  18.9 0.7 dynamic-slice_reduce_fusion.1
  19.6 0.1 and.24
  19.7 0.1 copy.76
  19.8 0.1 copy.77
  19.9 3.2 %convolution_convert_fusion.3 = bf16[16,5,8192]{2,1,0:T(8,128)(2,1)S(1)} fusion(f32[16,8,8192]{2,1,0:T(8,128)} %stack.36, f32[16,8]{1,0:T(8,128)S(1)} %mul.52, s32[16,8]{1,0:T(8,128)S(1)} %copy.77, pred[16,8]{1,0:T(8,128)(4,1)S(1)} %and.24), kind=kOutput, calls=%fused_computation.3 | convolution fusion | flops 13239552 | bytes 5506176 | tf_op jit(solution)/shard_map/aks,asf->akf/dot_general | solution.py:62
  23.1 2.7 %reshape.457 = bf16[16,5,2,16,256]{4,3,2,1,0:T(8,128)(2,1)} reshape(bf16[16,5,8192]{2,1,0:T(8,128)(2,1)S(1)} %convolution_convert_fusion.3) | data formatting | bytes 2621440 | tf_op jit(solution)/shard_map/reshape | solution.py:63
  25.7 6.8 %all-to-all-start.1 = ((bf16[16,5,2,16,256]{4,3,2,1,0:T(8,128)(2,1)}), bf16[16,5,2,16,256]{4,3,2,1,0:T(8,128)(2,1)S(1)}, u32[]{:S(2)}, u32[]{:S(2)}) async-start(bf16[16,5,2,16,256]{4,3,2,1,0:T(8,128)(2,1)} %reshape.457), calls=%async_computation.1 | async-start | bytes 2621440 | tf_op jit(solution)/shard_map/all_to_all | solution.py:82
  32.6 0.1 copy.74
  32.7 2.6 %copy.90 = bf16[1,2,16,256,128]{3,4,2,1,0:T(8,128)(2,1)} copy(bf16[1,2,16,256,128]{4,3,2,1,0:T(8,128)(2,1)S(1)} %copy-done.4) | data formatting | bytes 4194304 | tf_op args[2]
  35.3 0.1 copy.75
  35.4 0.1 copy.102
  35.4 27.0 %all-to-all-done.1 = bf16[16,5,2,16,256]{4,3,2,1,0:T(8,128)(2,1)S(1)} async-done(((bf16[16,5,2,16,256]{4,3,2,1,0:T(8,128)(2,1)}), bf16[16,5,2,16,256]{4,3,2,1,0:T(8,128)(2,1)S(1)}, u32[]{:S(2)}, u32[]{:S(2)}) %all-to-all-start.1) | async-done | bytes 1310752 | tf_op jit(solution)/shard_map/all_to_all | solution.py:82
  62.5 2.4 %reshape.458 = bf16[16,5,8192]{2,1,0:T(8,128)(2,1)} reshape(bf16[16,5,2,16,256]{4,3,2,1,0:T(8,128)(2,1)S(1)} %all-to-all-done.1) | data formatting | bytes 2621440 | tf_op jit(solution)/shard_map/reshape | solution.py:67
  64.8 2.4 %convolution_convert_fusion.2 = bf16[16,8,8192]{2,1,0:T(8,128)(2,1)S(1)} fusion(bf16[16,5,8192]{2,1,0:T(8,128)(2,1)} %reshape.458, s32[16,8]{1,0:T(8,128)S(1)} %copy.75, pred[16,8]{1,0:T(8,128)(4,1)S(1)} %copy.74), kind=kOutput, calls=%fused_computation.2 | convolution fusion | flops 11535616 | bytes 3408512 | tf_op jit(solution)/shard_map/aks,akf->asf/dot_general | solution.py:68
  67.3 0.6 copy.153
  67.9 1.0 copy-done.6
  68.9 1.3 fusion.13
  70.2 0.1 copy.170
  70.3 0.1 fusion.50
  70.4 1.1 copy-done.1
  71.6 0.6 copy-done.3
  72.1 0.1 fusion.49
  72.2 1.3 fusion.6
  73.5 0.5 fusion
  74.0 0.5 fusion.2
  74.5 0.8 pad_maximum_fusion.1
  75.3 2.6 %copy.101 = f32[16,2,1,4,2,16,256]{6,5,4,3,1,0,2:T(8,128)} copy(f32[16,2,1,4,2,16,256]{6,5,3,0,1,4,2:T(8,128)S(1)} %pad_maximum_fusion.1) | data formatting | bytes 8388608 | tf_op jit(solution)/shard_map/stack | solution.py:20
  77.9 5.0 %stack.42 = f32[16,8,8192]{2,1,0:T(8,128)} reshape(f32[16,2,1,4,2,16,256]{6,5,4,3,1,0,2:T(8,128)} %copy.101) | data formatting | bytes 8388608 | tf_op jit(solution)/shard_map/stack | solution.py:20
  82.8 2.9 %convolution_convert_fusion.1 = bf16[16,5,8192]{2,1,0:T(8,128)(2,1)S(1)} fusion(f32[16,8,8192]{2,1,0:T(8,128)} %stack.42, f32[16,8]{1,0:T(8,128)S(1)} %copy.102, s32[16,8]{1,0:T(8,128)S(1)} %copy.75, pred[16,8]{1,0:T(8,128)(4,1)S(1)} %copy.74), kind=kOutput, calls=%fused_computation.1 | convolution fusion | flops 13239552 | bytes 5506176 | tf_op jit(solution)/shard_map/aks,asf->akf/dot_general | solution.py:62
  85.8 2.7 %reshape.459 = bf16[16,5,2,16,256]{4,3,2,1,0:T(8,128)(2,1)} reshape(bf16[16,5,8192]{2,1,0:T(8,128)(2,1)S(1)} %convolution_convert_fusion.1) | data formatting | bytes 2621440 | tf_op jit(solution)/shard_map/reshape | solution.py:63
  88.5 5.5 %all-to-all-start.2 = ((bf16[16,5,2,16,256]{4,3,2,1,0:T(8,128)(2,1)}), bf16[16,5,2,16,256]{4,3,2,1,0:T(8,128)(2,1)S(1)}, u32[]{:S(2)}, u32[]{:S(2)}) async-start(bf16[16,5,2,16,256]{4,3,2,1,0:T(8,128)(2,1)} %reshape.459), calls=%async_computation.2 | async-start | bytes 2621440 | tf_op jit(solution)/shard_map/all_to_all | solution.py:102
  93.9 2.9 %copy.107 = bf16[1,32,1,256,128]{3,4,1,2,0:T(8,128)(2,1)} copy(bf16[1,32,1,256,128]{4,3,2,1,0:T(8,128)(2,1)S(1)} %copy-done) | data formatting | bytes 4194304 | tf_op args[1]
  96.8 1.4 %fusion.23 = bf16[2,256,1,1,256]{4,1,0,2,3:T(8,128)(2,1)S(1)} fusion(f32[2,256,2,2,256]{4,1,0,2,3:T(8,128)} %bitcast.170), kind=kLoop, calls=%fused_computation.35 | loop fusion | flops 262144 | bytes 1310720 | tf_op jit(solution)/shard_map/convert.10
  98.3 0.4 copy.96
  98.7 0.1 copy-done.2
  98.8 0.1 fusion.25
  98.8 0.4 copy.95
  99.2 2.0 %pad_maximum_fusion.2 = bf16[1,512,2,256]{3,2,1,0:T(2,128)(2,1)} fusion(bf16[1,512,1,256]{3,2,1,0:T(2,128)(2,1)S(1)} %copy.96, bf16[1,512,1,256]{3,2,1,0:T(2,128)(2,1)S(1)} %copy.95), kind=kLoop, calls=%fused_computation.40 | loop fusion | flops 1048576 | bytes 1048576 | tf_op jit(solution)/shard_map/stack | solution.py:26
  101.2 22.8 %all-to-all-done.2 = bf16[16,5,2,16,256]{4,3,2,1,0:T(8,128)(2,1)S(1)} async-done(((bf16[16,5,2,16,256]{4,3,2,1,0:T(8,128)(2,1)}), bf16[16,5,2,16,256]{4,3,2,1,0:T(8,128)(2,1)S(1)}, u32[]{:S(2)}, u32[]{:S(2)}) %all-to-all-start.2) | async-done | bytes 1310752 | tf_op jit(solution)/shard_map/all_to_all | solution.py:102
  124.0 1.4 %reshape.460 = bf16[16,5,8192]{2,1,0:T(8,128)(2,1)S(1)} reshape(bf16[16,5,2,16,256]{4,3,2,1,0:T(8,128)(2,1)S(1)} %all-to-all-done.2) | data formatting | bytes 2621440 | tf_op jit(solution)/shard_map/reshape | solution.py:67
  125.4 0.8 convolution_convert_fusion
  126.2 0.0 copy-start.5
  126.2 0.6 copy.154
  126.8 1.0 copy-done.5
  127.8 1.3 fusion.18
  129.2 0.3 copy.112
  129.4 6.2 %all_to_all.44 = bf16[1,256,2,256]{1,2,0,3:T(2,128)(2,1)S(1)} all-to-all(bf16[1,256,2,256]{1,2,0,3:T(2,128)(2,1)S(1)} %copy.112), channel_id=1, replica_groups=mesh['freq'=2,'tile'=16] {'freq'}, dimensions={3} | all-to-all | bytes 524288 | tf_op jit(solution)/shard_map/all_to_all | solution.py:110
  135.7 1.0 copy.113
  (22 shorter events, 0.2 us)
Async XLA Ops:
  13.3 5.0 %copy-start.7 = (f32[1,32,16]{1,2,0:T(8,128)S(1)}, f32[1,32,16]{1,2,0:T(8,128)}, u32[]{:S(2)}) copy-start(f32[1,32,16]{1,2,0:T(8,128)} %param.8) | copy-start | bytes 6148
  13.3 5.1 %copy-start.8 = (s32[1,32,16]{1,2,0:T(8,128)S(1)}, s32[1,32,16]{1,2,0:T(8,128)}, u32[]{:S(2)}) copy-start(s32[1,32,16]{1,2,0:T(8,128)} %param.9) | copy-start | bytes 6148
  25.7 6.9 %copy-start.4 = (bf16[1,2,16,256,128]{4,3,2,1,0:T(8,128)(2,1)S(1)}, bf16[1,2,16,256,128]{4,3,2,1,0:T(8,128)(2,1)}, u32[]{:S(2)}) copy-start(bf16[1,2,16,256,128]{4,3,2,1,0:T(8,128)(2,1)} %param.7) | copy-start | bytes 6291460
  25.7 36.7 %all-to-all-start.1 = ((bf16[16,5,2,16,256]{4,3,2,1,0:T(8,128)(2,1)}), bf16[16,5,2,16,256]{4,3,2,1,0:T(8,128)(2,1)S(1)}, u32[]{:S(2)}, u32[]{:S(2)}) async-start(bf16[16,5,2,16,256]{4,3,2,1,0:T(8,128)(2,1)} %reshape.457), calls=%async_computation.1 | async-start | bytes 2621440 | tf_op jit(solution)/shard_map/all_to_all | solution.py:82
  67.3 1.6 %copy-start.6 = (bf16[1,2,16,256,128]{3,4,2,1,0:T(8,128)(2,1)S(1)}, bf16[1,2,16,256,128]{3,4,2,1,0:T(8,128)(2,1)}, u32[]{:S(2)}) copy-start(bf16[1,2,16,256,128]{3,4,2,1,0:T(8,128)(2,1)} %copy.90) | copy-start | bytes 6291460
  70.2 1.4 %copy-start.1 = (f32[2,2,256,256,2,1,1]{2,3,5,1,0,4,6:T(8,128)}, f32[2,2,256,256,2,1,1]{2,3,5,1,0,4,6:T(8,128)S(1)}, u32[]{:S(2)}) copy-start(f32[2,2,256,256,2,1,1]{2,3,5,1,0,4,6:T(8,128)S(1)} %fusion.13) | copy-start | bytes 6291460
  70.3 1.8 %copy-start.3 = (f32[2,2,256,256,2,1,1]{2,3,0,4,1,5,6:T(8,128)}, f32[2,2,256,256,2,1,1]{2,3,0,4,1,5,6:T(8,128)S(1)}, u32[]{:S(2)}) copy-start(f32[2,2,256,256,2,1,1]{2,3,0,4,1,5,6:T(8,128)S(1)} %copy.170) | copy-start | bytes 6291460
  88.5 5.5 %copy-start = (bf16[1,32,1,256,128]{4,3,2,1,0:T(8,128)(2,1)S(1)}, bf16[1,32,1,256,128]{4,3,2,1,0:T(8,128)(2,1)}, u32[]{:S(2)}) copy-start(bf16[1,32,1,256,128]{4,3,2,1,0:T(8,128)(2,1)} %param.6) | copy-start | bytes 6291460
  88.5 35.5 %all-to-all-start.2 = ((bf16[16,5,2,16,256]{4,3,2,1,0:T(8,128)(2,1)}), bf16[16,5,2,16,256]{4,3,2,1,0:T(8,128)(2,1)S(1)}, u32[]{:S(2)}, u32[]{:S(2)}) async-start(bf16[16,5,2,16,256]{4,3,2,1,0:T(8,128)(2,1)} %reshape.459), calls=%async_computation.2 | async-start | bytes 2621440 | tf_op jit(solution)/shard_map/all_to_all | solution.py:102
  96.8 1.9 %copy-start.2 = (f32[2,2,256,256,2,1,1]{2,3,5,1,0,4,6:T(8,128)S(1)}, f32[2,2,256,256,2,1,1]{2,3,5,1,0,4,6:T(8,128)}, u32[]{:S(2)}) copy-start(f32[2,2,256,256,2,1,1]{2,3,5,1,0,4,6:T(8,128)} %copy-done.1) | copy-start | bytes 6291460
  126.2 1.6 %copy-start.5 = (bf16[1,32,1,256,128]{3,4,1,2,0:T(8,128)(2,1)S(1)}, bf16[1,32,1,256,128]{3,4,1,2,0:T(8,128)(2,1)}, u32[]{:S(2)}) copy-start(bf16[1,32,1,256,128]{3,4,1,2,0:T(8,128)(2,1)} %copy.107) | copy-start | bytes 6291460
where the time goes:
time: 137 us
  waiting for transfers between devices  49.8 us (36%)
  local copies, waits for them, and re-layouts  39 us (28%)
  matrix products  16.1 us (12%)
  starting transfers between devices  12.3 us (9%)
  blocking collectives  11.5 us (8%)
  other arithmetic  6.98 us (5%)
    all_to_all x1, waiting for transfers between devices, per_device(): lax.all_to_all(pack_rows(coded_rows, col_table), 'tile', split_axis=0, co...  27 us
    all_to_all x1, waiting for transfers between devices, per_device(): lax.all_to_all(pack_rows(returned, row_table), 'tile', split_axis=0, conc...  22.8 us
    another operation x4, local copies, waits for them, and re-layouts, combine_conj(): return jnp.stack([real_part, imag_part], -3)  15.2 us
    unnamed x22, local copies, waits for them, and re-layouts  10.5 us
    all_to_all x1, starting transfers between devices, per_device(): lax.all_to_all(pack_rows(coded_rows, col_table), 'tile', split_axis=0, co...  6.79 us
    all_to_all x1, blocking collectives, per_device(): lax.all_to_all(adjoint, 'freq', split_axis=3, concat_axis=0, tiled=True)  6.22 us
    dot_general x2, matrix products, pack_rows(): jnp.einsum('aks,asf->akf', selector, flattened, preferred_element_type=jn...  6.16 us
    all_to_all x1, starting transfers between devices, per_device(): lax.all_to_all(pack_rows(returned, row_table), 'tile', split_axis=0, conc...  5.48 us
  transfers between devices with their start and end apart: 2, of which 2 were waited for; matrix products, arithmetic and copies ran while one was open for 7% of the time, Pallas kernels for 0%

commit v1 on v0

v1 whole, which is shorter than its diff:
```python
import jax
import jax.numpy as jnp
from jax import lax
from jax.experimental import pallas as pl
from jax.experimental.pallas import tpu as pltpu
from jax.sharding import PartitionSpec as P

CAP = 5
RB = 16
VMEM = pl.BlockSpec(memory_space=pltpu.VMEM)
SMEM = pl.BlockSpec(memory_space=pltpu.SMEM)


def params():
    return pltpu.CompilerParams(vmem_limit_bytes=32 * 1024 * 1024)


def code_tiles(bases, waves, scales, first_blocks, store):
    coded = []
    for base, wave, scale in zip(bases, waves, scales):
        product = lax.dot_general(
            base, wave, (((0,), (0,)), ((), ())), preferred_element_type=jnp.float32
        )
        n = product.shape[1] // 2
        blocks = []
        for k in range(product.shape[0] // (2 * RB)):
            top = product[2 * RB * k : 2 * RB * k + RB]
            low = product[2 * RB * k + RB : 2 * RB * (k + 1)]
            both = jnp.concatenate([top[:, :n] + low[:, n:], top[:, n:] - low[:, :n]], 0)
            blocks.append((both * scale).astype(jnp.bfloat16))
        coded.append(blocks)
    for k, block in enumerate(coded[0]):
        store(min(k, CAP - 1), block)
    for k in reversed(range(len(coded[1]))):
        store(jnp.minimum(first_blocks + k, CAP - 1), coded[1][k])


def open_slots(load, counts, tile, blocks):
    rows = []
    for k in range(blocks):
        slot = min(k, CAP - 1) if tile == 0 else jnp.minimum(counts[0] + k, CAP - 1)
        block = load(slot)
        block = jnp.where(k < counts[tile], block, jnp.zeros_like(block))
        real, imag = block[:RB], block[RB:]
        rows.append(jnp.concatenate([real, imag], 1))
        rows.append(jnp.concatenate([-imag, real], 1))
    return jnp.concatenate(rows, 0)


def counts_of(ranks_ref, group, column):
    return ranks_ref[2 * group, column] // RB, ranks_ref[2 * group + 1, column] // RB


def coded_kernel(tiles, me_ref, ranks_ref, scale_ref, v_ref, x_ref, out_ref):
    me = me_ref[0]

    def step(r, carry):
        group = r
        first, _ = counts_of(ranks_ref, group, me)

        def store(slot, block):
            out_ref[r, slot] = block

        wave = x_ref[...]
        code_tiles(
            [v_ref[2 * group], v_ref[2 * group + 1]],
            [wave, wave],
            [scale_ref[2 * group, me], scale_ref[2 * group + 1, me]],
            first,
            store,
        )
        return carry

    lax.fori_loop(0, tiles, step, 0, unroll=4)


def middle_kernel(tiles, me_ref, ranks_ref, scale_ref, u_ref, in_ref, y_ref, out_ref, rhs):
    me = me_ref[0]
    blocks = u_ref.shape[3] // (2 * RB)
    depth = u_ref.shape[3]

    def unpack(r, carry):
        counts = counts_of(ranks_ref, me, r)
        for tile in range(2):
            rhs[tile, r] = open_slots(lambda slot: in_ref[r, slot], counts, tile, blocks)
        return carry

    lax.fori_loop(0, tiles, unpack, 0, unroll=2)
    for tile in range(2):

        def add(pair, total):
            left = jnp.concatenate([u_ref[tile, 2 * pair], u_ref[tile, 2 * pair + 1]], 1)
            right = jnp.concatenate([rhs[tile, 2 * pair], rhs[tile, 2 * pair + 1]], 0)
            return total + jnp.dot(left, right, preferred_element_type=jnp.float32)

        total = jnp.zeros(y_ref.shape[1:], jnp.float32)
        y_ref[tile] = lax.fori_loop(0, tiles // 2, add, total, unroll=8).astype(jnp.bfloat16)

    def back(r, carry):
        first, _ = counts_of(ranks_ref, me, r)

        def store(slot, block):
            out_ref[r, slot] = block

        code_tiles(
            [u_ref[0, r], u_ref[1, r]],
            [y_ref[0], y_ref[1]],
            [scale_ref[2 * me, r], scale_ref[2 * me + 1, r]],
            first,
            store,
        )
        return carry

    lax.fori_loop(0, tiles, back, 0, unroll=4)


def adjoint_kernel(tiles, me_ref, ranks_ref, v_ref, in_ref, z_ref):
    me = me_ref[0]
    blocks = v_ref.shape[2] // (2 * RB)

    def add(r, total):
        counts = counts_of(ranks_ref, r, me)
        right = jnp.concatenate(
            [open_slots(lambda slot: in_ref[r, slot], counts, t, blocks) for t in range(2)], 0
        )
        left = jnp.concatenate([v_ref[2 * r], v_ref[2 * r + 1]], 1)
        return total + jnp.dot(left, right, preferred_element_type=jnp.float32)

    total = lax.fori_loop(0, tiles, add, jnp.zeros(z_ref.shape, jnp.float32), unroll=4)
    z_ref[...] = total.astype(jnp.bfloat16)


def per_device(wave_in, column_basis, row_basis, tile_scale, tile_ranks):
    tiles = lax.axis_size("tile")
    core = lax.axis_index("freq")
    me = lax.axis_index("tile").astype(jnp.int32).reshape(1)
    v, u = column_basis[0].reshape(column_basis.shape[1], *column_basis.shape[3:]), row_basis[0]
    scales, ranks = tile_scale[0], tile_ranks[0]
    height, width, depth = v.shape[1], v.shape[2], 2 * RB
    half = wave_in.shape[3]
    n = 2 * half

    swap = [(0, 1), (1, 0)]
    mine = lax.dynamic_index_in_dim(wave_in, core, 0, keepdims=False)
    theirs = lax.dynamic_index_in_dim(wave_in, 1 - core, 0, keepdims=False)
    other = lax.ppermute(theirs, "freq", swap)
    x = jnp.concatenate([mine, other], 2).reshape(height, 2 * n)

    def send(blocks):
        return lax.all_to_all(blocks, "tile", split_axis=0, concat_axis=0, tiled=True)

    slots = jax.ShapeDtypeStruct((tiles, CAP, depth, n), jnp.bfloat16)
    coded = pl.pallas_call(
        lambda *refs: coded_kernel(tiles, *refs),
        out_shape=slots,
        in_specs=[SMEM, SMEM, SMEM, VMEM, VMEM],
        out_specs=VMEM,
        compiler_params=params(),
    )(me, ranks, scales, v, x)
    y, back = pl.pallas_call(
        lambda *refs: middle_kernel(tiles, *refs),
        out_shape=(jax.ShapeDtypeStruct((2, height, 2 * n), jnp.bfloat16), slots),
        in_specs=[SMEM, SMEM, SMEM, VMEM, VMEM],
        out_specs=(VMEM, VMEM),
        scratch_shapes=[pltpu.VMEM((2, tiles, width, 2 * n), jnp.bfloat16)],
        compiler_params=params(),
    )(me, ranks, scales, u, send(coded))
    z = pl.pallas_call(
        lambda *refs: adjoint_kernel(tiles, *refs),
        out_shape=jax.ShapeDtypeStruct((height, 2 * n), jnp.bfloat16),
        in_specs=[SMEM, SMEM, VMEM, VMEM],
        out_specs=VMEM,
        compiler_params=params(),
    )(me, ranks, v, send(back))

    def in_order(first, second):
        return jnp.where(core == 0, first, second), jnp.where(core == 0, second, first)

    y = y.reshape(2 * height, 2, n)
    forward_out = jnp.concatenate(in_order(y[:, :, :half], y[:, :, half:]), 2)[None]
    z = z.reshape(height, 2, n)
    adjoint_out = jnp.stack(in_order(z[:, :, :half], lax.ppermute(z[:, :, half:], "freq", swap)))
    return forward_out, adjoint_out


def solution(mesh):
    return jax.shard_map(
        per_device,
        mesh=mesh,
        in_specs=(
            P(None, "tile", None, "freq"),
            P("freq", None, "tile", None, None),
            P("freq", "tile", None, None, None),
            P("freq", None, None),
            P("freq", None, None),
        ),
        out_specs=(P("freq", "tile", None, None), P(None, "tile", None, "freq")),
        check_vma=False,
    )
```

time: 137 us -> 99.7 us (0.73)
  local copies, waits for them, and re-layouts: 39 us -> 9.96 us
  blocking collectives: 11.5 us -> 37.7 us
  waiting for transfers between devices: 49.8 us -> 28.1 us
  matrix products: 16.1 us -> 0 us
  Pallas kernels: 0 us -> 10.5 us
  starting transfers between devices: 12.3 us -> 7.83 us
  other arithmetic: 6.98 us -> 4.39 us
    all_to_all x2 -> x1, blocking collectives: 11.5 us -> 37.7 us  [send(): lax.all_to_all(blocks, 'tile', split_axis=0, concat_axis=0, tiled=True)]
    all_to_all x2 -> x1, waiting for transfers between devices: 49.8 us -> 28.1 us  [send(): lax.all_to_all(blocks, 'tile', split_axis=0, concat_axis=0, tiled=True)]
    another operation x7 -> x0, local copies, waits for them, and re-layouts: 16.3 us -> none  [the longest x4 15.2 us: combine_conj(): return jnp.stack([real_part, imag_part], -3)]
    dot_general x8 -> x0, matrix products: 16.1 us -> none  [the longest x2 6.16 us: pack_rows(): jnp.einsum('aks,asf->akf', selector, flattened, preferred_element_type=jn...]
    pallas_call x0 -> x3, Pallas kernels: none -> 10.5 us  [the longest x1 4.7 us: per_device(): pl.pallas_call(lambda *refs: middle_kernel(tiles, *refs), out_shape=(jax....]
    all_to_all x2 -> x1, starting transfers between devices: 12.3 us -> 4.39 us  [send(): lax.all_to_all(blocks, 'tile', split_axis=0, concat_axis=0, tiled=True)]
    reshape x5 -> x2, local copies, waits for them, and re-layouts: 9.28 us -> 2.98 us  [the longest x1 1.97 us: per_device(): y = y.reshape(2 * height, 2, n)]
    unnamed x22 -> x15, local copies, waits for them, and re-layouts: 10.5 us -> 5.73 us
  transfers between devices with their start and end apart: 2 -> 3, of which waited for: 2 -> 1; matrix products, arithmetic and copies ran while one was open for 7% -> 6% of each run, Pallas kernels for 0% -> 0%
where the time goes in v1:
time: 99.7 us; the launch traced here: 99.2 us
  blocking collectives  37.7 us (38%)
  waiting for transfers between devices  28.1 us (28%)
  Pallas kernels  10.5 us (11%)
  local copies, waits for them, and re-layouts  9.96 us (10%)
  starting transfers between devices  7.83 us (8%)
  other arithmetic  4.39 us (4%)
    all_to_all x1, blocking collectives, send(): lax.all_to_all(blocks, 'tile', split_axis=0, concat_axis=0, tiled=True)  37.7 us
    all_to_all x1, waiting for transfers between devices, send(): lax.all_to_all(blocks, 'tile', split_axis=0, concat_axis=0, tiled=True)  28.1 us
    unnamed x15, local copies, waits for them, and re-layouts  5.73 us
    pallas_call x1, Pallas kernels, per_device(): pl.pallas_call(lambda *refs: middle_kernel(tiles, *refs), out_shape=(jax....  4.7 us
    all_to_all x1, starting transfers between devices, send(): lax.all_to_all(blocks, 'tile', split_axis=0, concat_axis=0, tiled=True)  4.39 us
    pallas_call x1, Pallas kernels, per_device(): pl.pallas_call(lambda *refs: coded_kernel(tiles, *refs), out_shape=slots,...  2.99 us
    pallas_call x1, Pallas kernels, per_device(): pl.pallas_call(lambda *refs: adjoint_kernel(tiles, *refs), out_shape=jax....  2.76 us
    ppermute x1, starting transfers between devices, per_device(): lax.ppermute(z[:, :, half:], 'freq', swap)  2.7 us
  transfers between devices with their start and end apart: 3, of which 1 were waited for; matrix products, arithmetic and copies ran while one was open for 6% of the time, Pallas kernels for 0%

profile of v1, /device:TPU:9, one launch (start us, length us, event | category | flops | bytes accessed | tf_op | source)
XLA Modules:
  0.0 99.2 jit_solution(16976884675948089394)
XLA Ops:
  0.6 1.2 %dynamic-slice_bitcast_fusion.1 = (bf16[256,2,128]{2,1,0:T(2,128)(2,1)S(1)}, bf16[256,2,128]{2,1,0:T(2,128)(2,1)S(1)}) fusion(bf16[2,256,2,128]{3,2,1,0:T(2,128)(2,1)} %param.5, s32[]{:T(128)S(6)} %select_n.32, s32[]{:T(128)S(6)} %select_n.33), kind=kLoop, calls=%fused_computation.10 | loop fusion | bytes 524296 | tf_op jit(solution)/shard_map/jit(dynamic_index_in_dim)/squeeze | solution.py:144
  1.8 0.7 collective-permute-start
  2.5 0.8 copy.8
  3.3 0.8 copy.7
  4.1 0.0 collective-permute-done
  4.1 0.3 pad_maximum_fusion
  4.4 0.0 copy-start
  4.4 1.6 %copy-done = bf16[1,32,1,256,128]{4,3,2,1,0:T(8,128)(2,1)S(1)} copy-done((bf16[1,32,1,256,128]{4,3,2,1,0:T(8,128)(2,1)S(1)}, bf16[1,32,1,256,128]{4,3,2,1,0:T(8,128)(2,1)}, u32[]{:S(2)}) %copy-start) | copy-done | bytes 2097176
  6.0 3.0 %shard_map.68 = bf16[16,5,32,256]{3,2,1,0:T(8,128)(2,1)S(1)} custom-call(s32[1]{0:T(128)} %bitcast.refs_0_, s32[32,16]{1,0:T(8,128)S(1)} %bitcast.21, f32[32,16]{1,0:T(8,128)S(1)} %bitcast.24, bf16[32,256,128]{2,1,0:T(8,128)(2,1)S(1)} %bitcast.17, bf16[256,512]{1,0:T(8,128)(2,1)S(1)} %bitcast.20), custom_call_target="tpu_custom_call" | custom-call | tf_op jit(solution)/shard_map/pallas_call | solution.py:153
  9.0 0.0 copy-start.2
  9.0 37.7 %all_to_all.10.refs_4_ = bf16[16,5,32,256]{3,2,1,0:T(8,128)(2,1)S(1)} all-to-all(bf16[16,5,32,256]{3,2,1,0:T(8,128)(2,1)S(1)} %shard_map.68), channel_id=1, replica_groups=mesh['freq'=2,'tile'=16] {'tile'}, dimensions={0} | all-to-all | bytes 2621440 | tf_op jit(solution)/shard_map/all_to_all | solution.py:150
  46.7 0.0 copy-done.2
  46.7 4.7 %shard_map.69 = (bf16[2,256,512]{2,1,0:T(8,128)(2,1)S(1)}, bf16[16,5,32,256]{3,2,1,0:T(8,128)(2,1)S(1)}) custom-call(s32[1]{0:T(128)} %bitcast.refs_0_, s32[32,16]{1,0:T(8,128)S(1)} %bitcast.22, f32[32,16]{1,0:T(8,128)S(1)} %bitcast.25, bf16[2,16,256,128]{3,2,1,0:T(8,128)(2,1)S(1)} %bitcast.19, bf16[16,5,32,256]{3,2,1,0:T(8,128)(2,1)S(1)} %all_to_all.10.refs_4_), custom_call_target="tpu_custom_call" | custom-call | tf_op jit(solution)/shard_map/pallas_call | solution.py:160
  51.5 0.0 copy-start.3
  51.5 1.1 %copy-done.3 = bf16[16,5,32,256]{3,2,1,0:T(8,128)(2,1)} copy-done((bf16[16,5,32,256]{3,2,1,0:T(8,128)(2,1)}, bf16[16,5,32,256]{3,2,1,0:T(8,128)(2,1)S(1)}, u32[]{:S(2)}) %copy-start.3) | copy-done | bytes 1310744
  52.5 0.0 copy-start.5
  52.5 0.8 copy-done.5
  53.3 0.0 copy-start.1
  53.3 4.4 %all-to-all-start.1 = ((bf16[16,5,32,256]{3,2,1,0:T(8,128)(2,1)}), bf16[16,5,32,256]{3,2,1,0:T(8,128)(2,1)S(1)}, u32[]{:S(2)}, u32[]{:S(2)}) async-start(bf16[16,5,32,256]{3,2,1,0:T(8,128)(2,1)} %copy-done.3), calls=%async_computation.1 | async-start | bytes 2621440 | tf_op jit(solution)/shard_map/all_to_all | solution.py:150
  57.7 2.0 %reshape.18 = bf16[512,2,256]{2,1,0:T(2,128)(2,1)} reshape(bf16[2,256,512]{2,1,0:T(8,128)(2,1)} %copy-done.5) | data formatting | bytes 1048576 | tf_op jit(solution)/shard_map/reshape | solution.py:179
  59.7 28.1 %all-to-all-done.1.refs_3_ = bf16[16,5,32,256]{3,2,1,0:T(8,128)(2,1)S(1)} async-done(((bf16[16,5,32,256]{3,2,1,0:T(8,128)(2,1)}), bf16[16,5,32,256]{3,2,1,0:T(8,128)(2,1)S(1)}, u32[]{:S(2)}, u32[]{:S(2)}) %all-to-all-start.1) | async-done | bytes 1310752 | tf_op jit(solution)/shard_map/all_to_all | solution.py:150
  87.8 0.0 copy-done.1
  87.8 2.8 %shard_map.70 = bf16[256,512]{1,0:T(8,128)(2,1)S(1)} custom-call(s32[1]{0:T(128)} %bitcast.refs_0_, s32[32,16]{1,0:T(8,128)S(1)} %bitcast.23, bf16[32,256,128]{2,1,0:T(8,128)(2,1)S(1)} %bitcast.18, bf16[16,5,32,256]{3,2,1,0:T(8,128)(2,1)S(1)} %all-to-all-done.1.refs_3_), custom_call_target="tpu_custom_call" | custom-call | tf_op jit(solution)/shard_map/pallas_call | solution.py:168
  90.6 0.0 copy-start.4
  90.6 0.7 copy-done.4
  91.3 1.0 %reshape.19 = bf16[256,2,256]{2,1,0:T(2,128)(2,1)S(1)} reshape(bf16[256,512]{1,0:T(8,128)(2,1)} %copy-done.4) | data formatting | bytes 524288 | tf_op jit(solution)/shard_map/reshape | solution.py:181
  92.3 0.1 slice.19
  92.4 2.7 %collective-permute-start.1 = (bf16[256,2,128]{2,1,0:T(2,128)(2,1)S(1)}, bf16[256,2,128]{2,1,0:T(2,128)(2,1)S(1)}, u32[]{:S(2)}, u32[]{:S(2)}) collective-permute-start(bf16[256,2,128]{2,1,0:T(2,128)(2,1)S(1)} %slice.19), channel_id=1, source_target_pairs={{0,16},{16,0},{1,17},{17,1},{2,18},{18,2},{3,19},{19,3},{4,20},{20... | collective-permute-start | bytes 393224 | tf_op jit(solution)/shard_map/ppermute | solution.py:182
  95.1 1.5 %broadcast_select_fusion.1 = (bf16[512,2,128]{2,1,0:T(2,128)(2,1)S(1)}, bf16[512,2,128]{2,1,0:T(2,128)(2,1)S(1)}) fusion(pred[]{:T(512)S(6)} %eq.2, bf16[512,2,256]{2,1,0:T(2,128)(2,1)} %reshape.18), kind=kLoop, calls=%fused_computation.2 | loop fusion | flops 262144 | bytes 1048577 | tf_op jit(solution)/shard_map/jit(_where)/select_n | solution.py:177
  96.6 1.4 %maximum_bitcast_fusion = bf16[1,512,2,256]{3,2,1,0:T(2,128)(2,1)} fusion(bf16[512,2,128]{2,1,0:T(2,128)(2,1)S(1)} %get-tuple-element.7, bf16[512,2,128]{2,1,0:T(2,128)(2,1)S(1)} %get-tuple-element.6), kind=kLoop, calls=%fused_computation | loop fusion | flops 1048576 | bytes 1048576 | tf_op jit(solution)/shard_map/broadcast_in_dim | solution.py:180
  98.0 0.0 collective-permute-done.1
  98.0 0.2 fusion
  98.2 1.1 %pad_maximum_fusion.1 = bf16[2,256,2,128]{3,2,1,0:T(2,128)(2,1)} fusion(bf16[1,256,2,128]{3,2,1,0:T(2,128)(2,1)S(1)} %get-tuple-element.9, bf16[1,256,2,128]{3,2,1,0:T(2,128)(2,1)S(1)} %get-tuple-element.8), kind=kLoop, calls=%fused_computation.4 | loop fusion | flops 131072 | bytes 524288 | tf_op jit(solution)/shard_map/stack | solution.py:182
  (1 shorter events, 0.0 us)
Async XLA Ops:
  1.8 2.3 %collective-permute-start = (bf16[256,2,128]{2,1,0:T(2,128)(2,1)S(1)}, bf16[256,2,128]{2,1,0:T(2,128)(2,1)S(1)}, u32[]{:S(2)}, u32[]{:S(2)}) collective-permute-start(bf16[256,2,128]{2,1,0:T(2,128)(2,1)S(1)} %get-tuple-element.11), channel_id=1, source_target_pairs={{0,16},{16,0},{1,17},{17,1},{2,18},{18,2},{3,19},{19,3},{4,20},{20... | collective-permute-start | bytes 393224 | tf_op jit(solution)/shard_map/ppermute | solution.py:146
  4.4 1.6 %copy-start = (bf16[1,32,1,256,128]{4,3,2,1,0:T(8,128)(2,1)S(1)}, bf16[1,32,1,256,128]{4,3,2,1,0:T(8,128)(2,1)}, u32[]{:S(2)}) copy-start(bf16[1,32,1,256,128]{4,3,2,1,0:T(8,128)(2,1)} %param.6) | copy-start | bytes 6291460
  9.0 37.8 %copy-start.2 = (bf16[1,2,16,256,128]{4,3,2,1,0:T(8,128)(2,1)S(1)}, bf16[1,2,16,256,128]{4,3,2,1,0:T(8,128)(2,1)}, u32[]{:S(2)}) copy-start(bf16[1,2,16,256,128]{4,3,2,1,0:T(8,128)(2,1)} %param.7) | copy-start | bytes 6291460
  51.5 1.1 %copy-start.3 = (bf16[16,5,32,256]{3,2,1,0:T(8,128)(2,1)}, bf16[16,5,32,256]{3,2,1,0:T(8,128)(2,1)S(1)}, u32[]{:S(2)}) copy-start(bf16[16,5,32,256]{3,2,1,0:T(8,128)(2,1)S(1)} %get-tuple-element.5) | copy-start | bytes 3932164
  52.5 0.8 copy-start.5
  53.3 34.5 %copy-start.1 = (bf16[1,32,1,256,128]{4,3,2,1,0:T(8,128)(2,1)S(1)}, bf16[1,32,1,256,128]{4,3,2,1,0:T(8,128)(2,1)}, u32[]{:S(2)}) copy-start(bf16[1,32,1,256,128]{4,3,2,1,0:T(8,128)(2,1)} %param.6) | copy-start | bytes 6291460
  53.3 34.5 %all-to-all-start.1 = ((bf16[16,5,32,256]{3,2,1,0:T(8,128)(2,1)}), bf16[16,5,32,256]{3,2,1,0:T(8,128)(2,1)S(1)}, u32[]{:S(2)}, u32[]{:S(2)}) async-start(bf16[16,5,32,256]{3,2,1,0:T(8,128)(2,1)} %copy-done.3), calls=%async_computation.1 | async-start | bytes 2621440 | tf_op jit(solution)/shard_map/all_to_all | solution.py:150
  90.6 0.7 copy-start.4
  92.4 5.5 %collective-permute-start.1 = (bf16[256,2,128]{2,1,0:T(2,128)(2,1)S(1)}, bf16[256,2,128]{2,1,0:T(2,128)(2,1)S(1)}, u32[]{:S(2)}, u32[]{:S(2)}) collective-permute-start(bf16[256,2,128]{2,1,0:T(2,128)(2,1)S(1)} %slice.19), channel_id=1, source_target_pairs={{0,16},{16,0},{1,17},{17,1},{2,18},{18,2},{3,19},{19,3},{4,20},{20... | collective-permute-start | bytes 393224 | tf_op jit(solution)/shard_map/ppermute | solution.py:182

commit v2 on v1

v2 whole, which is shorter than its diff:
```python
import jax
import jax.numpy as jnp
from jax import lax
from jax.experimental import pallas as pl
from jax.experimental.pallas import tpu as pltpu
from jax.sharding import PartitionSpec as P

CAP = 5
RB = 16
VMEM = pl.BlockSpec(memory_space=pltpu.VMEM)
SMEM = pl.BlockSpec(memory_space=pltpu.SMEM)


def params():
    return pltpu.CompilerParams(vmem_limit_bytes=32 * 1024 * 1024)


def code_tiles(bases, waves, scales, first_blocks, store):
    coded = []
    for base, wave, scale in zip(bases, waves, scales):
        product = lax.dot_general(
            base, wave, (((0,), (0,)), ((), ())), preferred_element_type=jnp.float32
        )
        n = product.shape[1] // 2
        blocks = []
        for k in range(product.shape[0] // (2 * RB)):
            top = product[2 * RB * k : 2 * RB * k + RB]
            low = product[2 * RB * k + RB : 2 * RB * (k + 1)]
            both = jnp.concatenate([top[:, :n] + low[:, n:], top[:, n:] - low[:, :n]], 0)
            blocks.append((both * scale).astype(jnp.bfloat16))
        coded.append(blocks)
    for k, block in enumerate(coded[0]):
        store(min(k, CAP - 1), block)
    for k in reversed(range(len(coded[1]))):
        store(jnp.minimum(first_blocks + k, CAP - 1), coded[1][k])


def open_slots(load, counts, tile, blocks):
    rows = []
    for k in range(blocks):
        slot = min(k, CAP - 1) if tile == 0 else jnp.minimum(counts[0] + k, CAP - 1)
        block = load(slot)
        block = jnp.where(k < counts[tile], block, jnp.zeros_like(block))
        real, imag = block[:RB], block[RB:]
        rows.append(jnp.concatenate([real, imag], 1))
        rows.append(jnp.concatenate([-imag, real], 1))
    return jnp.concatenate(rows, 0)


def counts_of(ranks_ref, group, column):
    return ranks_ref[2 * group, column] // RB, ranks_ref[2 * group + 1, column] // RB


def far_first(tiles):
    bits = tiles.bit_length() - 1
    low, high = 2 ** (bits // 2), 2 ** (bits - bits // 2)
    return high, low, low, 1


def near_first(tiles):
    count_a, s1, count_b, s2 = far_first(tiles)
    return count_b, s2, count_a, s1


def at_once(tiles):
    return None


def exchange(blocks, route, tiles):
    if route is None:
        return [lax.all_to_all(blocks[0], "tile", split_axis=0, concat_axis=0, tiled=True)]
    count_a, s1, count_b, s2 = route

    def swap(block, offset):
        return lax.ppermute(block, "tile", [(i, i ^ offset) for i in range(tiles)])

    hops = {a: swap(blocks[a], a * s1) for a in reversed(range(1, count_a))}
    first = [blocks[0]] + [hops[a] for a in range(1, count_a)]
    hops = {
        b: swap(jnp.stack([first[a][b] for a in range(count_a)]), b * s2)
        for b in reversed(range(1, count_b))
    }
    return first + [hops[b] for b in range(1, count_b)]


def shapes_sent(route, tiles, shape):
    if route is None:
        return [jax.ShapeDtypeStruct((tiles,) + shape, jnp.bfloat16)]
    return [jax.ShapeDtypeStruct((route[2],) + shape, jnp.bfloat16)] * route[0]


def n_arrays(route):
    return 1 if route is None else route[0] + route[2] - 1


def each_arrival(route, me, refs, visit):
    if route is None:

        def direct(i, carry):
            visit(i, lambda slot: refs[0][i, slot])
            return carry

        lax.fori_loop(0, refs[0].shape[0], direct, 0, unroll=4)
        return
    count_a, s1, count_b, s2 = route
    for a in range(count_a):
        visit(me ^ (a * s1), lambda slot, a=a: refs[a][0, slot])
    for b in range(1, count_b):
        ref = refs[count_a + b - 1]

        def step(a, carry, ref=ref, b=b):
            visit(me ^ (a * s1) ^ (b * s2), lambda slot: ref[a, slot])
            return carry

        lax.fori_loop(0, count_a, step, 0, unroll=4)


def each_departure(route, me, refs, visit):
    for a, ref in enumerate(refs):

        def step(b, carry, ref=ref, a=a):
            def store(slot, block):
                ref[b, slot] = block

            visit(b if route is None else me ^ (a * route[1]) ^ (b * route[3]), store)
            return carry

        lax.fori_loop(0, ref.shape[0], step, 0, unroll=4)


def coded_kernel(route, me_ref, ranks_ref, scale_ref, v_ref, x_ref, *out_refs):
    me = me_ref[0]

    def visit(group, store):
        first, _ = counts_of(ranks_ref, group, me)
        wave = x_ref[...]
        code_tiles(
            [v_ref[2 * group], v_ref[2 * group + 1]],
            [wave, wave],
            [scale_ref[2 * group, me], scale_ref[2 * group + 1, me]],
            first,
            store,
        )

    each_departure(route, me, out_refs, visit)


def middle_kernel(route_in, route_out, tiles, *refs):
    me_ref, ranks_ref, scale_ref, u_ref = refs[:4]
    in_refs, y_ref, out_refs, rhs = (
        refs[4 : 4 + n_arrays(route_in)],
        refs[4 + n_arrays(route_in)],
        refs[5 + n_arrays(route_in) : -1],
        refs[-1],
    )
    me = me_ref[0]
    blocks = u_ref.shape[3] // (2 * RB)

    def unpack(column, load):
        counts = counts_of(ranks_ref, me, column)
        for tile in range(2):
            rhs[tile, column] = open_slots(load, counts, tile, blocks)

    each_arrival(route_in, me, in_refs, unpack)
    for tile in range(2):

        def add(pair, total):
            left = jnp.concatenate([u_ref[tile, 2 * pair], u_ref[tile, 2 * pair + 1]], 1)
            right = jnp.concatenate([rhs[tile, 2 * pair], rhs[tile, 2 * pair + 1]], 0)
            return total + jnp.dot(left, right, preferred_element_type=jnp.float32)

        total = jnp.zeros(y_ref.shape[1:], jnp.float32)
        y_ref[tile] = lax.fori_loop(0, tiles // 2, add, total, unroll=8).astype(jnp.bfloat16)

    def visit(column, store):
        first, _ = counts_of(ranks_ref, me, column)
        code_tiles(
            [u_ref[0, column], u_ref[1, column]],
            [y_ref[0], y_ref[1]],
            [scale_ref[2 * me, column], scale_ref[2 * me + 1, column]],
            first,
            store,
        )

    each_departure(route_out, me, out_refs, visit)


def adjoint_kernel(route, tiles, *refs):
    me_ref, ranks_ref, v_ref, in_refs, z_ref, rhs = *refs[:3], refs[3:-2], *refs[-2:]
    me = me_ref[0]
    blocks = v_ref.shape[2] // (2 * RB)

    def unpack(group, load):
        counts = counts_of(ranks_ref, group, me)
        rhs[group] = jnp.concatenate([open_slots(load, counts, t, blocks) for t in range(2)], 0)

    each_arrival(route, me, in_refs, unpack)

    def add(group, total):
        left = jnp.concatenate([v_ref[2 * group], v_ref[2 * group + 1]], 1)
        return total + jnp.dot(left, rhs[group], preferred_element_type=jnp.float32)

    total = lax.fori_loop(0, tiles, add, jnp.zeros(z_ref.shape, jnp.float32), unroll=8)
    z_ref[...] = total.astype(jnp.bfloat16)


def order_rows_kernel(core_ref, first_ref, second_ref, out_ref):
    n = first_ref.shape[1] // 2
    swapped = core_ref[0] == 1
    first, second = first_ref[...], second_ref[...]
    low = jnp.where(swapped, second, first)
    high = jnp.where(swapped, first, second)
    out_ref[:, 0 * n : 1 * n] = low[:, :n]
    out_ref[:, 1 * n : 2 * n] = high[:, :n]
    out_ref[:, 2 * n : 3 * n] = low[:, n:]
    out_ref[:, 3 * n : 4 * n] = high[:, n:]


def order_parts_kernel(core_ref, first_ref, second_ref, out_ref):
    out_ref[core_ref[0]] = first_ref[...]
    out_ref[1 - core_ref[0]] = second_ref[...]


WAYS = {"1a": far_first, "1b": near_first, "2a": far_first, "2b": near_first}


def per_device(wave_in, column_basis, row_basis, tile_scale, tile_ranks):
    tiles = lax.axis_size("tile")
    core = lax.axis_index("freq").astype(jnp.int32)
    core_at = core.reshape(1)
    me = lax.axis_index("tile").astype(jnp.int32).reshape(1)
    v = column_basis.reshape(column_basis.shape[1], *column_basis.shape[3:])
    u = row_basis[0]
    scales, ranks = tile_scale[0], tile_ranks[0]
    height, width = v.shape[1], v.shape[2]
    n = wave_in.shape[3]
    slots = (CAP, 2 * RB, n)
    swap = [(0, 1), (1, 0)]
    way = {name: pick(tiles) for name, pick in WAYS.items()}

    def cost(products, operands):
        return pl.CostEstimate(
            flops=4 * products * tiles * height * width * 2 * n,
            bytes_accessed=sum(a.size * a.dtype.itemsize for a in operands),
            transcendentals=0,
        )

    def code(x, route):
        shapes = shapes_sent(route, tiles, slots)
        return pl.pallas_call(
            lambda *refs: coded_kernel(route, *refs),
            out_shape=shapes,
            in_specs=[SMEM, SMEM, SMEM, VMEM, VMEM],
            out_specs=[VMEM] * len(shapes),
            compiler_params=params(),
            cost_estimate=cost(1, [v, x]),
        )(me, ranks, scales, v, x)

    def middle(arrived, route_in, route_out):
        shapes = shapes_sent(route_out, tiles, slots)
        result = pl.pallas_call(
            lambda *refs: middle_kernel(route_in, route_out, tiles, *refs),
            out_shape=[jax.ShapeDtypeStruct((2, height, 2 * n), jnp.bfloat16)] + shapes,
            in_specs=[SMEM, SMEM, SMEM, VMEM] + [VMEM] * len(arrived),
            out_specs=[VMEM] * (1 + len(shapes)),
            scratch_shapes=[pltpu.VMEM((2, tiles, width, 2 * n), jnp.bfloat16)],
            compiler_params=params(),
            cost_estimate=cost(2, [u, *arrived]),
        )(me, ranks, scales, u, *arrived)
        return result[0].reshape(2 * height, 2 * n), result[1:]

    def adjoint(arrived, route):
        return pl.pallas_call(
            lambda *refs: adjoint_kernel(route, tiles, *refs),
            out_shape=jax.ShapeDtypeStruct((height, 2 * n), jnp.bfloat16),
            in_specs=[SMEM, SMEM, VMEM] + [VMEM] * len(arrived),
            out_specs=VMEM,
            scratch_shapes=[pltpu.VMEM((tiles, 2 * width, 2 * n), jnp.bfloat16)],
            compiler_params=params(),
            cost_estimate=cost(1, [v, *arrived]),
        )(me, ranks, v, *arrived)

    def ordered(kernel, first, second, shape):
        return pl.pallas_call(
            kernel,
            out_shape=jax.ShapeDtypeStruct(shape, jnp.bfloat16),
            in_specs=[SMEM, VMEM, VMEM],
            out_specs=VMEM,
            compiler_params=params(),
        )(core_at, first, second)

    theirs = lax.dynamic_index_in_dim(wave_in, 1 - core, 0, keepdims=False)
    mine = lax.dynamic_index_in_dim(wave_in, core, 0, keepdims=False)
    other = lax.ppermute(theirs, "freq", swap)
    coded_a = exchange(code(mine.reshape(height, 2 * n), way["1a"]), way["1a"], tiles)
    coded_b = exchange(code(other.reshape(height, 2 * n), way["1b"]), way["1b"], tiles)
    y_a, back_a = middle(coded_a, way["1a"], way["2a"])
    back_a = exchange(back_a, way["2a"], tiles)
    y_b, back_b = middle(coded_b, way["1b"], way["2b"])
    back_b = exchange(back_b, way["2b"], tiles)
    z_a = adjoint(back_a, way["2a"])
    z_b = lax.ppermute(adjoint(back_b, way["2b"]), "freq", swap)
    forward_out = ordered(order_rows_kernel, y_a, y_b, (2 * height, 4 * n))
    adjoint_out = ordered(order_parts_kernel, z_a, z_b, (2, height, 2 * n))
    return forward_out.reshape(1, 2 * height, 2, 2 * n), adjoint_out.reshape(2, height, 2, n)


def solution(mesh):
    return jax.shard_map(
        per_device,
        mesh=mesh,
        in_specs=(
            P(None, "tile", None, "freq"),
            P("freq", None, "tile", None, None),
            P("freq", "tile", None, None, None),
            P("freq", None, None),
            P("freq", None, None),
        ),
        out_specs=(P("freq", "tile", None, None), P(None, "tile", None, "freq")),
        check_vma=False,
    )
```

time: 99.7 us -> 89.9 us (0.902)
  blocking collectives: 37.7 us -> 0 us
  starting transfers between devices: 7.83 us -> 30.1 us
  waiting for transfers between devices: 28.1 us -> 34 us
  Pallas kernels: 10.5 us -> 15.9 us
  local copies, waits for them, and re-layouts: 9.96 us -> 6.17 us
  other arithmetic: 4.39 us -> 2.28 us
    all_to_all x1 -> x0, blocking collectives: 37.7 us -> none  [send(): lax.all_to_all(blocks, 'tile', split_axis=0, concat_axis=0, tiled=True)]
    ppermute x1 -> x25, waiting for transfers between devices: 0.01 us -> 34 us  [the longest x24 34 us: swap(): return lax.ppermute(block, 'tile', [(i, i ^ offset) for i in range(tiles)])]
    all_to_all x1 -> x0, waiting for transfers between devices: 28.1 us -> none  [send(): lax.all_to_all(blocks, 'tile', split_axis=0, concat_axis=0, tiled=True)]
    ppermute x1 -> x25, starting transfers between devices: 2.7 us -> 29.4 us  [the longest x24 26.7 us: swap(): return lax.ppermute(block, 'tile', [(i, i ^ offset) for i in range(tiles)])]
    pallas_call x3 -> x8, Pallas kernels: 10.5 us -> 15.9 us  [the longest x2 6.02 us: middle(): pl.pallas_call(lambda *refs: middle_kernel(route_in, route_out, tiles, *r...]
    all_to_all x1 -> x0, starting transfers between devices: 4.39 us -> none  [send(): lax.all_to_all(blocks, 'tile', split_axis=0, concat_axis=0, tiled=True)]
    unnamed x15 -> x10, local copies, waits for them, and re-layouts: 5.73 us -> 3.18 us
    select_n x1 -> x0, other arithmetic: 1.47 us -> none  [in_order(): jnp.where(core == 0, first, second)]
  transfers between devices with their start and end apart: 3 -> 26, of which waited for: 1 -> 8; matrix products, arithmetic and copies ran while one was open for 6% -> 6% of each run, Pallas kernels for 0% -> 17%
where the time goes in v2:
time: 89.9 us; the launch traced here: 89.4 us
  waiting for transfers between devices  34 us (38%)
  starting transfers between devices  30.1 us (33%)
  Pallas kernels  15.9 us (18%)
  local copies, waits for them, and re-layouts  6.17 us (7%)
  other arithmetic  2.28 us (3%)
  between operations  1 us (1%)
    ppermute x24, waiting for transfers between devices, swap(): return lax.ppermute(block, 'tile', [(i, i ^ offset) for i in range(tiles)])  34 us
    ppermute x24, starting transfers between devices, swap(): return lax.ppermute(block, 'tile', [(i, i ^ offset) for i in range(tiles)])  26.7 us
    pallas_call x2, Pallas kernels, middle(): pl.pallas_call(lambda *refs: middle_kernel(route_in, route_out, tiles, *r...  6.02 us
    pallas_call x2, Pallas kernels, adjoint(): pl.pallas_call(lambda *refs: adjoint_kernel(route, tiles, *refs), out_sha...  5.17 us
    pallas_call x2, Pallas kernels, code(): pl.pallas_call(lambda *refs: coded_kernel(route, *refs), out_shape=shapes...  3.68 us
    unnamed x10, local copies, waits for them, and re-layouts  3.18 us
    ppermute x1, starting transfers between devices, per_device(): z_b = lax.ppermute(adjoint(back_b, way['2b']), 'freq', swap)  2.68 us
    another operation x12, other arithmetic, exchange(): jnp.stack([first[a][b] for a in range(count_a)])  2.28 us
  transfers between devices with their start and end apart: 26, of which 8 were waited for; matrix products, arithmetic and copies ran while one was open for 6% of the time, Pallas kernels for 17%

profile of v2, /device:TPU:9, one launch (start us, length us, event | category | flops | bytes accessed | tf_op | source)
XLA Modules:
  0.0 89.4 jit_solution(5889914633327794469)
XLA Ops:
  0.6 1.2 %dynamic-slice_bitcast_fusion = (bf16[256,2,128]{2,1,0:T(2,128)(2,1)S(1)}, bf16[1,256,2,128]{3,2,1,0:T(2,128)(2,1)S(1)}) fusion(bf16[2,256,2,128]{3,2,1,0:T(2,128)(2,1)} %param.5, s32[]{:T(128)S(6)} %select_n.8, s32[]{:T(128)S(6)} %select_n.7), kind=kLoop, calls=%fused_computation.14 | loop fusion | bytes 524296 | tf_op jit(solution)/shard_map/jit(dynamic_index_in_dim)/squeeze | solution.py:292
  1.8 0.7 collective-permute-start.6
  2.5 0.8 copy.8
  3.3 0.8 copy.7
  4.1 0.0 copy-start
  4.1 1.6 %copy-done = bf16[1,32,1,256,128]{4,3,2,1,0:T(8,128)(2,1)S(1)} copy-done((bf16[1,32,1,256,128]{4,3,2,1,0:T(8,128)(2,1)S(1)}, bf16[1,32,1,256,128]{4,3,2,1,0:T(8,128)(2,1)}, u32[]{:S(2)}) %copy-start) | copy-done | bytes 2097176
  5.7 1.8 %shard_map.68 = (bf16[4,5,32,128]{3,2,1,0:T(8,128)(2,1)S(1)}, bf16[4,5,32,128]{3,2,1,0:T(8,128)(2,1)S(1)}, bf16[4,5,32,128]{3,2,1,0:T(8,128)(2,1)S(1)}, bf16[4,5,32,128]{3,2,1,0:T(8,128)(2,1)S(1)}) custom-call(s32[1]{0:T(128)} %bitcast.1.refs_0_, s32[32,16]{1,0:T(8,128)S(1)} %bitcast.25, f32[32,16]{1,0:T(8,128)S(1)} %bitcast.33, ...), custom_call_target="tpu_custom_call" | custom-call | flops 536870912 | bytes 2228224 | tf_op jit(solution)/shard_map/pallas_call | solution.py:250
  7.5 0.1 collective-permute-start
  7.6 2.5 %collective-permute-start.1 = (bf16[4,5,32,128]{3,2,1,0:T(8,128)(2,1)S(1)}, bf16[4,5,32,128]{3,2,1,0:T(8,128)(2,1)S(1)}, u32[]{:S(2)}, u32[]{:S(2)}) collective-permute-start(bf16[4,5,32,128]{3,2,1,0:T(8,128)(2,1)S(1)} %get-tuple-element.22), channel_id=1, source_target_pairs={{0,8},{1,9},{2,10},{3,11},{4,12},{5,13},{6,14},{7,15},{8,0},{9,1},... | collective-permute-start | bytes 491528 | tf_op jit(solution)/shard_map/ppermute | solution.py:75
  10.1 0.2 collective-permute-start.2
  10.3 0.0 collective-permute-done.6
  10.3 1.8 %shard_map.70 = (bf16[4,5,32,128]{3,2,1,0:T(8,128)(2,1)S(1)}, bf16[4,5,32,128]{3,2,1,0:T(8,128)(2,1)S(1)}, bf16[4,5,32,128]{3,2,1,0:T(8,128)(2,1)S(1)}, bf16[4,5,32,128]{3,2,1,0:T(8,128)(2,1)S(1)}) custom-call(s32[1]{0:T(128)} %bitcast.1.refs_0_, s32[32,16]{1,0:T(8,128)S(1)} %bitcast.26, f32[32,16]{1,0:T(8,128)S(1)} %bitcast.34, ...), custom_call_target="tpu_custom_call" | custom-call | flops 536870912 | bytes 2228224 | tf_op jit(solution)/shard_map/pallas_call | solution.py:250
  12.2 0.0 copy-start.2
  12.2 1.3 %collective-permute-start.7 = (bf16[4,5,32,128]{3,2,1,0:T(8,128)(2,1)S(1)}, bf16[4,5,32,128]{3,2,1,0:T(8,128)(2,1)S(1)}, u32[]{:S(2)}, u32[]{:S(2)}) collective-permute-start(bf16[4,5,32,128]{3,2,1,0:T(8,128)(2,1)S(1)} %get-tuple-element.26), channel_id=1, source_target_pairs={{0,1},{1,0},{2,3},{3,2},{4,5},{5,4},{6,7},{7,6},{8,9},{9,8},{10,11... | collective-permute-start | bytes 491528 | tf_op jit(solution)/shard_map/ppermute | solution.py:75
  13.4 1.2 %collective-permute-start.8 = (bf16[4,5,32,128]{3,2,1,0:T(8,128)(2,1)S(1)}, bf16[4,5,32,128]{3,2,1,0:T(8,128)(2,1)S(1)}, u32[]{:S(2)}, u32[]{:S(2)}) collective-permute-start(bf16[4,5,32,128]{3,2,1,0:T(8,128)(2,1)S(1)} %get-tuple-element.27), channel_id=1, source_target_pairs={{0,2},{1,3},{2,0},{3,1},{4,6},{5,7},{6,4},{7,5},{8,10},{9,11},{10,... | collective-permute-start | bytes 491528 | tf_op jit(solution)/shard_map/ppermute | solution.py:75
  14.7 0.0 collective-permute-done.refs_5_
  14.7 1.7 %collective-permute-start.9 = (bf16[4,5,32,128]{3,2,1,0:T(8,128)(2,1)S(1)}, bf16[4,5,32,128]{3,2,1,0:T(8,128)(2,1)S(1)}, u32[]{:S(2)}, u32[]{:S(2)}) collective-permute-start(bf16[4,5,32,128]{3,2,1,0:T(8,128)(2,1)S(1)} %get-tuple-element.28), channel_id=1, source_target_pairs={{0,3},{1,2},{2,1},{3,0},{4,7},{5,6},{6,5},{7,4},{8,11},{9,10},{10,... | collective-permute-start | bytes 491528 | tf_op jit(solution)/shard_map/ppermute | solution.py:75
  16.4 3.9 %collective-permute-done.1.refs_6_ = bf16[4,5,32,128]{3,2,1,0:T(8,128)(2,1)S(1)} collective-permute-done((bf16[4,5,32,128]{3,2,1,0:T(8,128)(2,1)S(1)}, bf16[4,5,32,128]{3,2,1,0:T(8,128)(2,1)S(1)}, u32[]{:S(2)}, u32[]{:S(2)}) %collective-permute-start.1) | collective-permute-done | bytes 163872 | tf_op jit(solution)/shard_map/ppermute | solution.py:75
  20.3 4.5 %collective-permute-done.2.refs_7_ = bf16[4,5,32,128]{3,2,1,0:T(8,128)(2,1)S(1)} collective-permute-done((bf16[4,5,32,128]{3,2,1,0:T(8,128)(2,1)S(1)}, bf16[4,5,32,128]{3,2,1,0:T(8,128)(2,1)S(1)}, u32[]{:S(2)}, u32[]{:S(2)}) %collective-permute-start.2) | collective-permute-done | bytes 163872 | tf_op jit(solution)/shard_map/ppermute | solution.py:75
  24.9 1.3 %collective-permute-start.3 = (bf16[4,5,32,128]{3,2,1,0:T(8,128)(2,1)S(1)}, bf16[4,5,32,128]{3,2,1,0:T(8,128)(2,1)S(1)}, u32[]{:S(2)}, u32[]{:S(2)}) collective-permute-start(bf16[4,5,32,128]{3,2,1,0:T(8,128)(2,1)S(1)} %pad_maximum_fusion), channel_id=1, source_target_pairs={{0,1},{1,0},{2,3},{3,2},{4,5},{5,4},{6,7},{7,6},{8,9},{9,8},{10,11... | collective-permute-start | bytes 491528 | tf_op jit(solution)/shard_map/ppermute | solution.py:75
  26.2 1.3 %collective-permute-start.4 = (bf16[4,5,32,128]{3,2,1,0:T(8,128)(2,1)S(1)}, bf16[4,5,32,128]{3,2,1,0:T(8,128)(2,1)S(1)}, u32[]{:S(2)}, u32[]{:S(2)}) collective-permute-start(bf16[4,5,32,128]{3,2,1,0:T(8,128)(2,1)S(1)} %pad_maximum_fusion.1), channel_id=1, source_target_pairs={{0,2},{1,3},{2,0},{3,1},{4,6},{5,7},{6,4},{7,5},{8,10},{9,11},{10,... | collective-permute-start | bytes 491528 | tf_op jit(solution)/shard_map/ppermute | solution.py:75
  27.5 0.0 collective-permute-done.7.refs_5_
  27.6 0.3 collective-permute-start.5
  27.8 0.0 collective-permute-done.8.refs_6_
  27.9 0.0 collective-permute-done.9.refs_7_
  27.9 0.1 collective-permute-start.10
  28.0 2.5 %collective-permute-start.11 = (bf16[4,5,32,128]{3,2,1,0:T(8,128)(2,1)S(1)}, bf16[4,5,32,128]{3,2,1,0:T(8,128)(2,1)S(1)}, u32[]{:S(2)}, u32[]{:S(2)}) collective-permute-start(bf16[4,5,32,128]{3,2,1,0:T(8,128)(2,1)S(1)} %pad_maximum_fusion.4), channel_id=1, source_target_pairs={{0,8},{1,9},{2,10},{3,11},{4,12},{5,13},{6,14},{7,15},{8,0},{9,1},... | collective-permute-start | bytes 491528 | tf_op jit(solution)/shard_map/ppermute | solution.py:75
  30.6 0.0 collective-permute-done.3.refs_8_
  30.6 0.3 collective-permute-start.12
  30.8 0.0 collective-permute-done.4.refs_9_
  30.8 3.6 %collective-permute-done.5.refs_10_ = bf16[4,5,32,128]{3,2,1,0:T(8,128)(2,1)S(1)} collective-permute-done((bf16[4,5,32,128]{3,2,1,0:T(8,128)(2,1)S(1)}, bf16[4,5,32,128]{3,2,1,0:T(8,128)(2,1)S(1)}, u32[]{:S(2)}, u32[]{:S(2)}) %collective-permute-start.5) | collective-permute-done | bytes 163872 | tf_op jit(solution)/shard_map/ppermute | solution.py:75
  34.4 3.0 %shard_map.69 = (bf16[2,256,256]{2,1,0:T(8,128)(2,1)S(1)}, bf16[4,5,32,128]{3,2,1,0:T(8,128)(2,1)S(1)}, bf16[4,5,32,128]{3,2,1,0:T(8,128)(2,1)S(1)}, bf16[4,5,32...) custom-call(s32[1]{0:T(128)} %bitcast.1.refs_0_, s32[32,16]{1,0:T(8,128)S(1)} %bitcast.27, f32[32,16]{1,0:T(8,128)S(1)} %bitcast.35, ...), custom_call_target="tpu_custom_call" | custom-call | flops 1073741824 | bytes 3244032 | tf_op jit(solution)/shard_map/pallas_call | solution.py:261
  37.4 0.1 collective-permute-start.13
  37.5 2.4 %collective-permute-start.14 = (bf16[4,5,32,128]{3,2,1,0:T(8,128)(2,1)S(1)}, bf16[4,5,32,128]{3,2,1,0:T(8,128)(2,1)S(1)}, u32[]{:S(2)}, u32[]{:S(2)}) collective-permute-start(bf16[4,5,32,128]{3,2,1,0:T(8,128)(2,1)S(1)} %get-tuple-element.32), channel_id=1, source_target_pairs={{0,8},{1,9},{2,10},{3,11},{4,12},{5,13},{6,14},{7,15},{8,0},{9,1},... | collective-permute-start | bytes 491528 | tf_op jit(solution)/shard_map/ppermute | solution.py:75
  40.0 0.3 collective-permute-start.15
  40.2 5.0 %collective-permute-done.12.refs_10_ = bf16[4,5,32,128]{3,2,1,0:T(8,128)(2,1)S(1)} collective-permute-done((bf16[4,5,32,128]{3,2,1,0:T(8,128)(2,1)S(1)}, bf16[4,5,32,128]{3,2,1,0:T(8,128)(2,1)S(1)}, u32[]{:S(2)}, u32[]{:S(2)}) %collective-permute-start.12) | collective-permute-done | bytes 163872 | tf_op jit(solution)/shard_map/ppermute | solution.py:75
  45.2 3.0 %shard_map.71 = (bf16[2,256,256]{2,1,0:T(8,128)(2,1)S(1)}, bf16[4,5,32,128]{3,2,1,0:T(8,128)(2,1)S(1)}, bf16[4,5,32,128]{3,2,1,0:T(8,128)(2,1)S(1)}, bf16[4,5,32...) custom-call(s32[1]{0:T(128)} %bitcast.1.refs_0_, s32[32,16]{1,0:T(8,128)S(1)} %bitcast.28, f32[32,16]{1,0:T(8,128)S(1)} %bitcast.36, ...), custom_call_target="tpu_custom_call" | custom-call | flops 1073741824 | bytes 3244032 | tf_op jit(solution)/shard_map/pallas_call | solution.py:261
  48.2 0.0 copy-start.1
  48.2 1.0 %collective-permute-start.19 = (bf16[4,5,32,128]{3,2,1,0:T(8,128)(2,1)S(1)}, bf16[4,5,32,128]{3,2,1,0:T(8,128)(2,1)S(1)}, u32[]{:S(2)}, u32[]{:S(2)}) collective-permute-start(bf16[4,5,32,128]{3,2,1,0:T(8,128)(2,1)S(1)} %get-tuple-element.35), channel_id=1, source_target_pairs={{0,1},{1,0},{2,3},{3,2},{4,5},{5,4},{6,7},{7,6},{8,9},{9,8},{10,11... | collective-permute-start | bytes 491528 | tf_op jit(solution)/shard_map/ppermute | solution.py:75
  49.2 2.2 %collective-permute-start.20 = (bf16[4,5,32,128]{3,2,1,0:T(8,128)(2,1)S(1)}, bf16[4,5,32,128]{3,2,1,0:T(8,128)(2,1)S(1)}, u32[]{:S(2)}, u32[]{:S(2)}) collective-permute-start(bf16[4,5,32,128]{3,2,1,0:T(8,128)(2,1)S(1)} %get-tuple-element.36), channel_id=1, source_target_pairs={{0,2},{1,3},{2,0},{3,1},{4,6},{5,7},{6,4},{7,5},{8,10},{9,11},{10,... | collective-permute-start | bytes 491528 | tf_op jit(solution)/shard_map/ppermute | solution.py:75
  51.4 0.0 collective-permute-done.13.refs_4_
  51.4 0.1 collective-permute-start.21
  51.5 2.9 %collective-permute-done.14.refs_5_ = bf16[4,5,32,128]{3,2,1,0:T(8,128)(2,1)S(1)} collective-permute-done((bf16[4,5,32,128]{3,2,1,0:T(8,128)(2,1)S(1)}, bf16[4,5,32,128]{3,2,1,0:T(8,128)(2,1)S(1)}, u32[]{:S(2)}, u32[]{:S(2)}) %collective-permute-start.14) | collective-permute-done | bytes 163872 | tf_op jit(solution)/shard_map/ppermute | solution.py:75
  54.5 3.6 %collective-permute-done.15.refs_6_ = bf16[4,5,32,128]{3,2,1,0:T(8,128)(2,1)S(1)} collective-permute-done((bf16[4,5,32,128]{3,2,1,0:T(8,128)(2,1)S(1)}, bf16[4,5,32,128]{3,2,1,0:T(8,128)(2,1)S(1)}, u32[]{:S(2)}, u32[]{:S(2)}) %collective-permute-start.15) | collective-permute-done | bytes 163872 | tf_op jit(solution)/shard_map/ppermute | solution.py:75
  58.1 0.7 pad_maximum_fusion.6
  58.8 1.2 %collective-permute-start.16 = (bf16[4,5,32,128]{3,2,1,0:T(8,128)(2,1)}, bf16[4,5,32,128]{3,2,1,0:T(8,128)(2,1)S(1)}, u32[]{:S(2)}, u32[]{:S(2)}) collective-permute-start(bf16[4,5,32,128]{3,2,1,0:T(8,128)(2,1)} %pad_maximum_fusion.6), channel_id=1, source_target_pairs={{0,1},{1,0},{2,3},{3,2},{4,5},{5,4},{6,7},{7,6},{8,9},{9,8},{10,11... | collective-permute-start | bytes 491528 | tf_op jit(solution)/shard_map/ppermute | solution.py:75
  60.0 0.0 collective-permute-done.21.refs_6_
  60.0 0.1 collective-permute-start.22
  60.2 5.9 %collective-permute-start.23 = (bf16[4,5,32,128]{3,2,1,0:T(8,128)(2,1)S(1)}, bf16[4,5,32,128]{3,2,1,0:T(8,128)(2,1)S(1)}, u32[]{:S(2)}, u32[]{:S(2)}) collective-permute-start(bf16[4,5,32,128]{3,2,1,0:T(8,128)(2,1)S(1)} %pad_maximum_fusion.10), channel_id=1, source_target_pairs={{0,8},{1,9},{2,10},{3,11},{4,12},{5,13},{6,14},{7,15},{8,0},{9,1},... | collective-permute-start | bytes 491528 | tf_op jit(solution)/shard_map/ppermute | solution.py:75
  66.1 0.1 collective-permute-start.24
  66.2 0.7 pad_maximum_fusion.7
  66.8 0.2 collective-permute-start.17
  67.1 0.7 pad_maximum_fusion.8
  67.8 0.0 collective-permute-done.22.refs_7_
  67.8 0.6 collective-permute-start.18
  68.4 3.2 %collective-permute-done.23.refs_8_ = bf16[4,5,32,128]{3,2,1,0:T(8,128)(2,1)S(1)} collective-permute-done((bf16[4,5,32,128]{3,2,1,0:T(8,128)(2,1)S(1)}, bf16[4,5,32,128]{3,2,1,0:T(8,128)(2,1)S(1)}, u32[]{:S(2)}, u32[]{:S(2)}) %collective-permute-start.23) | collective-permute-done | bytes 163872 | tf_op jit(solution)/shard_map/ppermute | solution.py:75
  71.6 7.3 %collective-permute-done.24.refs_9_ = bf16[4,5,32,128]{3,2,1,0:T(8,128)(2,1)S(1)} collective-permute-done((bf16[4,5,32,128]{3,2,1,0:T(8,128)(2,1)S(1)}, bf16[4,5,32,128]{3,2,1,0:T(8,128)(2,1)S(1)}, u32[]{:S(2)}, u32[]{:S(2)}) %collective-permute-start.24) | collective-permute-done | bytes 163872 | tf_op jit(solution)/shard_map/ppermute | solution.py:75
  78.9 2.8 %shard_map.74 = bf16[256,256]{1,0:T(8,128)(2,1)} custom-call(s32[1]{0:T(128)} %bitcast.1.refs_0_, s32[32,16]{1,0:T(8,128)S(1)} %bitcast.29, bf16[32,256,128]{2,1,0:T(8,128)(2,1)S(1)} %bitcast.21, bf16[4,5,32,128]{3,2,1,0:T(8,128)(2,1)S(1)} %get-tuple-element.34.refs_3_, bf16[4,5,32,128]{3,2,1,0:T(8,128)(2,1)S(1)} %collective-permute-done.19.refs_4_, ...), custom_call_target="tpu_custom_call" | custom-call | flops 536870912 | bytes 3244032 | tf_op jit(solution)/shard_map/pallas_call | solution.py:273
  81.7 2.7 %collective-permute-start.25 = (bf16[256,256]{1,0:T(8,128)(2,1)}, bf16[256,256]{1,0:T(8,128)(2,1)}, u32[]{:S(2)}, u32[]{:S(2)}) collective-permute-start(bf16[256,256]{1,0:T(8,128)(2,1)} %shard_map.74), channel_id=1, source_target_pairs={{0,16},{16,0},{1,17},{17,1},{2,18},{18,2},{3,19},{19,3},{4,20},{20... | collective-permute-start | bytes 393224 | tf_op jit(solution)/shard_map/ppermute | solution.py:302
  84.4 0.1 shard_map.72
  84.4 0.9 %reshape.39 = bf16[1,512,2,256]{3,2,1,0:T(2,128)(2,1)} reshape(bf16[512,512]{1,0:T(8,128)(2,1)S(1)} %shard_map.72) | data formatting | bytes 1048576 | tf_op jit(solution)/shard_map/reshape | solution.py:305
  85.4 2.4 %shard_map.73.first_ref = bf16[256,256]{1,0:T(8,128)(2,1)S(1)} custom-call(s32[1]{0:T(128)} %bitcast.1.refs_0_, s32[32,16]{1,0:T(8,128)S(1)} %bitcast.30, bf16[32,256,128]{2,1,0:T(8,128)(2,1)S(1)} %bitcast.22, bf16[4,5,32,128]{3,2,1,0:T(8,128)(2,1)S(1)} %get-tuple-element.30.refs_3_, bf16[4,5,32,128]{3,2,1,0:T(8,128)(2,1)S(1)} %collective-permute-done.13.refs_4_, ...), custom_call_target="tpu_custom_call" | custom-call | flops 536870912 | bytes 3244032 | tf_op jit(solution)/shard_map/pallas_call | solution.py:273
  87.8 0.9 %shard_map.75 = bf16[2,256,256]{2,1,0:T(8,128)(2,1)S(1)} custom-call(s32[1]{0:T(128)} %bitcast.core_ref, bf16[256,256]{1,0:T(8,128)(2,1)S(1)} %shard_map.73.first_ref, bf16[256,256]{1,0:T(8,128)(2,1)} %collective-permute-done.25.second_ref), custom_call_target="tpu_custom_call" | custom-call | tf_op jit(solution)/shard_map/pallas_call | solution.py:284
  88.7 0.8 reshape.40
  (37 shorter events, 0.4 us)
Async XLA Ops:
  1.8 8.5 %collective-permute-start.6 = (bf16[256,2,128]{2,1,0:T(2,128)(2,1)S(1)}, bf16[256,2,128]{2,1,0:T(2,128)(2,1)S(1)}, u32[]{:S(2)}, u32[]{:S(2)}) collective-permute-start(bf16[256,2,128]{2,1,0:T(2,128)(2,1)S(1)} %get-tuple-element.38), channel_id=1, source_target_pairs={{0,16},{16,0},{1,17},{17,1},{2,18},{18,2},{3,19},{19,3},{4,20},{20... | collective-permute-start | bytes 393224 | tf_op jit(solution)/shard_map/ppermute | solution.py:294
  4.1 1.6 %copy-start = (bf16[1,32,1,256,128]{4,3,2,1,0:T(8,128)(2,1)S(1)}, bf16[1,32,1,256,128]{4,3,2,1,0:T(8,128)(2,1)}, u32[]{:S(2)}) copy-start(bf16[1,32,1,256,128]{4,3,2,1,0:T(8,128)(2,1)} %param.6) | copy-start | bytes 6291460
  7.5 7.2 %collective-permute-start = (bf16[4,5,32,128]{3,2,1,0:T(8,128)(2,1)S(1)}, bf16[4,5,32,128]{3,2,1,0:T(8,128)(2,1)S(1)}, u32[]{:S(2)}, u32[]{:S(2)}) collective-permute-start(bf16[4,5,32,128]{3,2,1,0:T(8,128)(2,1)S(1)} %get-tuple-element.21), channel_id=1, source_target_pairs={{0,4},{1,5},{2,6},{3,7},{4,0},{5,1},{6,2},{7,3},{8,12},{9,13},{10,... | collective-permute-start | bytes 491528 | tf_op jit(solution)/shard_map/ppermute | solution.py:75
  7.6 12.7 %collective-permute-start.1 = (bf16[4,5,32,128]{3,2,1,0:T(8,128)(2,1)S(1)}, bf16[4,5,32,128]{3,2,1,0:T(8,128)(2,1)S(1)}, u32[]{:S(2)}, u32[]{:S(2)}) collective-permute-start(bf16[4,5,32,128]{3,2,1,0:T(8,128)(2,1)S(1)} %get-tuple-element.22), channel_id=1, source_target_pairs={{0,8},{1,9},{2,10},{3,11},{4,12},{5,13},{6,14},{7,15},{8,0},{9,1},... | collective-permute-start | bytes 491528 | tf_op jit(solution)/shard_map/ppermute | solution.py:75
  10.1 14.8 %collective-permute-start.2 = (bf16[4,5,32,128]{3,2,1,0:T(8,128)(2,1)S(1)}, bf16[4,5,32,128]{3,2,1,0:T(8,128)(2,1)S(1)}, u32[]{:S(2)}, u32[]{:S(2)}) collective-permute-start(bf16[4,5,32,128]{3,2,1,0:T(8,128)(2,1)S(1)} %get-tuple-element.23), channel_id=1, source_target_pairs={{0,12},{1,13},{2,14},{3,15},{4,8},{5,9},{6,10},{7,11},{8,4},{9,5},... | collective-permute-start | bytes 491528 | tf_op jit(solution)/shard_map/ppermute | solution.py:75
  12.2 22.3 %copy-start.2 = (bf16[1,2,16,256,128]{4,3,2,1,0:T(8,128)(2,1)S(1)}, bf16[1,2,16,256,128]{4,3,2,1,0:T(8,128)(2,1)}, u32[]{:S(2)}) copy-start(bf16[1,2,16,256,128]{4,3,2,1,0:T(8,128)(2,1)} %param.7) | copy-start | bytes 6291460
  12.2 15.4 %collective-permute-start.7 = (bf16[4,5,32,128]{3,2,1,0:T(8,128)(2,1)S(1)}, bf16[4,5,32,128]{3,2,1,0:T(8,128)(2,1)S(1)}, u32[]{:S(2)}, u32[]{:S(2)}) collective-permute-start(bf16[4,5,32,128]{3,2,1,0:T(8,128)(2,1)S(1)} %get-tuple-element.26), channel_id=1, source_target_pairs={{0,1},{1,0},{2,3},{3,2},{4,5},{5,4},{6,7},{7,6},{8,9},{9,8},{10,11... | collective-permute-start | bytes 491528 | tf_op jit(solution)/shard_map/ppermute | solution.py:75
  13.4 14.4 %collective-permute-start.8 = (bf16[4,5,32,128]{3,2,1,0:T(8,128)(2,1)S(1)}, bf16[4,5,32,128]{3,2,1,0:T(8,128)(2,1)S(1)}, u32[]{:S(2)}, u32[]{:S(2)}) collective-permute-start(bf16[4,5,32,128]{3,2,1,0:T(8,128)(2,1)S(1)} %get-tuple-element.27), channel_id=1, source_target_pairs={{0,2},{1,3},{2,0},{3,1},{4,6},{5,7},{6,4},{7,5},{8,10},{9,11},{10,... | collective-permute-start | bytes 491528 | tf_op jit(solution)/shard_map/ppermute | solution.py:75
  14.7 13.2 %collective-permute-start.9 = (bf16[4,5,32,128]{3,2,1,0:T(8,128)(2,1)S(1)}, bf16[4,5,32,128]{3,2,1,0:T(8,128)(2,1)S(1)}, u32[]{:S(2)}, u32[]{:S(2)}) collective-permute-start(bf16[4,5,32,128]{3,2,1,0:T(8,128)(2,1)S(1)} %get-tuple-element.28), channel_id=1, source_target_pairs={{0,3},{1,2},{2,1},{3,0},{4,7},{5,6},{6,5},{7,4},{8,11},{9,10},{10,... | collective-permute-start | bytes 491528 | tf_op jit(solution)/shard_map/ppermute | solution.py:75
  24.9 5.7 %collective-permute-start.3 = (bf16[4,5,32,128]{3,2,1,0:T(8,128)(2,1)S(1)}, bf16[4,5,32,128]{3,2,1,0:T(8,128)(2,1)S(1)}, u32[]{:S(2)}, u32[]{:S(2)}) collective-permute-start(bf16[4,5,32,128]{3,2,1,0:T(8,128)(2,1)S(1)} %pad_maximum_fusion), channel_id=1, source_target_pairs={{0,1},{1,0},{2,3},{3,2},{4,5},{5,4},{6,7},{7,6},{8,9},{9,8},{10,11... | collective-permute-start | bytes 491528 | tf_op jit(solution)/shard_map/ppermute | solution.py:75
  26.2 4.6 %collective-permute-start.4 = (bf16[4,5,32,128]{3,2,1,0:T(8,128)(2,1)S(1)}, bf16[4,5,32,128]{3,2,1,0:T(8,128)(2,1)S(1)}, u32[]{:S(2)}, u32[]{:S(2)}) collective-permute-start(bf16[4,5,32,128]{3,2,1,0:T(8,128)(2,1)S(1)} %pad_maximum_fusion.1), channel_id=1, source_target_pairs={{0,2},{1,3},{2,0},{3,1},{4,6},{5,7},{6,4},{7,5},{8,10},{9,11},{10,... | collective-permute-start | bytes 491528 | tf_op jit(solution)/shard_map/ppermute | solution.py:75
  27.6 6.9 %collective-permute-start.5 = (bf16[4,5,32,128]{3,2,1,0:T(8,128)(2,1)S(1)}, bf16[4,5,32,128]{3,2,1,0:T(8,128)(2,1)S(1)}, u32[]{:S(2)}, u32[]{:S(2)}) collective-permute-start(bf16[4,5,32,128]{3,2,1,0:T(8,128)(2,1)S(1)} %pad_maximum_fusion.2), channel_id=1, source_target_pairs={{0,3},{1,2},{2,1},{3,0},{4,7},{5,6},{6,5},{7,4},{8,11},{9,10},{10,... | collective-permute-start | bytes 491528 | tf_op jit(solution)/shard_map/ppermute | solution.py:75
  27.9 12.0 %collective-permute-start.10 = (bf16[4,5,32,128]{3,2,1,0:T(8,128)(2,1)S(1)}, bf16[4,5,32,128]{3,2,1,0:T(8,128)(2,1)S(1)}, u32[]{:S(2)}, u32[]{:S(2)}) collective-permute-start(bf16[4,5,32,128]{3,2,1,0:T(8,128)(2,1)S(1)} %pad_maximum_fusion.3), channel_id=1, source_target_pairs={{0,4},{1,5},{2,6},{3,7},{4,0},{5,1},{6,2},{7,3},{8,12},{9,13},{10,... | collective-permute-start | bytes 491528 | tf_op jit(solution)/shard_map/ppermute | solution.py:75
  28.0 12.2 %collective-permute-start.11 = (bf16[4,5,32,128]{3,2,1,0:T(8,128)(2,1)S(1)}, bf16[4,5,32,128]{3,2,1,0:T(8,128)(2,1)S(1)}, u32[]{:S(2)}, u32[]{:S(2)}) collective-permute-start(bf16[4,5,32,128]{3,2,1,0:T(8,128)(2,1)S(1)} %pad_maximum_fusion.4), channel_id=1, source_target_pairs={{0,8},{1,9},{2,10},{3,11},{4,12},{5,13},{6,14},{7,15},{8,0},{9,1},... | collective-permute-start | bytes 491528 | tf_op jit(solution)/shard_map/ppermute | solution.py:75
  30.6 14.6 %collective-permute-start.12 = (bf16[4,5,32,128]{3,2,1,0:T(8,128)(2,1)S(1)}, bf16[4,5,32,128]{3,2,1,0:T(8,128)(2,1)S(1)}, u32[]{:S(2)}, u32[]{:S(2)}) collective-permute-start(bf16[4,5,32,128]{3,2,1,0:T(8,128)(2,1)S(1)} %pad_maximum_fusion.5), channel_id=1, source_target_pairs={{0,12},{1,13},{2,14},{3,15},{4,8},{5,9},{6,10},{7,11},{8,4},{9,5},... | collective-permute-start | bytes 491528 | tf_op jit(solution)/shard_map/ppermute | solution.py:75
  37.4 14.0 %collective-permute-start.13 = (bf16[4,5,32,128]{3,2,1,0:T(8,128)(2,1)S(1)}, bf16[4,5,32,128]{3,2,1,0:T(8,128)(2,1)S(1)}, u32[]{:S(2)}, u32[]{:S(2)}) collective-permute-start(bf16[4,5,32,128]{3,2,1,0:T(8,128)(2,1)S(1)} %get-tuple-element.31), channel_id=1, source_target_pairs={{0,4},{1,5},{2,6},{3,7},{4,0},{5,1},{6,2},{7,3},{8,12},{9,13},{10,... | collective-permute-start | bytes 491528 | tf_op jit(solution)/shard_map/ppermute | solution.py:75
  37.5 16.9 %collective-permute-start.14 = (bf16[4,5,32,128]{3,2,1,0:T(8,128)(2,1)S(1)}, bf16[4,5,32,128]{3,2,1,0:T(8,128)(2,1)S(1)}, u32[]{:S(2)}, u32[]{:S(2)}) collective-permute-start(bf16[4,5,32,128]{3,2,1,0:T(8,128)(2,1)S(1)} %get-tuple-element.32), channel_id=1, source_target_pairs={{0,8},{1,9},{2,10},{3,11},{4,12},{5,13},{6,14},{7,15},{8,0},{9,1},... | collective-permute-start | bytes 491528 | tf_op jit(solution)/shard_map/ppermute | solution.py:75
  40.0 18.1 %collective-permute-start.15 = (bf16[4,5,32,128]{3,2,1,0:T(8,128)(2,1)S(1)}, bf16[4,5,32,128]{3,2,1,0:T(8,128)(2,1)S(1)}, u32[]{:S(2)}, u32[]{:S(2)}) collective-permute-start(bf16[4,5,32,128]{3,2,1,0:T(8,128)(2,1)S(1)} %get-tuple-element.33), channel_id=1, source_target_pairs={{0,12},{1,13},{2,14},{3,15},{4,8},{5,9},{6,10},{7,11},{8,4},{9,5},... | collective-permute-start | bytes 491528 | tf_op jit(solution)/shard_map/ppermute | solution.py:75
  48.2 30.7 %copy-start.1 = (bf16[1,32,1,256,128]{4,3,2,1,0:T(8,128)(2,1)S(1)}, bf16[1,32,1,256,128]{4,3,2,1,0:T(8,128)(2,1)}, u32[]{:S(2)}) copy-start(bf16[1,32,1,256,128]{4,3,2,1,0:T(8,128)(2,1)} %param.6) | copy-start | bytes 6291460
  48.2 11.7 %collective-permute-start.19 = (bf16[4,5,32,128]{3,2,1,0:T(8,128)(2,1)S(1)}, bf16[4,5,32,128]{3,2,1,0:T(8,128)(2,1)S(1)}, u32[]{:S(2)}, u32[]{:S(2)}) collective-permute-start(bf16[4,5,32,128]{3,2,1,0:T(8,128)(2,1)S(1)} %get-tuple-element.35), channel_id=1, source_target_pairs={{0,1},{1,0},{2,3},{3,2},{4,5},{5,4},{6,7},{7,6},{8,9},{9,8},{10,11... | collective-permute-start | bytes 491528 | tf_op jit(solution)/shard_map/ppermute | solution.py:75
  49.2 10.8 %collective-permute-start.20 = (bf16[4,5,32,128]{3,2,1,0:T(8,128)(2,1)S(1)}, bf16[4,5,32,128]{3,2,1,0:T(8,128)(2,1)S(1)}, u32[]{:S(2)}, u32[]{:S(2)}) collective-permute-start(bf16[4,5,32,128]{3,2,1,0:T(8,128)(2,1)S(1)} %get-tuple-element.36), channel_id=1, source_target_pairs={{0,2},{1,3},{2,0},{3,1},{4,6},{5,7},{6,4},{7,5},{8,10},{9,11},{10,... | collective-permute-start | bytes 491528 | tf_op jit(solution)/shard_map/ppermute | solution.py:75
  51.4 8.6 %collective-permute-start.21 = (bf16[4,5,32,128]{3,2,1,0:T(8,128)(2,1)S(1)}, bf16[4,5,32,128]{3,2,1,0:T(8,128)(2,1)S(1)}, u32[]{:S(2)}, u32[]{:S(2)}) collective-permute-start(bf16[4,5,32,128]{3,2,1,0:T(8,128)(2,1)S(1)} %get-tuple-element.37), channel_id=1, source_target_pairs={{0,3},{1,2},{2,1},{3,0},{4,7},{5,6},{6,5},{7,4},{8,11},{9,10},{10,... | collective-permute-start | bytes 491528 | tf_op jit(solution)/shard_map/ppermute | solution.py:75
  58.8 26.6 %collective-permute-start.16 = (bf16[4,5,32,128]{3,2,1,0:T(8,128)(2,1)}, bf16[4,5,32,128]{3,2,1,0:T(8,128)(2,1)S(1)}, u32[]{:S(2)}, u32[]{:S(2)}) collective-permute-start(bf16[4,5,32,128]{3,2,1,0:T(8,128)(2,1)} %pad_maximum_fusion.6), channel_id=1, source_target_pairs={{0,1},{1,0},{2,3},{3,2},{4,5},{5,4},{6,7},{7,6},{8,9},{9,8},{10,11... | collective-permute-start | bytes 491528 | tf_op jit(solution)/shard_map/ppermute | solution.py:75
  60.0 7.7 %collective-permute-start.22 = (bf16[4,5,32,128]{3,2,1,0:T(8,128)(2,1)S(1)}, bf16[4,5,32,128]{3,2,1,0:T(8,128)(2,1)S(1)}, u32[]{:S(2)}, u32[]{:S(2)}) collective-permute-start(bf16[4,5,32,128]{3,2,1,0:T(8,128)(2,1)S(1)} %pad_maximum_fusion.9), channel_id=1, source_target_pairs={{0,4},{1,5},{2,6},{3,7},{4,0},{5,1},{6,2},{7,3},{8,12},{9,13},{10,... | collective-permute-start | bytes 491528 | tf_op jit(solution)/shard_map/ppermute | solution.py:75
  60.2 11.5 %collective-permute-start.23 = (bf16[4,5,32,128]{3,2,1,0:T(8,128)(2,1)S(1)}, bf16[4,5,32,128]{3,2,1,0:T(8,128)(2,1)S(1)}, u32[]{:S(2)}, u32[]{:S(2)}) collective-permute-start(bf16[4,5,32,128]{3,2,1,0:T(8,128)(2,1)S(1)} %pad_maximum_fusion.10), channel_id=1, source_target_pairs={{0,8},{1,9},{2,10},{3,11},{4,12},{5,13},{6,14},{7,15},{8,0},{9,1},... | collective-permute-start | bytes 491528 | tf_op jit(solution)/shard_map/ppermute | solution.py:75
  66.1 12.8 %collective-permute-start.24 = (bf16[4,5,32,128]{3,2,1,0:T(8,128)(2,1)S(1)}, bf16[4,5,32,128]{3,2,1,0:T(8,128)(2,1)S(1)}, u32[]{:S(2)}, u32[]{:S(2)}) collective-permute-start(bf16[4,5,32,128]{3,2,1,0:T(8,128)(2,1)S(1)} %pad_maximum_fusion.11), channel_id=1, source_target_pairs={{0,12},{1,13},{2,14},{3,15},{4,8},{5,9},{6,10},{7,11},{8,4},{9,5},... | collective-permute-start | bytes 491528 | tf_op jit(solution)/shard_map/ppermute | solution.py:75
  66.8 18.5 %collective-permute-start.17 = (bf16[4,5,32,128]{3,2,1,0:T(8,128)(2,1)}, bf16[4,5,32,128]{3,2,1,0:T(8,128)(2,1)}, u32[]{:S(2)}, u32[]{:S(2)}) collective-permute-start(bf16[4,5,32,128]{3,2,1,0:T(8,128)(2,1)} %pad_maximum_fusion.7), channel_id=1, source_target_pairs={{0,2},{1,3},{2,0},{3,1},{4,6},{5,7},{6,4},{7,5},{8,10},{9,11},{10,... | collective-permute-start | bytes 491528 | tf_op jit(solution)/shard_map/ppermute | solution.py:75
  67.8 17.6 %collective-permute-start.18 = (bf16[4,5,32,128]{3,2,1,0:T(8,128)(2,1)}, bf16[4,5,32,128]{3,2,1,0:T(8,128)(2,1)}, u32[]{:S(2)}, u32[]{:S(2)}) collective-permute-start(bf16[4,5,32,128]{3,2,1,0:T(8,128)(2,1)} %pad_maximum_fusion.8), channel_id=1, source_target_pairs={{0,3},{1,2},{2,1},{3,0},{4,7},{5,6},{6,5},{7,4},{8,11},{9,10},{10,... | collective-permute-start | bytes 491528 | tf_op jit(solution)/shard_map/ppermute | solution.py:75
  81.7 6.1 %collective-permute-start.25 = (bf16[256,256]{1,0:T(8,128)(2,1)}, bf16[256,256]{1,0:T(8,128)(2,1)}, u32[]{:S(2)}, u32[]{:S(2)}) collective-permute-start(bf16[256,256]{1,0:T(8,128)(2,1)} %shard_map.74), channel_id=1, source_target_pairs={{0,16},{16,0},{1,17},{17,1},{2,18},{18,2},{3,19},{19,3},{4,20},{20... | collective-permute-start | bytes 393224 | tf_op jit(solution)/shard_map/ppermute | solution.py:302

commit v3 on v2

--- a/solution.py
+++ b/solution.py
@@ -68,19 +68,32 @@
 
 def exchange(blocks, route, tiles):
     if route is None:
-        return [lax.all_to_all(blocks[0], "tile", split_axis=0, concat_axis=0, tiled=True)]
+        return [lax.all_to_all(blocks[0], "tile", split_axis=0, concat_axis=0, tiled=True)], []
     count_a, s1, count_b, s2 = route
 
     def swap(block, offset):
         return lax.ppermute(block, "tile", [(i, i ^ offset) for i in range(tiles)])
 
-    hops = {a: swap(blocks[a], a * s1) for a in reversed(range(1, count_a))}
+    hops = {a: swap(blocks[a], a * s1) for a in range(1, count_a)}
     first = [blocks[0]] + [hops[a] for a in range(1, count_a)]
-    hops = {
-        b: swap(jnp.stack([first[a][b] for a in range(count_a)]), b * s2)
-        for b in reversed(range(1, count_b))
-    }
+    sends = [jnp.stack([first[a][b] for a in range(count_a)]) for b in range(1, count_b)]
+    return first, sends
+
+
+def second_hop(first, sends, route, tiles):
+    if route is None:
+        return first
+    count_a, s1, count_b, s2 = route
+
+    def swap(block, offset):
+        return lax.ppermute(block, "tile", [(i, i ^ offset) for i in range(tiles)])
+
+    hops = {b: swap(sends[b - 1], b * s2) for b in range(1, count_b)}
     return first + [hops[b] for b in range(1, count_b)]
+
+
+def after(values, others):
+    return lax.optimization_barrier((list(values), list(others)))[0]
 
 
 def shapes_sent(route, tiles, shape):
@@ -221,7 +234,7 @@
     out_ref[1 - core_ref[0]] = second_ref[...]
 
 
-WAYS = {"1a": far_first, "1b": near_first, "2a": far_first, "2b": near_first}
+WAYS = {"1a": far_first, "1b": near_first, "2a": far_first, "2b": at_once}
 
 
 def per_device(wave_in, column_basis, row_basis, tile_scale, tile_ranks):
@@ -292,17 +305,23 @@
     theirs = lax.dynamic_index_in_dim(wave_in, 1 - core, 0, keepdims=False)
     mine = lax.dynamic_index_in_dim(wave_in, core, 0, keepdims=False)
     other = lax.ppermute(theirs, "freq", swap)
-    coded_a = exchange(code(mine.reshape(height, 2 * n), way["1a"]), way["1a"], tiles)
-    coded_b = exchange(code(other.reshape(height, 2 * n), way["1b"]), way["1b"], tiles)
+    first_a, sends_a = exchange(code(mine.reshape(height, 2 * n), way["1a"]), way["1a"], tiles)
+    first_b, sends_b = exchange(code(other.reshape(height, 2 * n), way["1b"]), way["1b"], tiles)
+    coded_a = second_hop(first_a, sends_a, way["1a"], tiles)
+    coded_b = second_hop(first_b, sends_b, way["1b"], tiles)
     y_a, back_a = middle(coded_a, way["1a"], way["2a"])
-    back_a = exchange(back_a, way["2a"], tiles)
+    first_a, sends_a = exchange(back_a, way["2a"], tiles)
+    coded_b = after(coded_b, back_a)
     y_b, back_b = middle(coded_b, way["1b"], way["2b"])
-    back_b = exchange(back_b, way["2b"], tiles)
+    first_b, sends_b = exchange(back_b, way["2b"], tiles)
+    back_a = second_hop(first_a, sends_a, way["2a"], tiles)
+    back_b = second_hop(first_b, sends_b, way["2b"], tiles)
     z_a = adjoint(back_a, way["2a"])
+    forward_out = ordered(order_rows_kernel, y_a, y_b, (2 * height, 4 * n))
+    forward_out = forward_out.reshape(1, 2 * height, 2, 2 * n)
     z_b = lax.ppermute(adjoint(back_b, way["2b"]), "freq", swap)
-    forward_out = ordered(order_rows_kernel, y_a, y_b, (2 * height, 4 * n))
     adjoint_out = ordered(order_parts_kernel, z_a, z_b, (2, height, 2 * n))
-    return forward_out.reshape(1, 2 * height, 2, 2 * n), adjoint_out.reshape(2, height, 2, n)
+    return forward_out, adjoint_out.reshape(2, height, 2, n)
 
 
 def solution(mesh):

time: 89.9 us -> 82.3 us (0.915)
  waiting for transfers between devices: 34 us -> 16.6 us
  starting transfers between devices: 30.1 us -> 37.2 us
  local copies, waits for them, and re-layouts: 6.17 us -> 7.55 us
    ppermute x24 -> x18, waiting for transfers between devices: 34 us -> 12.7 us  [swap(): return lax.ppermute(block, 'tile', [(i, i ^ offset) for i in range(tiles)])]
    all_to_all x0 -> x1, starting transfers between devices: none -> 8.03 us  [exchange(): lax.all_to_all(blocks[0], 'tile', split_axis=0, concat_axis=0, tiled=True)]
    ppermute x24 -> x18, starting transfers between devices: 26.7 us -> 19.4 us  [swap(): return lax.ppermute(block, 'tile', [(i, i ^ offset) for i in range(tiles)])]
    ppermute x1, starting transfers between devices: 2.68 us -> 8.21 us  [per_device(): z_b = lax.ppermute(adjoint(back_b, way['2b']), 'freq', swap)]
    all_to_all x0 -> x1, waiting for transfers between devices: none -> 2.99 us  [exchange(): lax.all_to_all(blocks[0], 'tile', split_axis=0, concat_axis=0, tiled=True)]
    pallas_call x2, Pallas kernels: 6.02 us -> 8.14 us  [middle(): pl.pallas_call(lambda *refs: middle_kernel(route_in, route_out, tiles, *r...]
    unnamed x10 -> x18, local copies, waits for them, and re-layouts: 3.18 us -> 4.6 us
    ppermute x1, waiting for transfers between devices: 0.01 us -> 0.97 us  [per_device(): other = lax.ppermute(theirs, 'freq', swap)]
  transfers between devices with their start and end apart: 26 -> 21, of which waited for: 8 -> 7; matrix products, arithmetic and copies ran while one was open for 6% -> 4% of each run, Pallas kernels for 17% -> 18%
where the time goes in v3:
time: 82.3 us; the launch traced here: 81 us
  starting transfers between devices  37.2 us (45%)
  Pallas kernels  16.6 us (20%)
  waiting for transfers between devices  16.6 us (20%)
  local copies, waits for them, and re-layouts  7.55 us (9%)
  other arithmetic  2.21 us (3%)
  between operations  0.89 us (1%)
    ppermute x18, starting transfers between devices, swap(): return lax.ppermute(block, 'tile', [(i, i ^ offset) for i in range(tiles)])  19.4 us
    ppermute x18, waiting for transfers between devices, swap(): return lax.ppermute(block, 'tile', [(i, i ^ offset) for i in range(tiles)])  12.7 us
    ppermute x1, starting transfers between devices, per_device(): z_b = lax.ppermute(adjoint(back_b, way['2b']), 'freq', swap)  8.21 us
    pallas_call x2, Pallas kernels, middle(): pl.pallas_call(lambda *refs: middle_kernel(route_in, route_out, tiles, *r...  8.14 us
    all_to_all x1, starting transfers between devices, exchange(): lax.all_to_all(blocks[0], 'tile', split_axis=0, concat_axis=0, tiled=True)  8.03 us
    pallas_call x2, Pallas kernels, adjoint(): pl.pallas_call(lambda *refs: adjoint_kernel(route, tiles, *refs), out_sha...  4.62 us
    unnamed x18, local copies, waits for them, and re-layouts  4.6 us
    pallas_call x2, Pallas kernels, code(): pl.pallas_call(lambda *refs: coded_kernel(route, *refs), out_shape=shapes...  3.69 us
  transfers between devices with their start and end apart: 21, of which 7 were waited for; matrix products, arithmetic and copies ran while one was open for 4% of the time, Pallas kernels for 18%

profile of v3, /device:TPU:9, one launch (start us, length us, event | category | flops | bytes accessed | tf_op | source)
XLA Modules:
  0.0 81.0 jit_solution(1036161874315415715)
XLA Ops:
  0.6 1.2 %dynamic-slice_bitcast_fusion = (bf16[256,2,128]{2,1,0:T(2,128)(2,1)S(1)}, bf16[1,256,2,128]{3,2,1,0:T(2,128)(2,1)S(1)}) fusion(bf16[2,256,2,128]{3,2,1,0:T(2,128)(2,1)} %param.5, s32[]{:T(128)S(6)} %select_n.8, s32[]{:T(128)S(6)} %select_n.7), kind=kLoop, calls=%fused_computation.11 | loop fusion | bytes 524296 | tf_op jit(solution)/shard_map/jit(dynamic_index_in_dim)/squeeze | solution.py:305
  1.8 0.8 copy.7
  2.6 0.8 copy.8
  3.4 1.6 %copy-done = bf16[1,32,1,256,128]{4,3,2,1,0:T(8,128)(2,1)S(1)} copy-done((bf16[1,32,1,256,128]{4,3,2,1,0:T(8,128)(2,1)S(1)}, bf16[1,32,1,256,128]{4,3,2,1,0:T(8,128)(2,1)}, u32[]{:S(2)}) %copy-start) | copy-done | bytes 2097176
  5.0 1.9 %shard_map.68 = (bf16[4,5,32,128]{3,2,1,0:T(8,128)(2,1)S(1)}, bf16[4,5,32,128]{3,2,1,0:T(8,128)(2,1)S(1)}, bf16[4,5,32,128]{3,2,1,0:T(8,128)(2,1)S(1)}, bf16[4,5,32,128]{3,2,1,0:T(8,128)(2,1)S(1)}) custom-call(s32[1]{0:T(128)} %bitcast.1.refs_0_, s32[32,16]{1,0:T(8,128)S(1)} %bitcast.25, f32[32,16]{1,0:T(8,128)S(1)} %bitcast.33, ...), custom_call_target="tpu_custom_call" | custom-call | flops 536870912 | bytes 2228224 | tf_op jit(solution)/shard_map/pallas_call | solution.py:263
  6.8 0.1 collective-permute-start
  6.9 2.5 %collective-permute-start.1 = (bf16[4,5,32,128]{3,2,1,0:T(8,128)(2,1)S(1)}, bf16[4,5,32,128]{3,2,1,0:T(8,128)(2,1)S(1)}, u32[]{:S(2)}, u32[]{:S(2)}) collective-permute-start(bf16[4,5,32,128]{3,2,1,0:T(8,128)(2,1)S(1)} %get-tuple-element.26), channel_id=1, source_target_pairs={{0,8},{1,9},{2,10},{3,11},{4,12},{5,13},{6,14},{7,15},{8,0},{9,1},... | collective-permute-start | bytes 491528 | tf_op jit(solution)/shard_map/ppermute | solution.py:75
  9.4 0.2 collective-permute-start.2
  9.5 1.5 %collective-permute-start.6 = (bf16[256,2,128]{2,1,0:T(2,128)(2,1)S(1)}, bf16[256,2,128]{2,1,0:T(2,128)(2,1)S(1)}, u32[]{:S(2)}, u32[]{:S(2)}) collective-permute-start(bf16[256,2,128]{2,1,0:T(2,128)(2,1)S(1)} %get-tuple-element.46), channel_id=1, source_target_pairs={{0,16},{16,0},{1,17},{17,1},{2,18},{18,2},{3,19},{19,3},{4,20},{20... | collective-permute-start | bytes 393224 | tf_op jit(solution)/shard_map/ppermute | solution.py:307
  11.1 1.0 %collective-permute-done.6 = bf16[256,2,128]{2,1,0:T(2,128)(2,1)S(1)} collective-permute-done((bf16[256,2,128]{2,1,0:T(2,128)(2,1)S(1)}, bf16[256,2,128]{2,1,0:T(2,128)(2,1)S(1)}, u32[]{:S(2)}, u32[]{:S(2)}) %collective-permute-start.6) | collective-permute-done | bytes 131104 | tf_op jit(solution)/shard_map/ppermute | solution.py:307
  12.1 1.8 %shard_map.70 = (bf16[4,5,32,128]{3,2,1,0:T(8,128)(2,1)S(1)}, bf16[4,5,32,128]{3,2,1,0:T(8,128)(2,1)S(1)}, bf16[4,5,32,128]{3,2,1,0:T(8,128)(2,1)S(1)}, bf16[4,5,32,128]{3,2,1,0:T(8,128)(2,1)S(1)}) custom-call(s32[1]{0:T(128)} %bitcast.1.refs_0_, s32[32,16]{1,0:T(8,128)S(1)} %bitcast.26, f32[32,16]{1,0:T(8,128)S(1)} %bitcast.34, ...), custom_call_target="tpu_custom_call" | custom-call | flops 536870912 | bytes 2228224 | tf_op jit(solution)/shard_map/pallas_call | solution.py:263
  13.9 0.0 copy-start.6
  13.9 1.3 %collective-permute-start.7 = (bf16[4,5,32,128]{3,2,1,0:T(8,128)(2,1)S(1)}, bf16[4,5,32,128]{3,2,1,0:T(8,128)(2,1)S(1)}, u32[]{:S(2)}, u32[]{:S(2)}) collective-permute-start(bf16[4,5,32,128]{3,2,1,0:T(8,128)(2,1)S(1)} %get-tuple-element.30), channel_id=1, source_target_pairs={{0,1},{1,0},{2,3},{3,2},{4,5},{5,4},{6,7},{7,6},{8,9},{9,8},{10,11... | collective-permute-start | bytes 491528 | tf_op jit(solution)/shard_map/ppermute | solution.py:75
  15.2 1.2 %collective-permute-start.8 = (bf16[4,5,32,128]{3,2,1,0:T(8,128)(2,1)S(1)}, bf16[4,5,32,128]{3,2,1,0:T(8,128)(2,1)S(1)}, u32[]{:S(2)}, u32[]{:S(2)}) collective-permute-start(bf16[4,5,32,128]{3,2,1,0:T(8,128)(2,1)S(1)} %get-tuple-element.31), channel_id=1, source_target_pairs={{0,2},{1,3},{2,0},{3,1},{4,6},{5,7},{6,4},{7,5},{8,10},{9,11},{10,... | collective-permute-start | bytes 491528 | tf_op jit(solution)/shard_map/ppermute | solution.py:75
  16.4 0.0 collective-permute-done.refs_5_
  16.5 0.3 collective-permute-start.9
  16.7 0.0 collective-permute-done.1.refs_6_
  16.8 6.7 %collective-permute-done.2.refs_7_ = bf16[4,5,32,128]{3,2,1,0:T(8,128)(2,1)S(1)} collective-permute-done((bf16[4,5,32,128]{3,2,1,0:T(8,128)(2,1)S(1)}, bf16[4,5,32,128]{3,2,1,0:T(8,128)(2,1)S(1)}, u32[]{:S(2)}, u32[]{:S(2)}) %collective-permute-start.2) | collective-permute-done | bytes 163872 | tf_op jit(solution)/shard_map/ppermute | solution.py:75
  23.5 2.2 %collective-permute-start.5 = (bf16[4,5,32,128]{3,2,1,0:T(8,128)(2,1)S(1)}, bf16[4,5,32,128]{3,2,1,0:T(8,128)(2,1)S(1)}, u32[]{:S(2)}, u32[]{:S(2)}) collective-permute-start(bf16[4,5,32,128]{3,2,1,0:T(8,128)(2,1)S(1)} %pad_maximum_fusion.2), channel_id=1, source_target_pairs={{0,3},{1,2},{2,1},{3,0},{4,7},{5,6},{6,5},{7,4},{8,11},{9,10},{10,... | collective-permute-start | bytes 491528 | tf_op jit(solution)/shard_map/ppermute | solution.py:89
  25.7 0.3 collective-permute-start.4
  26.1 0.0 collective-permute-done.7.refs_5_
  26.1 0.3 collective-permute-start.3
  26.4 0.0 collective-permute-done.8.refs_6_
  26.4 0.0 collective-permute-done.9.refs_7_
  26.5 0.7 collective-permute-start.11
  27.3 0.9 %collective-permute-start.12 = (bf16[4,5,32,128]{3,2,1,0:T(8,128)(2,1)S(1)}, bf16[4,5,32,128]{3,2,1,0:T(8,128)(2,1)S(1)}, u32[]{:S(2)}, u32[]{:S(2)}) collective-permute-start(bf16[4,5,32,128]{3,2,1,0:T(8,128)(2,1)S(1)} %pad_maximum_fusion.5), channel_id=1, source_target_pairs={{0,12},{1,13},{2,14},{3,15},{4,8},{5,9},{6,10},{7,11},{8,4},{9,5},... | collective-permute-start | bytes 491528 | tf_op jit(solution)/shard_map/ppermute | solution.py:89
  28.2 0.5 collective-permute-done.5.refs_10_
  28.7 1.6 %collective-permute-start.10 = (bf16[4,5,32,128]{3,2,1,0:T(8,128)(2,1)S(1)}, bf16[4,5,32,128]{3,2,1,0:T(8,128)(2,1)S(1)}, u32[]{:S(2)}, u32[]{:S(2)}) collective-permute-start(bf16[4,5,32,128]{3,2,1,0:T(8,128)(2,1)S(1)} %pad_maximum_fusion.3), channel_id=1, source_target_pairs={{0,4},{1,5},{2,6},{3,7},{4,0},{5,1},{6,2},{7,3},{8,12},{9,13},{10,... | collective-permute-start | bytes 491528 | tf_op jit(solution)/shard_map/ppermute | solution.py:89
  30.3 2.6 %collective-permute-done.4.refs_9_ = bf16[4,5,32,128]{3,2,1,0:T(8,128)(2,1)S(1)} collective-permute-done((bf16[4,5,32,128]{3,2,1,0:T(8,128)(2,1)S(1)}, bf16[4,5,32,128]{3,2,1,0:T(8,128)(2,1)S(1)}, u32[]{:S(2)}, u32[]{:S(2)}) %collective-permute-start.4) | collective-permute-done | bytes 163872 | tf_op jit(solution)/shard_map/ppermute | solution.py:89
  32.9 0.0 collective-permute-done.3.refs_8_
  32.9 0.0 copy-done.6
  32.9 3.7 %shard_map.69 = (bf16[2,256,256]{2,1,0:T(8,128)(2,1)S(1)}, bf16[4,5,32,128]{3,2,1,0:T(8,128)(2,1)S(1)}, bf16[4,5,32,128]{3,2,1,0:T(8,128)(2,1)}, bf16[4,5,32,128]{3,2,1,0:T(8,128)(2,1)}, bf16[4,5,32,128]{3,2,1,0:T(8,128)(2,1)}) custom-call(s32[1]{0:T(128)} %bitcast.1.refs_0_, s32[32,16]{1,0:T(8,128)S(1)} %bitcast.27, f32[32,16]{1,0:T(8,128)S(1)} %bitcast.35, ...), custom_call_target="tpu_custom_call" | custom-call | flops 1073741824 | bytes 3244032 | tf_op jit(solution)/shard_map/pallas_call | solution.py:274
  36.6 0.7 copy-done.2
  37.3 0.0 collective-permute-start.13
  37.3 2.9 %collective-permute-start.14 = (bf16[4,5,32,128]{3,2,1,0:T(8,128)(2,1)}, bf16[4,5,32,128]{3,2,1,0:T(8,128)(2,1)S(1)}, u32[]{:S(2)}, u32[]{:S(2)}) collective-permute-start(bf16[4,5,32,128]{3,2,1,0:T(8,128)(2,1)} %get-tuple-element.35), channel_id=1, source_target_pairs={{0,8},{1,9},{2,10},{3,11},{4,12},{5,13},{6,14},{7,15},{8,0},{9,1},... | collective-permute-start | bytes 491528 | tf_op jit(solution)/shard_map/ppermute | solution.py:75
  40.2 0.0 collective-permute-done.11.refs_9_
  40.2 0.0 collective-permute-start.15
  40.2 2.1 %collective-permute-done.12.refs_10_ = bf16[4,5,32,128]{3,2,1,0:T(8,128)(2,1)S(1)} collective-permute-done((bf16[4,5,32,128]{3,2,1,0:T(8,128)(2,1)S(1)}, bf16[4,5,32,128]{3,2,1,0:T(8,128)(2,1)S(1)}, u32[]{:S(2)}, u32[]{:S(2)}) %collective-permute-start.12) | collective-permute-done | bytes 163872 | tf_op jit(solution)/shard_map/ppermute | solution.py:89
  42.3 0.0 collective-permute-done.10.refs_8_
  42.3 4.4 %shard_map.71 = (bf16[2,256,256]{2,1,0:T(8,128)(2,1)S(1)}, bf16[16,5,32,128]{3,2,1,0:T(8,128)(2,1)}) custom-call(s32[1]{0:T(128)} %bitcast.1.refs_0_, s32[32,16]{1,0:T(8,128)S(1)} %bitcast.28, f32[32,16]{1,0:T(8,128)S(1)} %bitcast.36, bf16[2,16,256,128]{3,2,1,0:T(8,128)(2,1)S(1)} %bitcast.38, bf16[4,5,32,128]{3,2,1,0:T(8,128)(2,1)S(1)} %get-tuple-element.37.refs_4_, ...), custom_call_target="tpu_custom_call" | custom-call | flops 1073741824 | bytes 3244032 | tf_op jit(solution)/shard_map/pallas_call | solution.py:274
  46.7 0.7 copy-done.4
  47.4 8.0 %all-to-all-start = ((bf16[16,5,32,128]{3,2,1,0:T(8,128)(2,1)}), bf16[16,5,32,128]{3,2,1,0:T(8,128)(2,1)S(1)}, u32[]{:S(2)}, u32[]{:S(2)}) async-start(bf16[16,5,32,128]{3,2,1,0:T(8,128)(2,1)} %get-tuple-element.45), calls=%async_computation | async-start | bytes 1310720 | tf_op jit(solution)/shard_map/all_to_all | solution.py:71
  55.5 0.0 collective-permute-done.13.refs_4_
  55.5 0.0 collective-permute-done.14.refs_5_
  55.5 0.8 collective-permute-done.15.refs_6_
  56.4 0.7 pad_maximum_fusion.8
  57.0 2.2 %collective-permute-start.18 = (bf16[4,5,32,128]{3,2,1,0:T(8,128)(2,1)}, bf16[4,5,32,128]{3,2,1,0:T(8,128)(2,1)}, u32[]{:S(2)}, u32[]{:S(2)}) collective-permute-start(bf16[4,5,32,128]{3,2,1,0:T(8,128)(2,1)} %pad_maximum_fusion.8), channel_id=1, source_target_pairs={{0,3},{1,2},{2,1},{3,0},{4,7},{5,6},{6,5},{7,4},{8,11},{9,10},{10,... | collective-permute-start | bytes 491528 | tf_op jit(solution)/shard_map/ppermute | solution.py:89
  59.2 0.7 pad_maximum_fusion.7
  59.9 1.5 %collective-permute-start.17 = (bf16[4,5,32,128]{3,2,1,0:T(8,128)(2,1)}, bf16[4,5,32,128]{3,2,1,0:T(8,128)(2,1)}, u32[]{:S(2)}, u32[]{:S(2)}) collective-permute-start(bf16[4,5,32,128]{3,2,1,0:T(8,128)(2,1)} %pad_maximum_fusion.7), channel_id=1, source_target_pairs={{0,2},{1,3},{2,0},{3,1},{4,6},{5,7},{6,4},{7,5},{8,10},{9,11},{10,... | collective-permute-start | bytes 491528 | tf_op jit(solution)/shard_map/ppermute | solution.py:89
  61.5 0.7 pad_maximum_fusion.6
  62.1 1.2 %collective-permute-start.16 = (bf16[4,5,32,128]{3,2,1,0:T(8,128)(2,1)}, bf16[4,5,32,128]{3,2,1,0:T(8,128)(2,1)}, u32[]{:S(2)}, u32[]{:S(2)}) collective-permute-start(bf16[4,5,32,128]{3,2,1,0:T(8,128)(2,1)} %pad_maximum_fusion.6), channel_id=1, source_target_pairs={{0,1},{1,0},{2,3},{3,2},{4,5},{5,4},{6,7},{7,6},{8,9},{9,8},{10,11... | collective-permute-start | bytes 491528 | tf_op jit(solution)/shard_map/ppermute | solution.py:89
  63.3 3.0 %all-to-all-done.refs_3_ = bf16[16,5,32,128]{3,2,1,0:T(8,128)(2,1)S(1)} async-done(((bf16[16,5,32,128]{3,2,1,0:T(8,128)(2,1)}), bf16[16,5,32,128]{3,2,1,0:T(8,128)(2,1)S(1)}, u32[]{:S(2)}, u32[]{:S(2)}) %all-to-all-start) | async-done | bytes 655392 | tf_op jit(solution)/shard_map/all_to_all | solution.py:71
  66.3 0.0 copy-done.1
  66.3 2.2 %shard_map.74 = bf16[256,256]{1,0:T(8,128)(2,1)S(1)} custom-call(s32[1]{0:T(128)} %bitcast.1.refs_0_, s32[32,16]{1,0:T(8,128)S(1)} %bitcast.29, bf16[32,256,128]{2,1,0:T(8,128)(2,1)S(1)} %bitcast.21, bf16[16,5,32,128]{3,2,1,0:T(8,128)(2,1)S(1)} %all-to-all-done.refs_3_), custom_call_target="tpu_custom_call" | custom-call | flops 536870912 | bytes 2752512 | tf_op jit(solution)/shard_map/pallas_call | solution.py:286
  68.5 8.2 %collective-permute-start.19 = (bf16[256,256]{1,0:T(8,128)(2,1)S(1)}, bf16[256,256]{1,0:T(8,128)(2,1)S(1)}, u32[]{:S(2)}, u32[]{:S(2)}) collective-permute-start(bf16[256,256]{1,0:T(8,128)(2,1)S(1)} %shard_map.74), channel_id=1, source_target_pairs={{0,16},{16,0},{1,17},{17,1},{2,18},{18,2},{3,19},{19,3},{4,20},{20... | collective-permute-start | bytes 393224 | tf_op jit(solution)/shard_map/ppermute | solution.py:322
  76.7 0.0 copy-done.5
  76.7 0.1 shard_map.72
  76.8 0.9 %reshape.39 = bf16[1,512,2,256]{3,2,1,0:T(2,128)(2,1)} reshape(bf16[512,512]{1,0:T(8,128)(2,1)S(1)} %shard_map.72) | data formatting | bytes 1048576 | tf_op jit(solution)/shard_map/reshape | solution.py:321
  77.7 0.0 collective-permute-done.18.refs_9_
  77.7 0.0 collective-permute-done.17.refs_8_
  77.7 0.0 collective-permute-done.16.refs_7_
  77.7 2.4 %shard_map.73.first_ref = bf16[256,256]{1,0:T(8,128)(2,1)S(1)} custom-call(s32[1]{0:T(128)} %bitcast.1.refs_0_, s32[32,16]{1,0:T(8,128)S(1)} %bitcast.30, bf16[32,256,128]{2,1,0:T(8,128)(2,1)S(1)} %bitcast.22, bf16[4,5,32,128]{3,2,1,0:T(8,128)(2,1)S(1)} %get-tuple-element.33.refs_3_, bf16[4,5,32,128]{3,2,1,0:T(8,128)(2,1)S(1)} %collective-permute-done.13.refs_4_, ...), custom_call_target="tpu_custom_call" | custom-call | flops 536870912 | bytes 3244032 | tf_op jit(solution)/shard_map/pallas_call | solution.py:286
  80.2 0.0 collective-permute-done.19.second_ref
  80.2 0.8 reshape.40
  (28 shorter events, 0.3 us)
Async XLA Ops:
  3.4 1.6 %copy-start = (bf16[1,32,1,256,128]{4,3,2,1,0:T(8,128)(2,1)S(1)}, bf16[1,32,1,256,128]{4,3,2,1,0:T(8,128)(2,1)}, u32[]{:S(2)}) copy-start(bf16[1,32,1,256,128]{4,3,2,1,0:T(8,128)(2,1)} %param.6) | copy-start | bytes 6291460
  6.8 9.6 %collective-permute-start = (bf16[4,5,32,128]{3,2,1,0:T(8,128)(2,1)S(1)}, bf16[4,5,32,128]{3,2,1,0:T(8,128)(2,1)S(1)}, u32[]{:S(2)}, u32[]{:S(2)}) collective-permute-start(bf16[4,5,32,128]{3,2,1,0:T(8,128)(2,1)S(1)} %get-tuple-element.25), channel_id=1, source_target_pairs={{0,4},{1,5},{2,6},{3,7},{4,0},{5,1},{6,2},{7,3},{8,12},{9,13},{10,... | collective-permute-start | bytes 491528 | tf_op jit(solution)/shard_map/ppermute | solution.py:75
  6.9 9.8 %collective-permute-start.1 = (bf16[4,5,32,128]{3,2,1,0:T(8,128)(2,1)S(1)}, bf16[4,5,32,128]{3,2,1,0:T(8,128)(2,1)S(1)}, u32[]{:S(2)}, u32[]{:S(2)}) collective-permute-start(bf16[4,5,32,128]{3,2,1,0:T(8,128)(2,1)S(1)} %get-tuple-element.26), channel_id=1, source_target_pairs={{0,8},{1,9},{2,10},{3,11},{4,12},{5,13},{6,14},{7,15},{8,0},{9,1},... | collective-permute-start | bytes 491528 | tf_op jit(solution)/shard_map/ppermute | solution.py:75
  9.4 14.1 %collective-permute-start.2 = (bf16[4,5,32,128]{3,2,1,0:T(8,128)(2,1)S(1)}, bf16[4,5,32,128]{3,2,1,0:T(8,128)(2,1)S(1)}, u32[]{:S(2)}, u32[]{:S(2)}) collective-permute-start(bf16[4,5,32,128]{3,2,1,0:T(8,128)(2,1)S(1)} %get-tuple-element.27), channel_id=1, source_target_pairs={{0,12},{1,13},{2,14},{3,15},{4,8},{5,9},{6,10},{7,11},{8,4},{9,5},... | collective-permute-start | bytes 491528 | tf_op jit(solution)/shard_map/ppermute | solution.py:75
  9.5 2.5 %collective-permute-start.6 = (bf16[256,2,128]{2,1,0:T(2,128)(2,1)S(1)}, bf16[256,2,128]{2,1,0:T(2,128)(2,1)S(1)}, u32[]{:S(2)}, u32[]{:S(2)}) collective-permute-start(bf16[256,2,128]{2,1,0:T(2,128)(2,1)S(1)} %get-tuple-element.46), channel_id=1, source_target_pairs={{0,16},{16,0},{1,17},{17,1},{2,18},{18,2},{3,19},{19,3},{4,20},{20... | collective-permute-start | bytes 393224 | tf_op jit(solution)/shard_map/ppermute | solution.py:307
  13.9 19.0 %copy-start.6 = (bf16[1,2,16,256,128]{4,3,2,1,0:T(8,128)(2,1)S(1)}, bf16[1,2,16,256,128]{4,3,2,1,0:T(8,128)(2,1)}, u32[]{:S(2)}) copy-start(bf16[1,2,16,256,128]{4,3,2,1,0:T(8,128)(2,1)} %param.7) | copy-start | bytes 6291460
  13.9 12.1 %collective-permute-start.7 = (bf16[4,5,32,128]{3,2,1,0:T(8,128)(2,1)S(1)}, bf16[4,5,32,128]{3,2,1,0:T(8,128)(2,1)S(1)}, u32[]{:S(2)}, u32[]{:S(2)}) collective-permute-start(bf16[4,5,32,128]{3,2,1,0:T(8,128)(2,1)S(1)} %get-tuple-element.30), channel_id=1, source_target_pairs={{0,1},{1,0},{2,3},{3,2},{4,5},{5,4},{6,7},{7,6},{8,9},{9,8},{10,11... | collective-permute-start | bytes 491528 | tf_op jit(solution)/shard_map/ppermute | solution.py:75
  15.2 11.2 %collective-permute-start.8 = (bf16[4,5,32,128]{3,2,1,0:T(8,128)(2,1)S(1)}, bf16[4,5,32,128]{3,2,1,0:T(8,128)(2,1)S(1)}, u32[]{:S(2)}, u32[]{:S(2)}) collective-permute-start(bf16[4,5,32,128]{3,2,1,0:T(8,128)(2,1)S(1)} %get-tuple-element.31), channel_id=1, source_target_pairs={{0,2},{1,3},{2,0},{3,1},{4,6},{5,7},{6,4},{7,5},{8,10},{9,11},{10,... | collective-permute-start | bytes 491528 | tf_op jit(solution)/shard_map/ppermute | solution.py:75
  16.5 10.0 %collective-permute-start.9 = (bf16[4,5,32,128]{3,2,1,0:T(8,128)(2,1)S(1)}, bf16[4,5,32,128]{3,2,1,0:T(8,128)(2,1)S(1)}, u32[]{:S(2)}, u32[]{:S(2)}) collective-permute-start(bf16[4,5,32,128]{3,2,1,0:T(8,128)(2,1)S(1)} %get-tuple-element.32), channel_id=1, source_target_pairs={{0,3},{1,2},{2,1},{3,0},{4,7},{5,6},{6,5},{7,4},{8,11},{9,10},{10,... | collective-permute-start | bytes 491528 | tf_op jit(solution)/shard_map/ppermute | solution.py:75
  23.5 5.2 %collective-permute-start.5 = (bf16[4,5,32,128]{3,2,1,0:T(8,128)(2,1)S(1)}, bf16[4,5,32,128]{3,2,1,0:T(8,128)(2,1)S(1)}, u32[]{:S(2)}, u32[]{:S(2)}) collective-permute-start(bf16[4,5,32,128]{3,2,1,0:T(8,128)(2,1)S(1)} %pad_maximum_fusion.2), channel_id=1, source_target_pairs={{0,3},{1,2},{2,1},{3,0},{4,7},{5,6},{6,5},{7,4},{8,11},{9,10},{10,... | collective-permute-start | bytes 491528 | tf_op jit(solution)/shard_map/ppermute | solution.py:89
  25.7 7.2 %collective-permute-start.4 = (bf16[4,5,32,128]{3,2,1,0:T(8,128)(2,1)S(1)}, bf16[4,5,32,128]{3,2,1,0:T(8,128)(2,1)S(1)}, u32[]{:S(2)}, u32[]{:S(2)}) collective-permute-start(bf16[4,5,32,128]{3,2,1,0:T(8,128)(2,1)S(1)} %pad_maximum_fusion.1), channel_id=1, source_target_pairs={{0,2},{1,3},{2,0},{3,1},{4,6},{5,7},{6,4},{7,5},{8,10},{9,11},{10,... | collective-permute-start | bytes 491528 | tf_op jit(solution)/shard_map/ppermute | solution.py:89
  26.1 6.8 %collective-permute-start.3 = (bf16[4,5,32,128]{3,2,1,0:T(8,128)(2,1)S(1)}, bf16[4,5,32,128]{3,2,1,0:T(8,128)(2,1)S(1)}, u32[]{:S(2)}, u32[]{:S(2)}) collective-permute-start(bf16[4,5,32,128]{3,2,1,0:T(8,128)(2,1)S(1)} %pad_maximum_fusion), channel_id=1, source_target_pairs={{0,1},{1,0},{2,3},{3,2},{4,5},{5,4},{6,7},{7,6},{8,9},{9,8},{10,11... | collective-permute-start | bytes 491528 | tf_op jit(solution)/shard_map/ppermute | solution.py:89
  26.5 13.7 %collective-permute-start.11 = (bf16[4,5,32,128]{3,2,1,0:T(8,128)(2,1)S(1)}, bf16[4,5,32,128]{3,2,1,0:T(8,128)(2,1)S(1)}, u32[]{:S(2)}, u32[]{:S(2)}) collective-permute-start(bf16[4,5,32,128]{3,2,1,0:T(8,128)(2,1)S(1)} %pad_maximum_fusion.4), channel_id=1, source_target_pairs={{0,8},{1,9},{2,10},{3,11},{4,12},{5,13},{6,14},{7,15},{8,0},{9,1},... | collective-permute-start | bytes 491528 | tf_op jit(solution)/shard_map/ppermute | solution.py:89
  27.3 15.0 %collective-permute-start.12 = (bf16[4,5,32,128]{3,2,1,0:T(8,128)(2,1)S(1)}, bf16[4,5,32,128]{3,2,1,0:T(8,128)(2,1)S(1)}, u32[]{:S(2)}, u32[]{:S(2)}) collective-permute-start(bf16[4,5,32,128]{3,2,1,0:T(8,128)(2,1)S(1)} %pad_maximum_fusion.5), channel_id=1, source_target_pairs={{0,12},{1,13},{2,14},{3,15},{4,8},{5,9},{6,10},{7,11},{8,4},{9,5},... | collective-permute-start | bytes 491528 | tf_op jit(solution)/shard_map/ppermute | solution.py:89
  28.7 13.6 %collective-permute-start.10 = (bf16[4,5,32,128]{3,2,1,0:T(8,128)(2,1)S(1)}, bf16[4,5,32,128]{3,2,1,0:T(8,128)(2,1)S(1)}, u32[]{:S(2)}, u32[]{:S(2)}) collective-permute-start(bf16[4,5,32,128]{3,2,1,0:T(8,128)(2,1)S(1)} %pad_maximum_fusion.3), channel_id=1, source_target_pairs={{0,4},{1,5},{2,6},{3,7},{4,0},{5,1},{6,2},{7,3},{8,12},{9,13},{10,... | collective-permute-start | bytes 491528 | tf_op jit(solution)/shard_map/ppermute | solution.py:89
  36.6 0.7 copy-start.2
  37.3 18.2 %collective-permute-start.13 = (bf16[4,5,32,128]{3,2,1,0:T(8,128)(2,1)}, bf16[4,5,32,128]{3,2,1,0:T(8,128)(2,1)S(1)}, u32[]{:S(2)}, u32[]{:S(2)}) collective-permute-start(bf16[4,5,32,128]{3,2,1,0:T(8,128)(2,1)} %get-tuple-element.34), channel_id=1, source_target_pairs={{0,4},{1,5},{2,6},{3,7},{4,0},{5,1},{6,2},{7,3},{8,12},{9,13},{10,... | collective-permute-start | bytes 491528 | tf_op jit(solution)/shard_map/ppermute | solution.py:75
  37.3 18.2 %collective-permute-start.14 = (bf16[4,5,32,128]{3,2,1,0:T(8,128)(2,1)}, bf16[4,5,32,128]{3,2,1,0:T(8,128)(2,1)S(1)}, u32[]{:S(2)}, u32[]{:S(2)}) collective-permute-start(bf16[4,5,32,128]{3,2,1,0:T(8,128)(2,1)} %get-tuple-element.35), channel_id=1, source_target_pairs={{0,8},{1,9},{2,10},{3,11},{4,12},{5,13},{6,14},{7,15},{8,0},{9,1},... | collective-permute-start | bytes 491528 | tf_op jit(solution)/shard_map/ppermute | solution.py:75
  40.2 16.1 %collective-permute-start.15 = (bf16[4,5,32,128]{3,2,1,0:T(8,128)(2,1)}, bf16[4,5,32,128]{3,2,1,0:T(8,128)(2,1)S(1)}, u32[]{:S(2)}, u32[]{:S(2)}) collective-permute-start(bf16[4,5,32,128]{3,2,1,0:T(8,128)(2,1)} %get-tuple-element.36), channel_id=1, source_target_pairs={{0,12},{1,13},{2,14},{3,15},{4,8},{5,9},{6,10},{7,11},{8,4},{9,5},... | collective-permute-start | bytes 491528 | tf_op jit(solution)/shard_map/ppermute | solution.py:75
  46.7 0.7 copy-start.4
  47.4 18.9 %copy-start.1 = (bf16[1,32,1,256,128]{4,3,2,1,0:T(8,128)(2,1)S(1)}, bf16[1,32,1,256,128]{4,3,2,1,0:T(8,128)(2,1)}, u32[]{:S(2)}) copy-start(bf16[1,32,1,256,128]{4,3,2,1,0:T(8,128)(2,1)} %param.6) | copy-start | bytes 6291460
  47.4 18.9 %all-to-all-start = ((bf16[16,5,32,128]{3,2,1,0:T(8,128)(2,1)}), bf16[16,5,32,128]{3,2,1,0:T(8,128)(2,1)S(1)}, u32[]{:S(2)}, u32[]{:S(2)}) async-start(bf16[16,5,32,128]{3,2,1,0:T(8,128)(2,1)} %get-tuple-element.45), calls=%async_computation | async-start | bytes 1310720 | tf_op jit(solution)/shard_map/all_to_all | solution.py:71
  57.0 20.7 %collective-permute-start.18 = (bf16[4,5,32,128]{3,2,1,0:T(8,128)(2,1)}, bf16[4,5,32,128]{3,2,1,0:T(8,128)(2,1)}, u32[]{:S(2)}, u32[]{:S(2)}) collective-permute-start(bf16[4,5,32,128]{3,2,1,0:T(8,128)(2,1)} %pad_maximum_fusion.8), channel_id=1, source_target_pairs={{0,3},{1,2},{2,1},{3,0},{4,7},{5,6},{6,5},{7,4},{8,11},{9,10},{10,... | collective-permute-start | bytes 491528 | tf_op jit(solution)/shard_map/ppermute | solution.py:89
  59.9 17.8 %collective-permute-start.17 = (bf16[4,5,32,128]{3,2,1,0:T(8,128)(2,1)}, bf16[4,5,32,128]{3,2,1,0:T(8,128)(2,1)}, u32[]{:S(2)}, u32[]{:S(2)}) collective-permute-start(bf16[4,5,32,128]{3,2,1,0:T(8,128)(2,1)} %pad_maximum_fusion.7), channel_id=1, source_target_pairs={{0,2},{1,3},{2,0},{3,1},{4,6},{5,7},{6,4},{7,5},{8,10},{9,11},{10,... | collective-permute-start | bytes 491528 | tf_op jit(solution)/shard_map/ppermute | solution.py:89
  62.1 15.6 %collective-permute-start.16 = (bf16[4,5,32,128]{3,2,1,0:T(8,128)(2,1)}, bf16[4,5,32,128]{3,2,1,0:T(8,128)(2,1)}, u32[]{:S(2)}, u32[]{:S(2)}) collective-permute-start(bf16[4,5,32,128]{3,2,1,0:T(8,128)(2,1)} %pad_maximum_fusion.6), channel_id=1, source_target_pairs={{0,1},{1,0},{2,3},{3,2},{4,5},{5,4},{6,7},{7,6},{8,9},{9,8},{10,11... | collective-permute-start | bytes 491528 | tf_op jit(solution)/shard_map/ppermute | solution.py:89
  66.3 10.4 %copy-start.3 = (bf16[2,256,256]{2,1,0:T(8,128)(2,1)S(1)}, bf16[2,256,256]{2,1,0:T(8,128)(2,1)}, u32[]{:S(2)}) copy-start(bf16[2,256,256]{2,1,0:T(8,128)(2,1)} %copy-done.2) | copy-start | bytes 786436
  66.3 10.4 %copy-start.5 = (bf16[2,256,256]{2,1,0:T(8,128)(2,1)S(1)}, bf16[2,256,256]{2,1,0:T(8,128)(2,1)}, u32[]{:S(2)}) copy-start(bf16[2,256,256]{2,1,0:T(8,128)(2,1)} %copy-done.4) | copy-start | bytes 786436
  68.5 11.7 %collective-permute-start.19 = (bf16[256,256]{1,0:T(8,128)(2,1)S(1)}, bf16[256,256]{1,0:T(8,128)(2,1)S(1)}, u32[]{:S(2)}, u32[]{:S(2)}) collective-permute-start(bf16[256,256]{1,0:T(8,128)(2,1)S(1)} %shard_map.74), channel_id=1, source_target_pairs={{0,16},{16,0},{1,17},{17,1},{2,18},{18,2},{3,19},{19,3},{4,20},{20... | collective-permute-start | bytes 393224 | tf_op jit(solution)/shard_map/ppermute | solution.py:322

commit v4 on v3

--- a/solution.py
+++ b/solution.py
@@ -48,7 +48,7 @@
 
 
 def counts_of(ranks_ref, group, column):
-    return ranks_ref[2 * group, column] // RB, ranks_ref[2 * group + 1, column] // RB
+    return ranks_ref[column, 2 * group] // RB, ranks_ref[column, 2 * group + 1] // RB
 
 
 def far_first(tiles):
@@ -89,7 +89,7 @@
         return lax.ppermute(block, "tile", [(i, i ^ offset) for i in range(tiles)])
 
     hops = {b: swap(sends[b - 1], b * s2) for b in range(1, count_b)}
-    return first + [hops[b] for b in range(1, count_b)]
+    return first + [hops[b] for b in reversed(range(1, count_b))]
 
 
 def after(values, others):
@@ -119,7 +119,7 @@
     for a in range(count_a):
         visit(me ^ (a * s1), lambda slot, a=a: refs[a][0, slot])
     for b in range(1, count_b):
-        ref = refs[count_a + b - 1]
+        ref = refs[count_a + count_b - 1 - b]
 
         def step(a, carry, ref=ref, b=b):
             visit(me ^ (a * s1) ^ (b * s2), lambda slot: ref[a, slot])
@@ -150,7 +150,7 @@
         code_tiles(
             [v_ref[2 * group], v_ref[2 * group + 1]],
             [wave, wave],
-            [scale_ref[2 * group, me], scale_ref[2 * group + 1, me]],
+            [scale_ref[me, 2 * group], scale_ref[me, 2 * group + 1]],
             first,
             store,
         )
@@ -190,7 +190,7 @@
         code_tiles(
             [u_ref[0, column], u_ref[1, column]],
             [y_ref[0], y_ref[1]],
-            [scale_ref[2 * me, column], scale_ref[2 * me + 1, column]],
+            [scale_ref[column, 2 * me], scale_ref[column, 2 * me + 1]],
             first,
             store,
         )
@@ -244,17 +244,17 @@
     me = lax.axis_index("tile").astype(jnp.int32).reshape(1)
     v = column_basis.reshape(column_basis.shape[1], *column_basis.shape[3:])
     u = row_basis[0]
-    scales, ranks = tile_scale[0], tile_ranks[0]
+    scales, ranks = tile_scale[0].T, tile_ranks[0].T
     height, width = v.shape[1], v.shape[2]
     n = wave_in.shape[3]
     slots = (CAP, 2 * RB, n)
     swap = [(0, 1), (1, 0)]
     way = {name: pick(tiles) for name, pick in WAYS.items()}
 
-    def cost(products, operands):
+    def cost(products, operands, weight=1):
         return pl.CostEstimate(
-            flops=4 * products * tiles * height * width * 2 * n,
-            bytes_accessed=sum(a.size * a.dtype.itemsize for a in operands),
+            flops=weight * 4 * products * tiles * height * width * 2 * n,
+            bytes_accessed=weight * sum(a.size * a.dtype.itemsize for a in operands),
             transcendentals=0,
         )
 
@@ -278,7 +278,7 @@
             out_specs=[VMEM] * (1 + len(shapes)),
             scratch_shapes=[pltpu.VMEM((2, tiles, width, 2 * n), jnp.bfloat16)],
             compiler_params=params(),
-            cost_estimate=cost(2, [u, *arrived]),
+            cost_estimate=cost(2, [u, *arrived], 10),
         )(me, ranks, scales, u, *arrived)
         return result[0].reshape(2 * height, 2 * n), result[1:]
 
@@ -305,8 +305,10 @@
     theirs = lax.dynamic_index_in_dim(wave_in, 1 - core, 0, keepdims=False)
     mine = lax.dynamic_index_in_dim(wave_in, core, 0, keepdims=False)
     other = lax.ppermute(theirs, "freq", swap)
-    first_a, sends_a = exchange(code(mine.reshape(height, 2 * n), way["1a"]), way["1a"], tiles)
-    first_b, sends_b = exchange(code(other.reshape(height, 2 * n), way["1b"]), way["1b"], tiles)
+    coded_a = code(other.reshape(height, 2 * n), way["1a"])
+    first_a, sends_a = exchange(coded_a, way["1a"], tiles)
+    (mine,) = after([mine], coded_a)
+    first_b, sends_b = exchange(code(mine.reshape(height, 2 * n), way["1b"]), way["1b"], tiles)
     coded_a = second_hop(first_a, sends_a, way["1a"], tiles)
     coded_b = second_hop(first_b, sends_b, way["1b"], tiles)
     y_a, back_a = middle(coded_a, way["1a"], way["2a"])
@@ -316,11 +318,11 @@
     first_b, sends_b = exchange(back_b, way["2b"], tiles)
     back_a = second_hop(first_a, sends_a, way["2a"], tiles)
     back_b = second_hop(first_b, sends_b, way["2b"], tiles)
-    z_a = adjoint(back_a, way["2a"])
-    forward_out = ordered(order_rows_kernel, y_a, y_b, (2 * height, 4 * n))
+    z_a = lax.ppermute(adjoint(back_a, way["2a"]), "freq", swap)
+    forward_out = ordered(order_rows_kernel, y_b, y_a, (2 * height, 4 * n))
     forward_out = forward_out.reshape(1, 2 * height, 2, 2 * n)
-    z_b = lax.ppermute(adjoint(back_b, way["2b"]), "freq", swap)
-    adjoint_out = ordered(order_parts_kernel, z_a, z_b, (2, height, 2 * n))
+    z_b = adjoint(back_b, way["2b"])
+    adjoint_out = ordered(order_parts_kernel, z_b, z_a, (2, height, 2 * n))
     return forward_out, adjoint_out.reshape(2, height, 2, n)
 
 

time: 82.3 us -> 81.6 us (level); the launches traced: 81 us -> 81.2 us
  waiting for transfers between devices: 16.6 us -> 24.3 us
  starting transfers between devices: 37.2 us -> 33.5 us
  other arithmetic: 2.21 us -> 0.22 us
  Pallas kernels: 16.6 us -> 14.9 us
    ppermute x18, waiting for transfers between devices: 12.7 us -> 23.3 us  [swap(): return lax.ppermute(block, 'tile', [(i, i ^ offset) for i in range(tiles)])]
    all_to_all x1, waiting for transfers between devices: 2.99 us -> 0.01 us  [exchange(): lax.all_to_all(blocks[0], 'tile', split_axis=0, concat_axis=0, tiled=True)]
    another operation x9, other arithmetic: 2.21 us -> 0.22 us  [exchange(): jnp.stack([first[a][b] for a in range(count_a)])]
    ppermute x1, starting transfers between devices: 8.21 us -> 6.87 us  [per_device(): z_a = lax.ppermute(adjoint(back_a, way['2a']), 'freq', swap)]
    all_to_all x1, starting transfers between devices: 8.03 us -> 6.88 us  [exchange(): lax.all_to_all(blocks[0], 'tile', split_axis=0, concat_axis=0, tiled=True)]
    unnamed x18 -> x22, local copies, waits for them, and re-layouts: 4.6 us -> 4.45 us
  transfers between devices with their start and end apart: 21 -> 21, of which waited for: 7 -> 8; matrix products, arithmetic and copies ran while one was open for 4% -> 2% of each run, Pallas kernels for 18% -> 16%
where the time goes in v4:
time: 81.6 us; the launch traced here: 81.2 us
  starting transfers between devices  33.5 us (41%)
  waiting for transfers between devices  24.3 us (30%)
  Pallas kernels  14.9 us (18%)
  local copies, waits for them, and re-layouts  7.4 us (9%)
  between operations  0.94 us (1%)
    ppermute x18, waiting for transfers between devices, swap(): return lax.ppermute(block, 'tile', [(i, i ^ offset) for i in range(tiles)])  23.3 us
    ppermute x18, starting transfers between devices, swap(): return lax.ppermute(block, 'tile', [(i, i ^ offset) for i in range(tiles)])  19 us
    pallas_call x2, Pallas kernels, middle(): pl.pallas_call(lambda *refs: middle_kernel(route_in, route_out, tiles, *r...  7.55 us
    all_to_all x1, starting transfers between devices, exchange(): lax.all_to_all(blocks[0], 'tile', split_axis=0, concat_axis=0, tiled=True)  6.88 us
    ppermute x1, starting transfers between devices, per_device(): z_a = lax.ppermute(adjoint(back_a, way['2a']), 'freq', swap)  6.87 us
    unnamed x22, local copies, waits for them, and re-layouts  4.45 us
    pallas_call x2, Pallas kernels, adjoint(): pl.pallas_call(lambda *refs: adjoint_kernel(route, tiles, *refs), out_sha...  4.09 us
    pallas_call x2, Pallas kernels, code(): pl.pallas_call(lambda *refs: coded_kernel(route, *refs), out_shape=shapes...  3.14 us
  transfers between devices with their start and end apart: 21, of which 8 were waited for; matrix products, arithmetic and copies ran while one was open for 2% of the time, Pallas kernels for 16%

profile of v4, /device:TPU:9, one launch (start us, length us, event | category | flops | bytes accessed | tf_op | source)
XLA Modules:
  0.0 81.2 jit_solution(10615978974360912486)
XLA Ops:
  0.6 1.2 %dynamic-slice_bitcast_fusion = (bf16[256,2,128]{2,1,0:T(2,128)(2,1)S(1)}, bf16[256,2,128]{2,1,0:T(2,128)(2,1)S(1)}) fusion(bf16[2,256,2,128]{3,2,1,0:T(2,128)(2,1)} %param.5, s32[]{:T(128)S(6)} %select_n.8, s32[]{:T(128)S(6)} %select_n.7), kind=kLoop, calls=%fused_computation.11 | loop fusion | bytes 524296 | tf_op jit(solution)/shard_map/jit(dynamic_index_in_dim)/squeeze | solution.py:305
  1.8 0.7 collective-permute-start
  2.5 1.0 %collective-permute-done = bf16[256,2,128]{2,1,0:T(2,128)(2,1)S(1)} collective-permute-done((bf16[256,2,128]{2,1,0:T(2,128)(2,1)S(1)}, bf16[256,2,128]{2,1,0:T(2,128)(2,1)S(1)}, u32[]{:S(2)}, u32[]{:S(2)}) %collective-permute-start) | collective-permute-done | bytes 131104 | tf_op jit(solution)/shard_map/ppermute | solution.py:307
  3.5 0.0 copy-start
  3.6 1.6 %copy-done = bf16[1,32,1,256,128]{4,3,2,1,0:T(8,128)(2,1)S(1)} copy-done((bf16[1,32,1,256,128]{4,3,2,1,0:T(8,128)(2,1)S(1)}, bf16[1,32,1,256,128]{4,3,2,1,0:T(8,128)(2,1)}, u32[]{:S(2)}) %copy-start) | copy-done | bytes 2097176
  5.1 0.7 copy-done.6
  5.8 0.7 copy-done.8
  6.5 1.6 %shard_map.68 = (bf16[4,5,32,128]{3,2,1,0:T(8,128)(2,1)S(1)}, bf16[4,5,32,128]{3,2,1,0:T(8,128)(2,1)S(1)}, bf16[4,5,32,128]{3,2,1,0:T(8,128)(2,1)S(1)}, bf16[4,5,32,128]{3,2,1,0:T(8,128)(2,1)S(1)}) custom-call(s32[1]{0:T(128)} %bitcast.1.refs_0_, s32[16,32]{1,0:T(8,128)S(1)} %bitcast.32, f32[16,32]{1,0:T(8,128)S(1)} %bitcast.38, ...), custom_call_target="tpu_custom_call" | custom-call | flops 536870912 | bytes 2228224 | tf_op jit(solution)/shard_map/pallas_call | solution.py:263
  8.1 0.1 collective-permute-start.7
  8.2 2.5 %collective-permute-start.8 = (bf16[4,5,32,128]{3,2,1,0:T(8,128)(2,1)S(1)}, bf16[4,5,32,128]{3,2,1,0:T(8,128)(2,1)S(1)}, u32[]{:S(2)}, u32[]{:S(2)}) collective-permute-start(bf16[4,5,32,128]{3,2,1,0:T(8,128)(2,1)S(1)} %get-tuple-element.27), channel_id=1, source_target_pairs={{0,8},{1,9},{2,10},{3,11},{4,12},{5,13},{6,14},{7,15},{8,0},{9,1},... | collective-permute-start | bytes 491528 | tf_op jit(solution)/shard_map/ppermute | solution.py:75
  10.7 0.2 collective-permute-start.9
  10.9 1.6 %shard_map.69 = (bf16[4,5,32,128]{3,2,1,0:T(8,128)(2,1)S(1)}, bf16[4,5,32,128]{3,2,1,0:T(8,128)(2,1)S(1)}, bf16[4,5,32,128]{3,2,1,0:T(8,128)(2,1)S(1)}, bf16[4,5,32,128]{3,2,1,0:T(8,128)(2,1)S(1)}) custom-call(s32[1]{0:T(128)} %bitcast.1.refs_0_, s32[16,32]{1,0:T(8,128)S(1)} %bitcast.33, f32[16,32]{1,0:T(8,128)S(1)} %bitcast.39, ...), custom_call_target="tpu_custom_call" | custom-call | flops 536870912 | bytes 2228224 | tf_op jit(solution)/shard_map/pallas_call | solution.py:263
  12.4 0.0 copy-start.9
  12.5 1.3 %collective-permute-start.1 = (bf16[4,5,32,128]{3,2,1,0:T(8,128)(2,1)S(1)}, bf16[4,5,32,128]{3,2,1,0:T(8,128)(2,1)S(1)}, u32[]{:S(2)}, u32[]{:S(2)}) collective-permute-start(bf16[4,5,32,128]{3,2,1,0:T(8,128)(2,1)S(1)} %get-tuple-element.31), channel_id=1, source_target_pairs={{0,1},{1,0},{2,3},{3,2},{4,5},{5,4},{6,7},{7,6},{8,9},{9,8},{10,11... | collective-permute-start | bytes 491528 | tf_op jit(solution)/shard_map/ppermute | solution.py:75
  13.7 1.2 %collective-permute-start.2 = (bf16[4,5,32,128]{3,2,1,0:T(8,128)(2,1)S(1)}, bf16[4,5,32,128]{3,2,1,0:T(8,128)(2,1)S(1)}, u32[]{:S(2)}, u32[]{:S(2)}) collective-permute-start(bf16[4,5,32,128]{3,2,1,0:T(8,128)(2,1)S(1)} %get-tuple-element.32), channel_id=1, source_target_pairs={{0,2},{1,3},{2,0},{3,1},{4,6},{5,7},{6,4},{7,5},{8,10},{9,11},{10,... | collective-permute-start | bytes 491528 | tf_op jit(solution)/shard_map/ppermute | solution.py:75
  15.0 0.0 collective-permute-done.7.refs_5_
  15.0 1.1 %collective-permute-start.3 = (bf16[4,5,32,128]{3,2,1,0:T(8,128)(2,1)S(1)}, bf16[4,5,32,128]{3,2,1,0:T(8,128)(2,1)S(1)}, u32[]{:S(2)}, u32[]{:S(2)}) collective-permute-start(bf16[4,5,32,128]{3,2,1,0:T(8,128)(2,1)S(1)} %get-tuple-element.33), channel_id=1, source_target_pairs={{0,3},{1,2},{2,1},{3,0},{4,7},{5,6},{6,5},{7,4},{8,11},{9,10},{10,... | collective-permute-start | bytes 491528 | tf_op jit(solution)/shard_map/ppermute | solution.py:75
  16.1 2.1 %collective-permute-done.8.refs_6_ = bf16[4,5,32,128]{3,2,1,0:T(8,128)(2,1)S(1)} collective-permute-done((bf16[4,5,32,128]{3,2,1,0:T(8,128)(2,1)S(1)}, bf16[4,5,32,128]{3,2,1,0:T(8,128)(2,1)S(1)}, u32[]{:S(2)}, u32[]{:S(2)}) %collective-permute-start.8) | collective-permute-done | bytes 163872 | tf_op jit(solution)/shard_map/ppermute | solution.py:75
  18.2 6.9 %collective-permute-done.9.refs_7_ = bf16[4,5,32,128]{3,2,1,0:T(8,128)(2,1)S(1)} collective-permute-done((bf16[4,5,32,128]{3,2,1,0:T(8,128)(2,1)S(1)}, bf16[4,5,32,128]{3,2,1,0:T(8,128)(2,1)S(1)}, u32[]{:S(2)}, u32[]{:S(2)}) %collective-permute-start.9) | collective-permute-done | bytes 163872 | tf_op jit(solution)/shard_map/ppermute | solution.py:75
  25.2 2.2 %collective-permute-start.10 = (bf16[4,5,32,128]{3,2,1,0:T(8,128)(2,1)S(1)}, bf16[4,5,32,128]{3,2,1,0:T(8,128)(2,1)S(1)}, u32[]{:S(2)}, u32[]{:S(2)}) collective-permute-start(bf16[4,5,32,128]{3,2,1,0:T(8,128)(2,1)S(1)} %pad_maximum_fusion.3), channel_id=1, source_target_pairs={{0,3},{1,2},{2,1},{3,0},{4,7},{5,6},{6,5},{7,4},{8,11},{9,10},{10,... | collective-permute-start | bytes 491528 | tf_op jit(solution)/shard_map/ppermute | solution.py:89
  27.4 0.3 collective-permute-start.11
  27.7 0.0 collective-permute-done.1.refs_5_
  27.7 0.3 collective-permute-start.12
  28.1 0.0 collective-permute-done.2.refs_6_
  28.1 0.0 collective-permute-done.3.refs_7_
  28.2 1.4 %collective-permute-start.4 = (bf16[4,5,32,128]{3,2,1,0:T(8,128)(2,1)S(1)}, bf16[4,5,32,128]{3,2,1,0:T(8,128)(2,1)S(1)}, u32[]{:S(2)}, u32[]{:S(2)}) collective-permute-start(bf16[4,5,32,128]{3,2,1,0:T(8,128)(2,1)S(1)} %pad_maximum_fusion), channel_id=1, source_target_pairs={{0,12},{1,13},{2,14},{3,15},{4,8},{5,9},{6,10},{7,11},{8,4},{9,5},... | collective-permute-start | bytes 491528 | tf_op jit(solution)/shard_map/ppermute | solution.py:89
  29.5 0.1 collective-permute-start.5
  29.7 0.7 collective-permute-done.10.refs_8_
  30.3 0.7 collective-permute-start.6
  31.1 4.1 %collective-permute-done.11.refs_9_ = bf16[4,5,32,128]{3,2,1,0:T(8,128)(2,1)S(1)} collective-permute-done((bf16[4,5,32,128]{3,2,1,0:T(8,128)(2,1)S(1)}, bf16[4,5,32,128]{3,2,1,0:T(8,128)(2,1)S(1)}, u32[]{:S(2)}, u32[]{:S(2)}) %collective-permute-start.11) | collective-permute-done | bytes 163872 | tf_op jit(solution)/shard_map/ppermute | solution.py:89
  35.1 0.0 collective-permute-done.12.refs_10_
  35.1 0.0 copy-done.9
  35.1 3.4 %shard_map.70 = (bf16[2,256,256]{2,1,0:T(8,128)(2,1)S(1)}, bf16[4,5,32,128]{3,2,1,0:T(8,128)(2,1)S(1)}, bf16[4,5,32,128]{3,2,1,0:T(8,128)(2,1)}, bf16[4,5,32,128]{3,2,1,0:T(8,128)(2,1)}, bf16[4,5,32,128]{3,2,1,0:T(8,128)(2,1)}) custom-call(s32[1]{0:T(128)} %bitcast.1.refs_0_, s32[16,32]{1,0:T(8,128)S(1)} %bitcast.34, f32[16,32]{1,0:T(8,128)S(1)} %bitcast.40, ...), custom_call_target="tpu_custom_call" | custom-call | flops 10737418240 | bytes 32440320 | tf_op jit(solution)/shard_map/pallas_call | solution.py:274
  38.5 0.7 copy-done.2
  39.2 0.0 collective-permute-start.13
  39.2 2.5 %collective-permute-start.14 = (bf16[4,5,32,128]{3,2,1,0:T(8,128)(2,1)}, bf16[4,5,32,128]{3,2,1,0:T(8,128)(2,1)S(1)}, u32[]{:S(2)}, u32[]{:S(2)}) collective-permute-start(bf16[4,5,32,128]{3,2,1,0:T(8,128)(2,1)} %get-tuple-element.36), channel_id=1, source_target_pairs={{0,8},{1,9},{2,10},{3,11},{4,12},{5,13},{6,14},{7,15},{8,0},{9,1},... | collective-permute-start | bytes 491528 | tf_op jit(solution)/shard_map/ppermute | solution.py:75
  41.7 0.0 collective-permute-done.4.refs_8_
  41.7 0.2 collective-permute-start.15
  41.9 0.0 collective-permute-done.5.refs_9_
  41.9 0.0 collective-permute-done.6.refs_10_
  41.9 4.2 %shard_map.71 = (bf16[2,256,256]{2,1,0:T(8,128)(2,1)S(1)}, bf16[16,5,32,128]{3,2,1,0:T(8,128)(2,1)}) custom-call(s32[1]{0:T(128)} %bitcast.1.refs_0_, s32[16,32]{1,0:T(8,128)S(1)} %bitcast.35, f32[16,32]{1,0:T(8,128)S(1)} %bitcast.41, bf16[2,16,256,128]{3,2,1,0:T(8,128)(2,1)S(1)} %bitcast.43, bf16[4,5,32,128]{3,2,1,0:T(8,128)(2,1)S(1)} %get-tuple-element.38.refs_4_, ...), custom_call_target="tpu_custom_call" | custom-call | flops 10737418240 | bytes 32440320 | tf_op jit(solution)/shard_map/pallas_call | solution.py:274
  46.0 0.7 copy-done.4
  46.8 6.9 %all-to-all-start = ((bf16[16,5,32,128]{3,2,1,0:T(8,128)(2,1)}), bf16[16,5,32,128]{3,2,1,0:T(8,128)(2,1)S(1)}, u32[]{:S(2)}, u32[]{:S(2)}) async-start(bf16[16,5,32,128]{3,2,1,0:T(8,128)(2,1)} %get-tuple-element.47), calls=%async_computation | async-start | bytes 1310720 | tf_op jit(solution)/shard_map/all_to_all | solution.py:71
  53.6 0.0 collective-permute-done.13.refs_4_
  53.7 0.0 collective-permute-done.14.refs_5_
  53.7 1.6 %collective-permute-done.15.refs_6_ = bf16[4,5,32,128]{3,2,1,0:T(8,128)(2,1)S(1)} collective-permute-done((bf16[4,5,32,128]{3,2,1,0:T(8,128)(2,1)}, bf16[4,5,32,128]{3,2,1,0:T(8,128)(2,1)S(1)}, u32[]{:S(2)}, u32[]{:S(2)}) %collective-permute-start.15) | collective-permute-done | bytes 163872 | tf_op jit(solution)/shard_map/ppermute | solution.py:75
  55.4 0.0 copy-start.3
  55.4 0.0 copy-start.5
  55.4 4.6 %collective-permute-start.16 = (bf16[4,5,32,128]{3,2,1,0:T(8,128)(2,1)S(1)}, bf16[4,5,32,128]{3,2,1,0:T(8,128)(2,1)S(1)}, u32[]{:S(2)}, u32[]{:S(2)}) collective-permute-start(bf16[4,5,32,128]{3,2,1,0:T(8,128)(2,1)S(1)} %pad_maximum_fusion.6), channel_id=1, source_target_pairs={{0,3},{1,2},{2,1},{3,0},{4,7},{5,6},{6,5},{7,4},{8,11},{9,10},{10,... | collective-permute-start | bytes 491528 | tf_op jit(solution)/shard_map/ppermute | solution.py:89
  60.0 0.1 collective-permute-start.17
  60.1 0.3 collective-permute-start.18
  60.5 5.3 %collective-permute-done.16.refs_7_ = bf16[4,5,32,128]{3,2,1,0:T(8,128)(2,1)S(1)} collective-permute-done((bf16[4,5,32,128]{3,2,1,0:T(8,128)(2,1)S(1)}, bf16[4,5,32,128]{3,2,1,0:T(8,128)(2,1)S(1)}, u32[]{:S(2)}, u32[]{:S(2)}) %collective-permute-start.16) | collective-permute-done | bytes 163872 | tf_op jit(solution)/shard_map/ppermute | solution.py:89
  65.8 2.6 %collective-permute-done.17.refs_8_ = bf16[4,5,32,128]{3,2,1,0:T(8,128)(2,1)S(1)} collective-permute-done((bf16[4,5,32,128]{3,2,1,0:T(8,128)(2,1)S(1)}, bf16[4,5,32,128]{3,2,1,0:T(8,128)(2,1)S(1)}, u32[]{:S(2)}, u32[]{:S(2)}) %collective-permute-start.17) | collective-permute-done | bytes 163872 | tf_op jit(solution)/shard_map/ppermute | solution.py:89
  68.4 0.0 collective-permute-done.18.refs_9_
  68.4 0.0 copy-done.1
  68.4 0.0 copy-done.7
  68.4 2.0 %shard_map.74 = bf16[256,256]{1,0:T(8,128)(2,1)S(1)} custom-call(s32[1]{0:T(128)} %bitcast.1.refs_0_, s32[16,32]{1,0:T(8,128)S(1)} %bitcast.36, bf16[32,256,128]{2,1,0:T(8,128)(2,1)S(1)} %bitcast.26, bf16[4,5,32,128]{3,2,1,0:T(8,128)(2,1)S(1)} %get-tuple-element.34.refs_3_, bf16[4,5,32,128]{3,2,1,0:T(8,128)(2,1)S(1)} %collective-permute-done.13.refs_4_, ...), custom_call_target="tpu_custom_call" | custom-call | flops 536870912 | bytes 3244032 | tf_op jit(solution)/shard_map/pallas_call | solution.py:286
  70.5 6.9 %collective-permute-start.19 = (bf16[256,256]{1,0:T(8,128)(2,1)S(1)}, bf16[256,256]{1,0:T(8,128)(2,1)S(1)}, u32[]{:S(2)}, u32[]{:S(2)}) collective-permute-start(bf16[256,256]{1,0:T(8,128)(2,1)S(1)} %shard_map.74), channel_id=1, source_target_pairs={{0,16},{16,0},{1,17},{17,1},{2,18},{18,2},{3,19},{19,3},{4,20},{20... | collective-permute-start | bytes 393224 | tf_op jit(solution)/shard_map/ppermute | solution.py:321
  77.3 0.1 shard_map.72
  77.4 0.9 %reshape.38 = bf16[1,512,2,256]{3,2,1,0:T(2,128)(2,1)} reshape(bf16[512,512]{1,0:T(8,128)(2,1)S(1)} %shard_map.72) | data formatting | bytes 1048576 | tf_op jit(solution)/shard_map/reshape | solution.py:323
  78.4 0.0 all-to-all-done.refs_3_
  78.4 2.1 %shard_map.73.first_ref = bf16[256,256]{1,0:T(8,128)(2,1)S(1)} custom-call(s32[1]{0:T(128)} %bitcast.1.refs_0_, s32[16,32]{1,0:T(8,128)S(1)} %bitcast.37, bf16[32,256,128]{2,1,0:T(8,128)(2,1)S(1)} %bitcast.27, bf16[16,5,32,128]{3,2,1,0:T(8,128)(2,1)S(1)} %all-to-all-done.refs_3_), custom_call_target="tpu_custom_call" | custom-call | flops 536870912 | bytes 2752512 | tf_op jit(solution)/shard_map/pallas_call | solution.py:286
  80.4 0.0 collective-permute-done.19.second_ref
  80.5 0.8 reshape.39
  (32 shorter events, 0.4 us)
Async XLA Ops:
  1.8 1.7 %collective-permute-start = (bf16[256,2,128]{2,1,0:T(2,128)(2,1)S(1)}, bf16[256,2,128]{2,1,0:T(2,128)(2,1)S(1)}, u32[]{:S(2)}, u32[]{:S(2)}) collective-permute-start(bf16[256,2,128]{2,1,0:T(2,128)(2,1)S(1)} %get-tuple-element.48), channel_id=1, source_target_pairs={{0,16},{16,0},{1,17},{17,1},{2,18},{18,2},{3,19},{19,3},{4,20},{20... | collective-permute-start | bytes 393224 | tf_op jit(solution)/shard_map/ppermute | solution.py:307
  3.5 1.6 %copy-start = (bf16[1,32,1,256,128]{4,3,2,1,0:T(8,128)(2,1)S(1)}, bf16[1,32,1,256,128]{4,3,2,1,0:T(8,128)(2,1)}, u32[]{:S(2)}) copy-start(bf16[1,32,1,256,128]{4,3,2,1,0:T(8,128)(2,1)} %param.6) | copy-start | bytes 6291460
  5.1 0.7 copy-start.6
  5.8 0.7 copy-start.8
  8.1 6.9 %collective-permute-start.7 = (bf16[4,5,32,128]{3,2,1,0:T(8,128)(2,1)S(1)}, bf16[4,5,32,128]{3,2,1,0:T(8,128)(2,1)S(1)}, u32[]{:S(2)}, u32[]{:S(2)}) collective-permute-start(bf16[4,5,32,128]{3,2,1,0:T(8,128)(2,1)S(1)} %get-tuple-element.26), channel_id=1, source_target_pairs={{0,4},{1,5},{2,6},{3,7},{4,0},{5,1},{6,2},{7,3},{8,12},{9,13},{10,... | collective-permute-start | bytes 491528 | tf_op jit(solution)/shard_map/ppermute | solution.py:75
  8.2 10.0 %collective-permute-start.8 = (bf16[4,5,32,128]{3,2,1,0:T(8,128)(2,1)S(1)}, bf16[4,5,32,128]{3,2,1,0:T(8,128)(2,1)S(1)}, u32[]{:S(2)}, u32[]{:S(2)}) collective-permute-start(bf16[4,5,32,128]{3,2,1,0:T(8,128)(2,1)S(1)} %get-tuple-element.27), channel_id=1, source_target_pairs={{0,8},{1,9},{2,10},{3,11},{4,12},{5,13},{6,14},{7,15},{8,0},{9,1},... | collective-permute-start | bytes 491528 | tf_op jit(solution)/shard_map/ppermute | solution.py:75
  10.7 14.4 %collective-permute-start.9 = (bf16[4,5,32,128]{3,2,1,0:T(8,128)(2,1)S(1)}, bf16[4,5,32,128]{3,2,1,0:T(8,128)(2,1)S(1)}, u32[]{:S(2)}, u32[]{:S(2)}) collective-permute-start(bf16[4,5,32,128]{3,2,1,0:T(8,128)(2,1)S(1)} %get-tuple-element.28), channel_id=1, source_target_pairs={{0,12},{1,13},{2,14},{3,15},{4,8},{5,9},{6,10},{7,11},{8,4},{9,5},... | collective-permute-start | bytes 491528 | tf_op jit(solution)/shard_map/ppermute | solution.py:75
  12.4 22.7 %copy-start.9 = (bf16[1,2,16,256,128]{4,3,2,1,0:T(8,128)(2,1)S(1)}, bf16[1,2,16,256,128]{4,3,2,1,0:T(8,128)(2,1)}, u32[]{:S(2)}) copy-start(bf16[1,2,16,256,128]{4,3,2,1,0:T(8,128)(2,1)} %param.7) | copy-start | bytes 6291460
  12.5 15.3 %collective-permute-start.1 = (bf16[4,5,32,128]{3,2,1,0:T(8,128)(2,1)S(1)}, bf16[4,5,32,128]{3,2,1,0:T(8,128)(2,1)S(1)}, u32[]{:S(2)}, u32[]{:S(2)}) collective-permute-start(bf16[4,5,32,128]{3,2,1,0:T(8,128)(2,1)S(1)} %get-tuple-element.31), channel_id=1, source_target_pairs={{0,1},{1,0},{2,3},{3,2},{4,5},{5,4},{6,7},{7,6},{8,9},{9,8},{10,11... | collective-permute-start | bytes 491528 | tf_op jit(solution)/shard_map/ppermute | solution.py:75
  13.7 14.3 %collective-permute-start.2 = (bf16[4,5,32,128]{3,2,1,0:T(8,128)(2,1)S(1)}, bf16[4,5,32,128]{3,2,1,0:T(8,128)(2,1)S(1)}, u32[]{:S(2)}, u32[]{:S(2)}) collective-permute-start(bf16[4,5,32,128]{3,2,1,0:T(8,128)(2,1)S(1)} %get-tuple-element.32), channel_id=1, source_target_pairs={{0,2},{1,3},{2,0},{3,1},{4,6},{5,7},{6,4},{7,5},{8,10},{9,11},{10,... | collective-permute-start | bytes 491528 | tf_op jit(solution)/shard_map/ppermute | solution.py:75
  15.0 13.1 %collective-permute-start.3 = (bf16[4,5,32,128]{3,2,1,0:T(8,128)(2,1)S(1)}, bf16[4,5,32,128]{3,2,1,0:T(8,128)(2,1)S(1)}, u32[]{:S(2)}, u32[]{:S(2)}) collective-permute-start(bf16[4,5,32,128]{3,2,1,0:T(8,128)(2,1)S(1)} %get-tuple-element.33), channel_id=1, source_target_pairs={{0,3},{1,2},{2,1},{3,0},{4,7},{5,6},{6,5},{7,4},{8,11},{9,10},{10,... | collective-permute-start | bytes 491528 | tf_op jit(solution)/shard_map/ppermute | solution.py:75
  25.2 5.2 %collective-permute-start.10 = (bf16[4,5,32,128]{3,2,1,0:T(8,128)(2,1)S(1)}, bf16[4,5,32,128]{3,2,1,0:T(8,128)(2,1)S(1)}, u32[]{:S(2)}, u32[]{:S(2)}) collective-permute-start(bf16[4,5,32,128]{3,2,1,0:T(8,128)(2,1)S(1)} %pad_maximum_fusion.3), channel_id=1, source_target_pairs={{0,3},{1,2},{2,1},{3,0},{4,7},{5,6},{6,5},{7,4},{8,11},{9,10},{10,... | collective-permute-start | bytes 491528 | tf_op jit(solution)/shard_map/ppermute | solution.py:89
  27.4 7.7 %collective-permute-start.11 = (bf16[4,5,32,128]{3,2,1,0:T(8,128)(2,1)S(1)}, bf16[4,5,32,128]{3,2,1,0:T(8,128)(2,1)S(1)}, u32[]{:S(2)}, u32[]{:S(2)}) collective-permute-start(bf16[4,5,32,128]{3,2,1,0:T(8,128)(2,1)S(1)} %pad_maximum_fusion.4), channel_id=1, source_target_pairs={{0,2},{1,3},{2,0},{3,1},{4,6},{5,7},{6,4},{7,5},{8,10},{9,11},{10,... | collective-permute-start | bytes 491528 | tf_op jit(solution)/shard_map/ppermute | solution.py:89
  27.7 7.4 %collective-permute-start.12 = (bf16[4,5,32,128]{3,2,1,0:T(8,128)(2,1)S(1)}, bf16[4,5,32,128]{3,2,1,0:T(8,128)(2,1)S(1)}, u32[]{:S(2)}, u32[]{:S(2)}) collective-permute-start(bf16[4,5,32,128]{3,2,1,0:T(8,128)(2,1)S(1)} %pad_maximum_fusion.5), channel_id=1, source_target_pairs={{0,1},{1,0},{2,3},{3,2},{4,5},{5,4},{6,7},{7,6},{8,9},{9,8},{10,11... | collective-permute-start | bytes 491528 | tf_op jit(solution)/shard_map/ppermute | solution.py:89
  28.2 13.5 %collective-permute-start.4 = (bf16[4,5,32,128]{3,2,1,0:T(8,128)(2,1)S(1)}, bf16[4,5,32,128]{3,2,1,0:T(8,128)(2,1)S(1)}, u32[]{:S(2)}, u32[]{:S(2)}) collective-permute-start(bf16[4,5,32,128]{3,2,1,0:T(8,128)(2,1)S(1)} %pad_maximum_fusion), channel_id=1, source_target_pairs={{0,12},{1,13},{2,14},{3,15},{4,8},{5,9},{6,10},{7,11},{8,4},{9,5},... | collective-permute-start | bytes 491528 | tf_op jit(solution)/shard_map/ppermute | solution.py:89
  29.5 12.3 %collective-permute-start.5 = (bf16[4,5,32,128]{3,2,1,0:T(8,128)(2,1)S(1)}, bf16[4,5,32,128]{3,2,1,0:T(8,128)(2,1)S(1)}, u32[]{:S(2)}, u32[]{:S(2)}) collective-permute-start(bf16[4,5,32,128]{3,2,1,0:T(8,128)(2,1)S(1)} %pad_maximum_fusion.1), channel_id=1, source_target_pairs={{0,8},{1,9},{2,10},{3,11},{4,12},{5,13},{6,14},{7,15},{8,0},{9,1},... | collective-permute-start | bytes 491528 | tf_op jit(solution)/shard_map/ppermute | solution.py:89
  30.3 11.6 %collective-permute-start.6 = (bf16[4,5,32,128]{3,2,1,0:T(8,128)(2,1)S(1)}, bf16[4,5,32,128]{3,2,1,0:T(8,128)(2,1)S(1)}, u32[]{:S(2)}, u32[]{:S(2)}) collective-permute-start(bf16[4,5,32,128]{3,2,1,0:T(8,128)(2,1)S(1)} %pad_maximum_fusion.2), channel_id=1, source_target_pairs={{0,4},{1,5},{2,6},{3,7},{4,0},{5,1},{6,2},{7,3},{8,12},{9,13},{10,... | collective-permute-start | bytes 491528 | tf_op jit(solution)/shard_map/ppermute | solution.py:89
  38.5 0.7 copy-start.2
  39.2 14.4 %collective-permute-start.13 = (bf16[4,5,32,128]{3,2,1,0:T(8,128)(2,1)}, bf16[4,5,32,128]{3,2,1,0:T(8,128)(2,1)S(1)}, u32[]{:S(2)}, u32[]{:S(2)}) collective-permute-start(bf16[4,5,32,128]{3,2,1,0:T(8,128)(2,1)} %get-tuple-element.35), channel_id=1, source_target_pairs={{0,4},{1,5},{2,6},{3,7},{4,0},{5,1},{6,2},{7,3},{8,12},{9,13},{10,... | collective-permute-start | bytes 491528 | tf_op jit(solution)/shard_map/ppermute | solution.py:75
  39.2 14.4 %collective-permute-start.14 = (bf16[4,5,32,128]{3,2,1,0:T(8,128)(2,1)}, bf16[4,5,32,128]{3,2,1,0:T(8,128)(2,1)S(1)}, u32[]{:S(2)}, u32[]{:S(2)}) collective-permute-start(bf16[4,5,32,128]{3,2,1,0:T(8,128)(2,1)} %get-tuple-element.36), channel_id=1, source_target_pairs={{0,8},{1,9},{2,10},{3,11},{4,12},{5,13},{6,14},{7,15},{8,0},{9,1},... | collective-permute-start | bytes 491528 | tf_op jit(solution)/shard_map/ppermute | solution.py:75
  41.7 13.6 %collective-permute-start.15 = (bf16[4,5,32,128]{3,2,1,0:T(8,128)(2,1)}, bf16[4,5,32,128]{3,2,1,0:T(8,128)(2,1)S(1)}, u32[]{:S(2)}, u32[]{:S(2)}) collective-permute-start(bf16[4,5,32,128]{3,2,1,0:T(8,128)(2,1)} %get-tuple-element.37), channel_id=1, source_target_pairs={{0,12},{1,13},{2,14},{3,15},{4,8},{5,9},{6,10},{7,11},{8,4},{9,5},... | collective-permute-start | bytes 491528 | tf_op jit(solution)/shard_map/ppermute | solution.py:75
  46.0 0.7 copy-start.4
  46.7 21.7 %copy-start.1 = (bf16[1,32,1,256,128]{4,3,2,1,0:T(8,128)(2,1)S(1)}, bf16[1,32,1,256,128]{4,3,2,1,0:T(8,128)(2,1)}, u32[]{:S(2)}) copy-start(bf16[1,32,1,256,128]{4,3,2,1,0:T(8,128)(2,1)} %param.6) | copy-start | bytes 6291460
  46.8 21.7 %copy-start.7 = (s32[1,32,16]{1,2,0:T(8,128)S(1)}, s32[1,32,16]{1,2,0:T(8,128)}, u32[]{:S(2)}) copy-start(s32[1,32,16]{1,2,0:T(8,128)} %param.9) | copy-start | bytes 6148
  46.8 31.6 %all-to-all-start = ((bf16[16,5,32,128]{3,2,1,0:T(8,128)(2,1)}), bf16[16,5,32,128]{3,2,1,0:T(8,128)(2,1)S(1)}, u32[]{:S(2)}, u32[]{:S(2)}) async-start(bf16[16,5,32,128]{3,2,1,0:T(8,128)(2,1)} %get-tuple-element.47), calls=%async_computation | async-start | bytes 1310720 | tf_op jit(solution)/shard_map/all_to_all | solution.py:71
  55.4 22.0 %copy-start.3 = (bf16[2,256,256]{2,1,0:T(8,128)(2,1)S(1)}, bf16[2,256,256]{2,1,0:T(8,128)(2,1)}, u32[]{:S(2)}) copy-start(bf16[2,256,256]{2,1,0:T(8,128)(2,1)} %copy-done.2) | copy-start | bytes 786436
  55.4 22.0 %copy-start.5 = (bf16[2,256,256]{2,1,0:T(8,128)(2,1)S(1)}, bf16[2,256,256]{2,1,0:T(8,128)(2,1)}, u32[]{:S(2)}) copy-start(bf16[2,256,256]{2,1,0:T(8,128)(2,1)} %copy-done.4) | copy-start | bytes 786436
  55.4 10.4 %collective-permute-start.16 = (bf16[4,5,32,128]{3,2,1,0:T(8,128)(2,1)S(1)}, bf16[4,5,32,128]{3,2,1,0:T(8,128)(2,1)S(1)}, u32[]{:S(2)}, u32[]{:S(2)}) collective-permute-start(bf16[4,5,32,128]{3,2,1,0:T(8,128)(2,1)S(1)} %pad_maximum_fusion.6), channel_id=1, source_target_pairs={{0,3},{1,2},{2,1},{3,0},{4,7},{5,6},{6,5},{7,4},{8,11},{9,10},{10,... | collective-permute-start | bytes 491528 | tf_op jit(solution)/shard_map/ppermute | solution.py:89
  60.0 8.4 %collective-permute-start.17 = (bf16[4,5,32,128]{3,2,1,0:T(8,128)(2,1)S(1)}, bf16[4,5,32,128]{3,2,1,0:T(8,128)(2,1)S(1)}, u32[]{:S(2)}, u32[]{:S(2)}) collective-permute-start(bf16[4,5,32,128]{3,2,1,0:T(8,128)(2,1)S(1)} %pad_maximum_fusion.7), channel_id=1, source_target_pairs={{0,2},{1,3},{2,0},{3,1},{4,6},{5,7},{6,4},{7,5},{8,10},{9,11},{10,... | collective-permute-start | bytes 491528 | tf_op jit(solution)/shard_map/ppermute | solution.py:89
  60.1 8.3 %collective-permute-start.18 = (bf16[4,5,32,128]{3,2,1,0:T(8,128)(2,1)S(1)}, bf16[4,5,32,128]{3,2,1,0:T(8,128)(2,1)S(1)}, u32[]{:S(2)}, u32[]{:S(2)}) collective-permute-start(bf16[4,5,32,128]{3,2,1,0:T(8,128)(2,1)S(1)} %pad_maximum_fusion.8), channel_id=1, source_target_pairs={{0,1},{1,0},{2,3},{3,2},{4,5},{5,4},{6,7},{7,6},{8,9},{9,8},{10,11... | collective-permute-start | bytes 491528 | tf_op jit(solution)/shard_map/ppermute | solution.py:89
  70.5 10.0 %collective-permute-start.19 = (bf16[256,256]{1,0:T(8,128)(2,1)S(1)}, bf16[256,256]{1,0:T(8,128)(2,1)S(1)}, u32[]{:S(2)}, u32[]{:S(2)}) collective-permute-start(bf16[256,256]{1,0:T(8,128)(2,1)S(1)} %shard_map.74), channel_id=1, source_target_pairs={{0,16},{16,0},{1,17},{17,1},{2,18},{18,2},{3,19},{19,3},{4,20},{20... | collective-permute-start | bytes 393224 | tf_op jit(solution)/shard_map/ppermute | solution.py:321

commit v5 on v4

--- a/solution.py
+++ b/solution.py
@@ -312,6 +312,8 @@
     coded_a = second_hop(first_a, sends_a, way["1a"], tiles)
     coded_b = second_hop(first_b, sends_b, way["1b"], tiles)
     y_a, back_a = middle(coded_a, way["1a"], way["2a"])
+    farthest_b = coded_b[way["1b"][0]]
+    back_a = [*back_a[:2], *after(back_a[2:], [farthest_b])]
     first_a, sends_a = exchange(back_a, way["2a"], tiles)
     coded_b = after(coded_b, back_a)
     y_b, back_b = middle(coded_b, way["1b"], way["2b"])

time: 81.6 us -> 80.2 us (0.983)
  waiting for transfers between devices: 24.3 us -> 21.3 us
  starting transfers between devices: 33.5 us -> 35.1 us
    ppermute x18, waiting for transfers between devices: 23.3 us -> 20.3 us  [swap(): return lax.ppermute(block, 'tile', [(i, i ^ offset) for i in range(tiles)])]
    ppermute x18, starting transfers between devices: 19 us -> 20.7 us  [swap(): return lax.ppermute(block, 'tile', [(i, i ^ offset) for i in range(tiles)])]
    all_to_all x1, starting transfers between devices: 6.88 us -> 5.89 us  [exchange(): lax.all_to_all(blocks[0], 'tile', split_axis=0, concat_axis=0, tiled=True)]
    ppermute x1, starting transfers between devices: 6.87 us -> 7.82 us  [per_device(): z_a = lax.ppermute(adjoint(back_a, way['2a']), 'freq', swap)]
  transfers between devices with their start and end apart: 21 -> 21, of which waited for: 8 -> 7; matrix products, arithmetic and copies ran while one was open for 2% -> 2% of each run, Pallas kernels for 16% -> 17%
where the time goes in v5:
time: 80.2 us; the launch traced here: 79.8 us
  starting transfers between devices  35.1 us (44%)
  waiting for transfers between devices  21.3 us (27%)
  Pallas kernels  14.9 us (19%)
  local copies, waits for them, and re-layouts  7.4 us (9%)
  between operations  0.92 us (1%)
    ppermute x18, starting transfers between devices, swap(): return lax.ppermute(block, 'tile', [(i, i ^ offset) for i in range(tiles)])  20.7 us
    ppermute x18, waiting for transfers between devices, swap(): return lax.ppermute(block, 'tile', [(i, i ^ offset) for i in range(tiles)])  20.3 us
    ppermute x1, starting transfers between devices, per_device(): z_a = lax.ppermute(adjoint(back_a, way['2a']), 'freq', swap)  7.82 us
    pallas_call x2, Pallas kernels, middle(): pl.pallas_call(lambda *refs: middle_kernel(route_in, route_out, tiles, *r...  7.55 us
    all_to_all x1, starting transfers between devices, exchange(): lax.all_to_all(blocks[0], 'tile', split_axis=0, concat_axis=0, tiled=True)  5.89 us
    unnamed x22, local copies, waits for them, and re-layouts  4.45 us
    pallas_call x2, Pallas kernels, adjoint(): pl.pallas_call(lambda *refs: adjoint_kernel(route, tiles, *refs), out_sha...  4.1 us
    pallas_call x2, Pallas kernels, code(): pl.pallas_call(lambda *refs: coded_kernel(route, *refs), out_shape=shapes...  3.14 us
  transfers between devices with their start and end apart: 21, of which 7 were waited for; matrix products, arithmetic and copies ran while one was open for 2% of the time, Pallas kernels for 17%

profile of v5, /device:TPU:9, one launch (start us, length us, event | category | flops | bytes accessed | tf_op | source)
XLA Modules:
  0.0 79.8 jit_solution(3027197659652248018)
XLA Ops:
  0.6 1.2 %dynamic-slice_bitcast_fusion = (bf16[256,2,128]{2,1,0:T(2,128)(2,1)S(1)}, bf16[256,2,128]{2,1,0:T(2,128)(2,1)S(1)}) fusion(bf16[2,256,2,128]{3,2,1,0:T(2,128)(2,1)} %param.5, s32[]{:T(128)S(6)} %select_n.8, s32[]{:T(128)S(6)} %select_n.7), kind=kLoop, calls=%fused_computation.11 | loop fusion | bytes 524296 | tf_op jit(solution)/shard_map/jit(dynamic_index_in_dim)/squeeze | solution.py:305
  1.8 0.7 collective-permute-start
  2.5 1.0 %collective-permute-done = bf16[256,2,128]{2,1,0:T(2,128)(2,1)S(1)} collective-permute-done((bf16[256,2,128]{2,1,0:T(2,128)(2,1)S(1)}, bf16[256,2,128]{2,1,0:T(2,128)(2,1)S(1)}, u32[]{:S(2)}, u32[]{:S(2)}) %collective-permute-start) | collective-permute-done | bytes 131104 | tf_op jit(solution)/shard_map/ppermute | solution.py:307
  3.5 0.0 copy-start
  3.6 1.6 %copy-done = bf16[1,32,1,256,128]{4,3,2,1,0:T(8,128)(2,1)S(1)} copy-done((bf16[1,32,1,256,128]{4,3,2,1,0:T(8,128)(2,1)S(1)}, bf16[1,32,1,256,128]{4,3,2,1,0:T(8,128)(2,1)}, u32[]{:S(2)}) %copy-start) | copy-done | bytes 2097176
  5.1 0.7 copy-done.6
  5.8 0.7 copy-done.8
  6.5 1.6 %shard_map.68 = (bf16[4,5,32,128]{3,2,1,0:T(8,128)(2,1)S(1)}, bf16[4,5,32,128]{3,2,1,0:T(8,128)(2,1)S(1)}, bf16[4,5,32,128]{3,2,1,0:T(8,128)(2,1)S(1)}, bf16[4,5,32,128]{3,2,1,0:T(8,128)(2,1)S(1)}) custom-call(s32[1]{0:T(128)} %bitcast.1.refs_0_, s32[16,32]{1,0:T(8,128)S(1)} %bitcast.32, f32[16,32]{1,0:T(8,128)S(1)} %bitcast.38, ...), custom_call_target="tpu_custom_call" | custom-call | flops 536870912 | bytes 2228224 | tf_op jit(solution)/shard_map/pallas_call | solution.py:263
  8.1 0.1 collective-permute-start.7
  8.2 2.5 %collective-permute-start.8 = (bf16[4,5,32,128]{3,2,1,0:T(8,128)(2,1)S(1)}, bf16[4,5,32,128]{3,2,1,0:T(8,128)(2,1)S(1)}, u32[]{:S(2)}, u32[]{:S(2)}) collective-permute-start(bf16[4,5,32,128]{3,2,1,0:T(8,128)(2,1)S(1)} %get-tuple-element.29), channel_id=1, source_target_pairs={{0,8},{1,9},{2,10},{3,11},{4,12},{5,13},{6,14},{7,15},{8,0},{9,1},... | collective-permute-start | bytes 491528 | tf_op jit(solution)/shard_map/ppermute | solution.py:75
  10.7 0.2 collective-permute-start.9
  10.9 1.6 %shard_map.69 = (bf16[4,5,32,128]{3,2,1,0:T(8,128)(2,1)S(1)}, bf16[4,5,32,128]{3,2,1,0:T(8,128)(2,1)S(1)}, bf16[4,5,32,128]{3,2,1,0:T(8,128)(2,1)S(1)}, bf16[4,5,32,128]{3,2,1,0:T(8,128)(2,1)S(1)}) custom-call(s32[1]{0:T(128)} %bitcast.1.refs_0_, s32[16,32]{1,0:T(8,128)S(1)} %bitcast.33, f32[16,32]{1,0:T(8,128)S(1)} %bitcast.39, ...), custom_call_target="tpu_custom_call" | custom-call | flops 536870912 | bytes 2228224 | tf_op jit(solution)/shard_map/pallas_call | solution.py:263
  12.4 0.0 copy-start.9
  12.5 1.3 %collective-permute-start.1 = (bf16[4,5,32,128]{3,2,1,0:T(8,128)(2,1)S(1)}, bf16[4,5,32,128]{3,2,1,0:T(8,128)(2,1)S(1)}, u32[]{:S(2)}, u32[]{:S(2)}) collective-permute-start(bf16[4,5,32,128]{3,2,1,0:T(8,128)(2,1)S(1)} %get-tuple-element.33), channel_id=1, source_target_pairs={{0,1},{1,0},{2,3},{3,2},{4,5},{5,4},{6,7},{7,6},{8,9},{9,8},{10,11... | collective-permute-start | bytes 491528 | tf_op jit(solution)/shard_map/ppermute | solution.py:75
  13.7 1.2 %collective-permute-start.3 = (bf16[4,5,32,128]{3,2,1,0:T(8,128)(2,1)S(1)}, bf16[4,5,32,128]{3,2,1,0:T(8,128)(2,1)S(1)}, u32[]{:S(2)}, u32[]{:S(2)}) collective-permute-start(bf16[4,5,32,128]{3,2,1,0:T(8,128)(2,1)S(1)} %get-tuple-element.35), channel_id=1, source_target_pairs={{0,3},{1,2},{2,1},{3,0},{4,7},{5,6},{6,5},{7,4},{8,11},{9,10},{10,... | collective-permute-start | bytes 491528 | tf_op jit(solution)/shard_map/ppermute | solution.py:75
  15.0 6.5 %collective-permute-done.3.refs_7_ = bf16[4,5,32,128]{3,2,1,0:T(8,128)(2,1)S(1)} collective-permute-done((bf16[4,5,32,128]{3,2,1,0:T(8,128)(2,1)S(1)}, bf16[4,5,32,128]{3,2,1,0:T(8,128)(2,1)S(1)}, u32[]{:S(2)}, u32[]{:S(2)}) %collective-permute-start.3) | collective-permute-done | bytes 163872 | tf_op jit(solution)/shard_map/ppermute | solution.py:75
  21.5 0.5 collective-permute-start.2
  22.0 3.9 %collective-permute-done.2.refs_6_ = bf16[4,5,32,128]{3,2,1,0:T(8,128)(2,1)S(1)} collective-permute-done((bf16[4,5,32,128]{3,2,1,0:T(8,128)(2,1)S(1)}, bf16[4,5,32,128]{3,2,1,0:T(8,128)(2,1)S(1)}, u32[]{:S(2)}, u32[]{:S(2)}) %collective-permute-start.2) | collective-permute-done | bytes 163872 | tf_op jit(solution)/shard_map/ppermute | solution.py:75
  26.0 0.0 collective-permute-done.1.refs_5_
  26.0 1.4 %collective-permute-start.4 = (bf16[4,5,32,128]{3,2,1,0:T(8,128)(2,1)S(1)}, bf16[4,5,32,128]{3,2,1,0:T(8,128)(2,1)S(1)}, u32[]{:S(2)}, u32[]{:S(2)}) collective-permute-start(bf16[4,5,32,128]{3,2,1,0:T(8,128)(2,1)S(1)} %pad_maximum_fusion), channel_id=1, source_target_pairs={{0,12},{1,13},{2,14},{3,15},{4,8},{5,9},{6,10},{7,11},{8,4},{9,5},... | collective-permute-start | bytes 491528 | tf_op jit(solution)/shard_map/ppermute | solution.py:89
  27.4 0.0 collective-permute-done.9.refs_7_
  27.4 0.0 collective-permute-done.8.refs_6_
  27.4 0.0 collective-permute-done.7.refs_5_
  27.5 1.2 %collective-permute-start.10 = (bf16[4,5,32,128]{3,2,1,0:T(8,128)(2,1)S(1)}, bf16[4,5,32,128]{3,2,1,0:T(8,128)(2,1)S(1)}, u32[]{:S(2)}, u32[]{:S(2)}) collective-permute-start(bf16[4,5,32,128]{3,2,1,0:T(8,128)(2,1)S(1)} %pad_maximum_fusion.3), channel_id=1, source_target_pairs={{0,3},{1,2},{2,1},{3,0},{4,7},{5,6},{6,5},{7,4},{8,11},{9,10},{10,... | collective-permute-start | bytes 491528 | tf_op jit(solution)/shard_map/ppermute | solution.py:89
  28.7 1.3 %collective-permute-start.11 = (bf16[4,5,32,128]{3,2,1,0:T(8,128)(2,1)S(1)}, bf16[4,5,32,128]{3,2,1,0:T(8,128)(2,1)S(1)}, u32[]{:S(2)}, u32[]{:S(2)}) collective-permute-start(bf16[4,5,32,128]{3,2,1,0:T(8,128)(2,1)S(1)} %pad_maximum_fusion.4), channel_id=1, source_target_pairs={{0,2},{1,3},{2,0},{3,1},{4,6},{5,7},{6,4},{7,5},{8,10},{9,11},{10,... | collective-permute-start | bytes 491528 | tf_op jit(solution)/shard_map/ppermute | solution.py:89
  30.1 0.3 collective-permute-start.12
  30.4 1.8 %collective-permute-start.5 = (bf16[4,5,32,128]{3,2,1,0:T(8,128)(2,1)S(1)}, bf16[4,5,32,128]{3,2,1,0:T(8,128)(2,1)S(1)}, u32[]{:S(2)}, u32[]{:S(2)}) collective-permute-start(bf16[4,5,32,128]{3,2,1,0:T(8,128)(2,1)S(1)} %pad_maximum_fusion.1), channel_id=1, source_target_pairs={{0,8},{1,9},{2,10},{3,11},{4,12},{5,13},{6,14},{7,15},{8,0},{9,1},... | collective-permute-start | bytes 491528 | tf_op jit(solution)/shard_map/ppermute | solution.py:89
  32.2 0.5 collective-permute-done.10.refs_8_
  32.7 3.0 %collective-permute-start.6 = (bf16[4,5,32,128]{3,2,1,0:T(8,128)(2,1)S(1)}, bf16[4,5,32,128]{3,2,1,0:T(8,128)(2,1)S(1)}, u32[]{:S(2)}, u32[]{:S(2)}) collective-permute-start(bf16[4,5,32,128]{3,2,1,0:T(8,128)(2,1)S(1)} %pad_maximum_fusion.2), channel_id=1, source_target_pairs={{0,4},{1,5},{2,6},{3,7},{4,0},{5,1},{6,2},{7,3},{8,12},{9,13},{10,... | collective-permute-start | bytes 491528 | tf_op jit(solution)/shard_map/ppermute | solution.py:89
  35.7 0.0 collective-permute-done.11.refs_9_
  35.7 0.0 collective-permute-done.12.refs_10_
  35.7 0.0 copy-done.9
  35.7 3.4 %shard_map.70 = (bf16[2,256,256]{2,1,0:T(8,128)(2,1)S(1)}, bf16[4,5,32,128]{3,2,1,0:T(8,128)(2,1)S(1)}, bf16[4,5,32,128]{3,2,1,0:T(8,128)(2,1)}, bf16[4,5,32,128]{3,2,1,0:T(8,128)(2,1)}, bf16[4,5,32,128]{3,2,1,0:T(8,128)(2,1)}) custom-call(s32[1]{0:T(128)} %bitcast.1.refs_0_, s32[16,32]{1,0:T(8,128)S(1)} %bitcast.34, f32[16,32]{1,0:T(8,128)S(1)} %bitcast.40, ...), custom_call_target="tpu_custom_call" | custom-call | flops 10737418240 | bytes 32440320 | tf_op jit(solution)/shard_map/pallas_call | solution.py:274
  39.1 0.7 copy-done.2
  39.8 0.0 collective-permute-done.4.refs_8_
  39.8 2.0 %collective-permute-start.13 = (bf16[4,5,32,128]{3,2,1,0:T(8,128)(2,1)}, bf16[4,5,32,128]{3,2,1,0:T(8,128)(2,1)S(1)}, u32[]{:S(2)}, u32[]{:S(2)}) collective-permute-start(bf16[4,5,32,128]{3,2,1,0:T(8,128)(2,1)} %get-tuple-element.37), channel_id=1, source_target_pairs={{0,4},{1,5},{2,6},{3,7},{4,0},{5,1},{6,2},{7,3},{8,12},{9,13},{10,... | collective-permute-start | bytes 491528 | tf_op jit(solution)/shard_map/ppermute | solution.py:75
  41.8 0.0 collective-permute-start.14
  41.8 1.2 %collective-permute-start.15 = (bf16[4,5,32,128]{3,2,1,0:T(8,128)(2,1)}, bf16[4,5,32,128]{3,2,1,0:T(8,128)(2,1)S(1)}, u32[]{:S(2)}, u32[]{:S(2)}) collective-permute-start(bf16[4,5,32,128]{3,2,1,0:T(8,128)(2,1)} %get-tuple-element.41), channel_id=1, source_target_pairs={{0,12},{1,13},{2,14},{3,15},{4,8},{5,9},{6,10},{7,11},{8,4},{9,5},... | collective-permute-start | bytes 491528 | tf_op jit(solution)/shard_map/ppermute | solution.py:75
  43.0 0.0 collective-permute-done.5.refs_9_
  43.0 0.0 collective-permute-done.6.refs_10_
  43.0 4.2 %shard_map.71 = (bf16[2,256,256]{2,1,0:T(8,128)(2,1)S(1)}, bf16[16,5,32,128]{3,2,1,0:T(8,128)(2,1)}) custom-call(s32[1]{0:T(128)} %bitcast.1.refs_0_, s32[16,32]{1,0:T(8,128)S(1)} %bitcast.35, f32[16,32]{1,0:T(8,128)S(1)} %bitcast.41, bf16[2,16,256,128]{3,2,1,0:T(8,128)(2,1)S(1)} %bitcast.43, bf16[4,5,32,128]{3,2,1,0:T(8,128)(2,1)S(1)} %get-tuple-element.42.refs_4_, ...), custom_call_target="tpu_custom_call" | custom-call | flops 10737418240 | bytes 32440320 | tf_op jit(solution)/shard_map/pallas_call | solution.py:274
  47.2 0.7 copy-done.4
  47.9 5.9 %all-to-all-start = ((bf16[16,5,32,128]{3,2,1,0:T(8,128)(2,1)}), bf16[16,5,32,128]{3,2,1,0:T(8,128)(2,1)S(1)}, u32[]{:S(2)}, u32[]{:S(2)}) async-start(bf16[16,5,32,128]{3,2,1,0:T(8,128)(2,1)} %get-tuple-element.51), calls=%async_computation | async-start | bytes 1310720 | tf_op jit(solution)/shard_map/all_to_all | solution.py:71
  53.8 1.9 %collective-permute-done.15.refs_6_ = bf16[4,5,32,128]{3,2,1,0:T(8,128)(2,1)S(1)} collective-permute-done((bf16[4,5,32,128]{3,2,1,0:T(8,128)(2,1)}, bf16[4,5,32,128]{3,2,1,0:T(8,128)(2,1)S(1)}, u32[]{:S(2)}, u32[]{:S(2)}) %collective-permute-start.15) | collective-permute-done | bytes 163872 | tf_op jit(solution)/shard_map/ppermute | solution.py:75
  55.7 0.0 collective-permute-done.14.refs_5_
  55.7 0.0 collective-permute-done.13.refs_4_
  55.8 0.0 copy-start.3
  55.8 0.0 copy-start.5
  55.8 1.1 %collective-permute-start.16 = (bf16[4,5,32,128]{3,2,1,0:T(8,128)(2,1)S(1)}, bf16[4,5,32,128]{3,2,1,0:T(8,128)(2,1)S(1)}, u32[]{:S(2)}, u32[]{:S(2)}) collective-permute-start(bf16[4,5,32,128]{3,2,1,0:T(8,128)(2,1)S(1)} %pad_maximum_fusion.6), channel_id=1, source_target_pairs={{0,3},{1,2},{2,1},{3,0},{4,7},{5,6},{6,5},{7,4},{8,11},{9,10},{10,... | collective-permute-start | bytes 491528 | tf_op jit(solution)/shard_map/ppermute | solution.py:89
  56.9 1.1 %collective-permute-start.17 = (bf16[4,5,32,128]{3,2,1,0:T(8,128)(2,1)S(1)}, bf16[4,5,32,128]{3,2,1,0:T(8,128)(2,1)S(1)}, u32[]{:S(2)}, u32[]{:S(2)}) collective-permute-start(bf16[4,5,32,128]{3,2,1,0:T(8,128)(2,1)S(1)} %pad_maximum_fusion.7), channel_id=1, source_target_pairs={{0,2},{1,3},{2,0},{3,1},{4,6},{5,7},{6,4},{7,5},{8,10},{9,11},{10,... | collective-permute-start | bytes 491528 | tf_op jit(solution)/shard_map/ppermute | solution.py:89
  58.1 0.6 collective-permute-start.18
  58.7 3.6 %collective-permute-done.16.refs_7_ = bf16[4,5,32,128]{3,2,1,0:T(8,128)(2,1)S(1)} collective-permute-done((bf16[4,5,32,128]{3,2,1,0:T(8,128)(2,1)S(1)}, bf16[4,5,32,128]{3,2,1,0:T(8,128)(2,1)S(1)}, u32[]{:S(2)}, u32[]{:S(2)}) %collective-permute-start.16) | collective-permute-done | bytes 163872 | tf_op jit(solution)/shard_map/ppermute | solution.py:89
  62.3 3.7 %collective-permute-done.17.refs_8_ = bf16[4,5,32,128]{3,2,1,0:T(8,128)(2,1)S(1)} collective-permute-done((bf16[4,5,32,128]{3,2,1,0:T(8,128)(2,1)S(1)}, bf16[4,5,32,128]{3,2,1,0:T(8,128)(2,1)S(1)}, u32[]{:S(2)}, u32[]{:S(2)}) %collective-permute-start.17) | collective-permute-done | bytes 163872 | tf_op jit(solution)/shard_map/ppermute | solution.py:89
  66.1 0.0 collective-permute-done.18.refs_9_
  66.1 0.0 copy-done.1
  66.1 0.0 copy-done.7
  66.1 2.0 %shard_map.74 = bf16[256,256]{1,0:T(8,128)(2,1)S(1)} custom-call(s32[1]{0:T(128)} %bitcast.1.refs_0_, s32[16,32]{1,0:T(8,128)S(1)} %bitcast.36, bf16[32,256,128]{2,1,0:T(8,128)(2,1)S(1)} %bitcast.26, bf16[4,5,32,128]{3,2,1,0:T(8,128)(2,1)S(1)} %get-tuple-element.36.refs_3_, bf16[4,5,32,128]{3,2,1,0:T(8,128)(2,1)S(1)} %collective-permute-done.13.refs_4_, ...), custom_call_target="tpu_custom_call" | custom-call | flops 536870912 | bytes 3244032 | tf_op jit(solution)/shard_map/pallas_call | solution.py:286
  68.1 7.8 %collective-permute-start.19 = (bf16[256,256]{1,0:T(8,128)(2,1)S(1)}, bf16[256,256]{1,0:T(8,128)(2,1)S(1)}, u32[]{:S(2)}, u32[]{:S(2)}) collective-permute-start(bf16[256,256]{1,0:T(8,128)(2,1)S(1)} %shard_map.74), channel_id=1, source_target_pairs={{0,16},{16,0},{1,17},{17,1},{2,18},{18,2},{3,19},{19,3},{4,20},{20... | collective-permute-start | bytes 393224 | tf_op jit(solution)/shard_map/ppermute | solution.py:323
  75.9 0.1 shard_map.72
  76.0 0.9 %reshape.38 = bf16[1,512,2,256]{3,2,1,0:T(2,128)(2,1)} reshape(bf16[512,512]{1,0:T(8,128)(2,1)S(1)} %shard_map.72) | data formatting | bytes 1048576 | tf_op jit(solution)/shard_map/reshape | solution.py:325
  76.9 0.0 all-to-all-done.refs_3_
  76.9 2.1 %shard_map.73.first_ref = bf16[256,256]{1,0:T(8,128)(2,1)S(1)} custom-call(s32[1]{0:T(128)} %bitcast.1.refs_0_, s32[16,32]{1,0:T(8,128)S(1)} %bitcast.37, bf16[32,256,128]{2,1,0:T(8,128)(2,1)S(1)} %bitcast.27, bf16[16,5,32,128]{3,2,1,0:T(8,128)(2,1)S(1)} %all-to-all-done.refs_3_), custom_call_target="tpu_custom_call" | custom-call | flops 536870912 | bytes 2752512 | tf_op jit(solution)/shard_map/pallas_call | solution.py:286
  79.0 0.0 collective-permute-done.19.second_ref
  79.0 0.8 reshape.39
  (32 shorter events, 0.4 us)
Async XLA Ops:
  1.8 1.7 %collective-permute-start = (bf16[256,2,128]{2,1,0:T(2,128)(2,1)S(1)}, bf16[256,2,128]{2,1,0:T(2,128)(2,1)S(1)}, u32[]{:S(2)}, u32[]{:S(2)}) collective-permute-start(bf16[256,2,128]{2,1,0:T(2,128)(2,1)S(1)} %get-tuple-element.52), channel_id=1, source_target_pairs={{0,16},{16,0},{1,17},{17,1},{2,18},{18,2},{3,19},{19,3},{4,20},{20... | collective-permute-start | bytes 393224 | tf_op jit(solution)/shard_map/ppermute | solution.py:307
  3.5 1.6 %copy-start = (bf16[1,32,1,256,128]{4,3,2,1,0:T(8,128)(2,1)S(1)}, bf16[1,32,1,256,128]{4,3,2,1,0:T(8,128)(2,1)}, u32[]{:S(2)}) copy-start(bf16[1,32,1,256,128]{4,3,2,1,0:T(8,128)(2,1)} %param.6) | copy-start | bytes 6291460
  5.1 0.7 copy-start.6
  5.8 0.7 copy-start.8
  8.1 19.3 %collective-permute-start.7 = (bf16[4,5,32,128]{3,2,1,0:T(8,128)(2,1)S(1)}, bf16[4,5,32,128]{3,2,1,0:T(8,128)(2,1)S(1)}, u32[]{:S(2)}, u32[]{:S(2)}) collective-permute-start(bf16[4,5,32,128]{3,2,1,0:T(8,128)(2,1)S(1)} %get-tuple-element.28), channel_id=1, source_target_pairs={{0,4},{1,5},{2,6},{3,7},{4,0},{5,1},{6,2},{7,3},{8,12},{9,13},{10,... | collective-permute-start | bytes 491528 | tf_op jit(solution)/shard_map/ppermute | solution.py:75
  8.2 19.2 %collective-permute-start.8 = (bf16[4,5,32,128]{3,2,1,0:T(8,128)(2,1)S(1)}, bf16[4,5,32,128]{3,2,1,0:T(8,128)(2,1)S(1)}, u32[]{:S(2)}, u32[]{:S(2)}) collective-permute-start(bf16[4,5,32,128]{3,2,1,0:T(8,128)(2,1)S(1)} %get-tuple-element.29), channel_id=1, source_target_pairs={{0,8},{1,9},{2,10},{3,11},{4,12},{5,13},{6,14},{7,15},{8,0},{9,1},... | collective-permute-start | bytes 491528 | tf_op jit(solution)/shard_map/ppermute | solution.py:75
  10.7 16.7 %collective-permute-start.9 = (bf16[4,5,32,128]{3,2,1,0:T(8,128)(2,1)S(1)}, bf16[4,5,32,128]{3,2,1,0:T(8,128)(2,1)S(1)}, u32[]{:S(2)}, u32[]{:S(2)}) collective-permute-start(bf16[4,5,32,128]{3,2,1,0:T(8,128)(2,1)S(1)} %get-tuple-element.30), channel_id=1, source_target_pairs={{0,12},{1,13},{2,14},{3,15},{4,8},{5,9},{6,10},{7,11},{8,4},{9,5},... | collective-permute-start | bytes 491528 | tf_op jit(solution)/shard_map/ppermute | solution.py:75
  12.4 23.3 %copy-start.9 = (bf16[1,2,16,256,128]{4,3,2,1,0:T(8,128)(2,1)S(1)}, bf16[1,2,16,256,128]{4,3,2,1,0:T(8,128)(2,1)}, u32[]{:S(2)}) copy-start(bf16[1,2,16,256,128]{4,3,2,1,0:T(8,128)(2,1)} %param.7) | copy-start | bytes 6291460
  12.5 13.5 %collective-permute-start.1 = (bf16[4,5,32,128]{3,2,1,0:T(8,128)(2,1)S(1)}, bf16[4,5,32,128]{3,2,1,0:T(8,128)(2,1)S(1)}, u32[]{:S(2)}, u32[]{:S(2)}) collective-permute-start(bf16[4,5,32,128]{3,2,1,0:T(8,128)(2,1)S(1)} %get-tuple-element.33), channel_id=1, source_target_pairs={{0,1},{1,0},{2,3},{3,2},{4,5},{5,4},{6,7},{7,6},{8,9},{9,8},{10,11... | collective-permute-start | bytes 491528 | tf_op jit(solution)/shard_map/ppermute | solution.py:75
  13.7 7.7 %collective-permute-start.3 = (bf16[4,5,32,128]{3,2,1,0:T(8,128)(2,1)S(1)}, bf16[4,5,32,128]{3,2,1,0:T(8,128)(2,1)S(1)}, u32[]{:S(2)}, u32[]{:S(2)}) collective-permute-start(bf16[4,5,32,128]{3,2,1,0:T(8,128)(2,1)S(1)} %get-tuple-element.35), channel_id=1, source_target_pairs={{0,3},{1,2},{2,1},{3,0},{4,7},{5,6},{6,5},{7,4},{8,11},{9,10},{10,... | collective-permute-start | bytes 491528 | tf_op jit(solution)/shard_map/ppermute | solution.py:75
  21.5 4.5 %collective-permute-start.2 = (bf16[4,5,32,128]{3,2,1,0:T(8,128)(2,1)S(1)}, bf16[4,5,32,128]{3,2,1,0:T(8,128)(2,1)S(1)}, u32[]{:S(2)}, u32[]{:S(2)}) collective-permute-start(bf16[4,5,32,128]{3,2,1,0:T(8,128)(2,1)S(1)} %get-tuple-element.34), channel_id=1, source_target_pairs={{0,2},{1,3},{2,0},{3,1},{4,6},{5,7},{6,4},{7,5},{8,10},{9,11},{10,... | collective-permute-start | bytes 491528 | tf_op jit(solution)/shard_map/ppermute | solution.py:75
  26.0 13.8 %collective-permute-start.4 = (bf16[4,5,32,128]{3,2,1,0:T(8,128)(2,1)S(1)}, bf16[4,5,32,128]{3,2,1,0:T(8,128)(2,1)S(1)}, u32[]{:S(2)}, u32[]{:S(2)}) collective-permute-start(bf16[4,5,32,128]{3,2,1,0:T(8,128)(2,1)S(1)} %pad_maximum_fusion), channel_id=1, source_target_pairs={{0,12},{1,13},{2,14},{3,15},{4,8},{5,9},{6,10},{7,11},{8,4},{9,5},... | collective-permute-start | bytes 491528 | tf_op jit(solution)/shard_map/ppermute | solution.py:89
  27.5 5.2 %collective-permute-start.10 = (bf16[4,5,32,128]{3,2,1,0:T(8,128)(2,1)S(1)}, bf16[4,5,32,128]{3,2,1,0:T(8,128)(2,1)S(1)}, u32[]{:S(2)}, u32[]{:S(2)}) collective-permute-start(bf16[4,5,32,128]{3,2,1,0:T(8,128)(2,1)S(1)} %pad_maximum_fusion.3), channel_id=1, source_target_pairs={{0,3},{1,2},{2,1},{3,0},{4,7},{5,6},{6,5},{7,4},{8,11},{9,10},{10,... | collective-permute-start | bytes 491528 | tf_op jit(solution)/shard_map/ppermute | solution.py:89
  28.7 7.0 %collective-permute-start.11 = (bf16[4,5,32,128]{3,2,1,0:T(8,128)(2,1)S(1)}, bf16[4,5,32,128]{3,2,1,0:T(8,128)(2,1)S(1)}, u32[]{:S(2)}, u32[]{:S(2)}) collective-permute-start(bf16[4,5,32,128]{3,2,1,0:T(8,128)(2,1)S(1)} %pad_maximum_fusion.4), channel_id=1, source_target_pairs={{0,2},{1,3},{2,0},{3,1},{4,6},{5,7},{6,4},{7,5},{8,10},{9,11},{10,... | collective-permute-start | bytes 491528 | tf_op jit(solution)/shard_map/ppermute | solution.py:89
  30.1 5.7 %collective-permute-start.12 = (bf16[4,5,32,128]{3,2,1,0:T(8,128)(2,1)S(1)}, bf16[4,5,32,128]{3,2,1,0:T(8,128)(2,1)S(1)}, u32[]{:S(2)}, u32[]{:S(2)}) collective-permute-start(bf16[4,5,32,128]{3,2,1,0:T(8,128)(2,1)S(1)} %pad_maximum_fusion.5), channel_id=1, source_target_pairs={{0,1},{1,0},{2,3},{3,2},{4,5},{5,4},{6,7},{7,6},{8,9},{9,8},{10,11... | collective-permute-start | bytes 491528 | tf_op jit(solution)/shard_map/ppermute | solution.py:89
  30.4 12.6 %collective-permute-start.5 = (bf16[4,5,32,128]{3,2,1,0:T(8,128)(2,1)S(1)}, bf16[4,5,32,128]{3,2,1,0:T(8,128)(2,1)S(1)}, u32[]{:S(2)}, u32[]{:S(2)}) collective-permute-start(bf16[4,5,32,128]{3,2,1,0:T(8,128)(2,1)S(1)} %pad_maximum_fusion.1), channel_id=1, source_target_pairs={{0,8},{1,9},{2,10},{3,11},{4,12},{5,13},{6,14},{7,15},{8,0},{9,1},... | collective-permute-start | bytes 491528 | tf_op jit(solution)/shard_map/ppermute | solution.py:89
  32.7 10.3 %collective-permute-start.6 = (bf16[4,5,32,128]{3,2,1,0:T(8,128)(2,1)S(1)}, bf16[4,5,32,128]{3,2,1,0:T(8,128)(2,1)S(1)}, u32[]{:S(2)}, u32[]{:S(2)}) collective-permute-start(bf16[4,5,32,128]{3,2,1,0:T(8,128)(2,1)S(1)} %pad_maximum_fusion.2), channel_id=1, source_target_pairs={{0,4},{1,5},{2,6},{3,7},{4,0},{5,1},{6,2},{7,3},{8,12},{9,13},{10,... | collective-permute-start | bytes 491528 | tf_op jit(solution)/shard_map/ppermute | solution.py:89
  39.1 0.7 copy-start.2
  39.8 15.9 %collective-permute-start.13 = (bf16[4,5,32,128]{3,2,1,0:T(8,128)(2,1)}, bf16[4,5,32,128]{3,2,1,0:T(8,128)(2,1)S(1)}, u32[]{:S(2)}, u32[]{:S(2)}) collective-permute-start(bf16[4,5,32,128]{3,2,1,0:T(8,128)(2,1)} %get-tuple-element.37), channel_id=1, source_target_pairs={{0,4},{1,5},{2,6},{3,7},{4,0},{5,1},{6,2},{7,3},{8,12},{9,13},{10,... | collective-permute-start | bytes 491528 | tf_op jit(solution)/shard_map/ppermute | solution.py:75
  41.8 13.9 %collective-permute-start.14 = (bf16[4,5,32,128]{3,2,1,0:T(8,128)(2,1)}, bf16[4,5,32,128]{3,2,1,0:T(8,128)(2,1)S(1)}, u32[]{:S(2)}, u32[]{:S(2)}) collective-permute-start(bf16[4,5,32,128]{3,2,1,0:T(8,128)(2,1)} %get-tuple-element.40), channel_id=1, source_target_pairs={{0,8},{1,9},{2,10},{3,11},{4,12},{5,13},{6,14},{7,15},{8,0},{9,1},... | collective-permute-start | bytes 491528 | tf_op jit(solution)/shard_map/ppermute | solution.py:75
  41.8 13.9 %collective-permute-start.15 = (bf16[4,5,32,128]{3,2,1,0:T(8,128)(2,1)}, bf16[4,5,32,128]{3,2,1,0:T(8,128)(2,1)S(1)}, u32[]{:S(2)}, u32[]{:S(2)}) collective-permute-start(bf16[4,5,32,128]{3,2,1,0:T(8,128)(2,1)} %get-tuple-element.41), channel_id=1, source_target_pairs={{0,12},{1,13},{2,14},{3,15},{4,8},{5,9},{6,10},{7,11},{8,4},{9,5},... | collective-permute-start | bytes 491528 | tf_op jit(solution)/shard_map/ppermute | solution.py:75
  47.2 0.7 copy-start.4
  47.9 18.2 %copy-start.1 = (bf16[1,32,1,256,128]{4,3,2,1,0:T(8,128)(2,1)S(1)}, bf16[1,32,1,256,128]{4,3,2,1,0:T(8,128)(2,1)}, u32[]{:S(2)}) copy-start(bf16[1,32,1,256,128]{4,3,2,1,0:T(8,128)(2,1)} %param.6) | copy-start | bytes 6291460
  47.9 18.2 %copy-start.7 = (s32[1,32,16]{1,2,0:T(8,128)S(1)}, s32[1,32,16]{1,2,0:T(8,128)}, u32[]{:S(2)}) copy-start(s32[1,32,16]{1,2,0:T(8,128)} %param.9) | copy-start | bytes 6148
  47.9 29.1 %all-to-all-start = ((bf16[16,5,32,128]{3,2,1,0:T(8,128)(2,1)}), bf16[16,5,32,128]{3,2,1,0:T(8,128)(2,1)S(1)}, u32[]{:S(2)}, u32[]{:S(2)}) async-start(bf16[16,5,32,128]{3,2,1,0:T(8,128)(2,1)} %get-tuple-element.51), calls=%async_computation | async-start | bytes 1310720 | tf_op jit(solution)/shard_map/all_to_all | solution.py:71
  55.8 20.1 %copy-start.3 = (bf16[2,256,256]{2,1,0:T(8,128)(2,1)S(1)}, bf16[2,256,256]{2,1,0:T(8,128)(2,1)}, u32[]{:S(2)}) copy-start(bf16[2,256,256]{2,1,0:T(8,128)(2,1)} %copy-done.2) | copy-start | bytes 786436
  55.8 20.1 %copy-start.5 = (bf16[2,256,256]{2,1,0:T(8,128)(2,1)S(1)}, bf16[2,256,256]{2,1,0:T(8,128)(2,1)}, u32[]{:S(2)}) copy-start(bf16[2,256,256]{2,1,0:T(8,128)(2,1)} %copy-done.4) | copy-start | bytes 786436
  55.8 6.5 %collective-permute-start.16 = (bf16[4,5,32,128]{3,2,1,0:T(8,128)(2,1)S(1)}, bf16[4,5,32,128]{3,2,1,0:T(8,128)(2,1)S(1)}, u32[]{:S(2)}, u32[]{:S(2)}) collective-permute-start(bf16[4,5,32,128]{3,2,1,0:T(8,128)(2,1)S(1)} %pad_maximum_fusion.6), channel_id=1, source_target_pairs={{0,3},{1,2},{2,1},{3,0},{4,7},{5,6},{6,5},{7,4},{8,11},{9,10},{10,... | collective-permute-start | bytes 491528 | tf_op jit(solution)/shard_map/ppermute | solution.py:89
  56.9 9.1 %collective-permute-start.17 = (bf16[4,5,32,128]{3,2,1,0:T(8,128)(2,1)S(1)}, bf16[4,5,32,128]{3,2,1,0:T(8,128)(2,1)S(1)}, u32[]{:S(2)}, u32[]{:S(2)}) collective-permute-start(bf16[4,5,32,128]{3,2,1,0:T(8,128)(2,1)S(1)} %pad_maximum_fusion.7), channel_id=1, source_target_pairs={{0,2},{1,3},{2,0},{3,1},{4,6},{5,7},{6,4},{7,5},{8,10},{9,11},{10,... | collective-permute-start | bytes 491528 | tf_op jit(solution)/shard_map/ppermute | solution.py:89
  58.1 8.0 %collective-permute-start.18 = (bf16[4,5,32,128]{3,2,1,0:T(8,128)(2,1)S(1)}, bf16[4,5,32,128]{3,2,1,0:T(8,128)(2,1)S(1)}, u32[]{:S(2)}, u32[]{:S(2)}) collective-permute-start(bf16[4,5,32,128]{3,2,1,0:T(8,128)(2,1)S(1)} %pad_maximum_fusion.8), channel_id=1, source_target_pairs={{0,1},{1,0},{2,3},{3,2},{4,5},{5,4},{6,7},{7,6},{8,9},{9,8},{10,11... | collective-permute-start | bytes 491528 | tf_op jit(solution)/shard_map/ppermute | solution.py:89
  68.1 10.9 %collective-permute-start.19 = (bf16[256,256]{1,0:T(8,128)(2,1)S(1)}, bf16[256,256]{1,0:T(8,128)(2,1)S(1)}, u32[]{:S(2)}, u32[]{:S(2)}) collective-permute-start(bf16[256,256]{1,0:T(8,128)(2,1)S(1)} %shard_map.74), channel_id=1, source_target_pairs={{0,16},{16,0},{1,17},{17,1},{2,18},{18,2},{3,19},{19,3},{4,20},{20... | collective-permute-start | bytes 393224 | tf_op jit(solution)/shard_map/ppermute | solution.py:323

commit v6 on v5

--- a/solution.py
+++ b/solution.py
@@ -312,10 +312,10 @@
     coded_a = second_hop(first_a, sends_a, way["1a"], tiles)
     coded_b = second_hop(first_b, sends_b, way["1b"], tiles)
     y_a, back_a = middle(coded_a, way["1a"], way["2a"])
+    coded_b = after(coded_b, back_a)
     farthest_b = coded_b[way["1b"][0]]
     back_a = [*back_a[:2], *after(back_a[2:], [farthest_b])]
     first_a, sends_a = exchange(back_a, way["2a"], tiles)
-    coded_b = after(coded_b, back_a)
     y_b, back_b = middle(coded_b, way["1b"], way["2b"])
     first_b, sends_b = exchange(back_b, way["2b"], tiles)
     back_a = second_hop(first_a, sends_a, way["2a"], tiles)

time: 80.2 us -> 84.6 us (1.055)
  waiting for transfers between devices: 21.3 us -> 32.9 us
  starting transfers between devices: 35.1 us -> 27.9 us
    ppermute x18, waiting for transfers between devices: 20.3 us -> 31.9 us  [swap(): return lax.ppermute(block, 'tile', [(i, i ^ offset) for i in range(tiles)])]
    ppermute x1, starting transfers between devices: 7.82 us -> 2.42 us  [per_device(): z_a = lax.ppermute(adjoint(back_a, way['2a']), 'freq', swap)]
    ppermute x18, starting transfers between devices: 20.7 us -> 16.9 us  [swap(): return lax.ppermute(block, 'tile', [(i, i ^ offset) for i in range(tiles)])]
    all_to_all x1, starting transfers between devices: 5.89 us -> 7.74 us  [exchange(): lax.all_to_all(blocks[0], 'tile', split_axis=0, concat_axis=0, tiled=True)]
  transfers between devices with their start and end apart: 21 -> 21, of which waited for: 7 -> 9; matrix products, arithmetic and copies ran while one was open for 2% -> 2% of each run, Pallas kernels for 17% -> 16%
where the time goes in v6:
time: 84.6 us; the launch traced here: 84.2 us
  waiting for transfers between devices  32.9 us (39%)
  starting transfers between devices  27.9 us (33%)
  Pallas kernels  14.9 us (18%)
  local copies, waits for them, and re-layouts  7.4 us (9%)
  between operations  0.93 us (1%)
    ppermute x18, waiting for transfers between devices, swap(): return lax.ppermute(block, 'tile', [(i, i ^ offset) for i in range(tiles)])  31.9 us
    ppermute x18, starting transfers between devices, swap(): return lax.ppermute(block, 'tile', [(i, i ^ offset) for i in range(tiles)])  16.9 us
    all_to_all x1, starting transfers between devices, exchange(): lax.all_to_all(blocks[0], 'tile', split_axis=0, concat_axis=0, tiled=True)  7.74 us
    pallas_call x2, Pallas kernels, middle(): pl.pallas_call(lambda *refs: middle_kernel(route_in, route_out, tiles, *r...  7.54 us
    unnamed x22, local copies, waits for them, and re-layouts  4.45 us
    pallas_call x2, Pallas kernels, adjoint(): pl.pallas_call(lambda *refs: adjoint_kernel(route, tiles, *refs), out_sha...  4.09 us
    pallas_call x2, Pallas kernels, code(): pl.pallas_call(lambda *refs: coded_kernel(route, *refs), out_shape=shapes...  3.14 us
    ppermute x1, starting transfers between devices, per_device(): z_a = lax.ppermute(adjoint(back_a, way['2a']), 'freq', swap)  2.42 us
  transfers between devices with their start and end apart: 21, of which 9 were waited for; matrix products, arithmetic and copies ran while one was open for 2% of the time, Pallas kernels for 16%

profile of v6, /device:TPU:9, one launch (start us, length us, event | category | flops | bytes accessed | tf_op | source)
XLA Modules:
  0.0 84.2 jit_solution(1200768757444571347)
XLA Ops:
  0.6 1.2 %dynamic-slice_bitcast_fusion = (bf16[256,2,128]{2,1,0:T(2,128)(2,1)S(1)}, bf16[256,2,128]{2,1,0:T(2,128)(2,1)S(1)}) fusion(bf16[2,256,2,128]{3,2,1,0:T(2,128)(2,1)} %param.5, s32[]{:T(128)S(6)} %select_n.8, s32[]{:T(128)S(6)} %select_n.7), kind=kLoop, calls=%fused_computation.11 | loop fusion | bytes 524296 | tf_op jit(solution)/shard_map/jit(dynamic_index_in_dim)/squeeze | solution.py:305
  1.8 0.7 collective-permute-start
  2.5 1.0 %collective-permute-done = bf16[256,2,128]{2,1,0:T(2,128)(2,1)S(1)} collective-permute-done((bf16[256,2,128]{2,1,0:T(2,128)(2,1)S(1)}, bf16[256,2,128]{2,1,0:T(2,128)(2,1)S(1)}, u32[]{:S(2)}, u32[]{:S(2)}) %collective-permute-start) | collective-permute-done | bytes 131104 | tf_op jit(solution)/shard_map/ppermute | solution.py:307
  3.5 0.0 copy-start
  3.6 1.6 %copy-done = bf16[1,32,1,256,128]{4,3,2,1,0:T(8,128)(2,1)S(1)} copy-done((bf16[1,32,1,256,128]{4,3,2,1,0:T(8,128)(2,1)S(1)}, bf16[1,32,1,256,128]{4,3,2,1,0:T(8,128)(2,1)}, u32[]{:S(2)}) %copy-start) | copy-done | bytes 2097176
  5.1 0.7 copy-done.6
  5.8 0.7 copy-done.8
  6.5 1.6 %shard_map.68 = (bf16[4,5,32,128]{3,2,1,0:T(8,128)(2,1)S(1)}, bf16[4,5,32,128]{3,2,1,0:T(8,128)(2,1)S(1)}, bf16[4,5,32,128]{3,2,1,0:T(8,128)(2,1)S(1)}, bf16[4,5,32,128]{3,2,1,0:T(8,128)(2,1)S(1)}) custom-call(s32[1]{0:T(128)} %bitcast.1.refs_0_, s32[16,32]{1,0:T(8,128)S(1)} %bitcast.32, f32[16,32]{1,0:T(8,128)S(1)} %bitcast.38, ...), custom_call_target="tpu_custom_call" | custom-call | flops 536870912 | bytes 2228224 | tf_op jit(solution)/shard_map/pallas_call | solution.py:263
  8.1 0.1 collective-permute-start.7
  8.2 2.5 %collective-permute-start.8 = (bf16[4,5,32,128]{3,2,1,0:T(8,128)(2,1)S(1)}, bf16[4,5,32,128]{3,2,1,0:T(8,128)(2,1)S(1)}, u32[]{:S(2)}, u32[]{:S(2)}) collective-permute-start(bf16[4,5,32,128]{3,2,1,0:T(8,128)(2,1)S(1)} %get-tuple-element.29), channel_id=1, source_target_pairs={{0,8},{1,9},{2,10},{3,11},{4,12},{5,13},{6,14},{7,15},{8,0},{9,1},... | collective-permute-start | bytes 491528 | tf_op jit(solution)/shard_map/ppermute | solution.py:75
  10.7 0.2 collective-permute-start.9
  10.9 1.6 %shard_map.69 = (bf16[4,5,32,128]{3,2,1,0:T(8,128)(2,1)S(1)}, bf16[4,5,32,128]{3,2,1,0:T(8,128)(2,1)S(1)}, bf16[4,5,32,128]{3,2,1,0:T(8,128)(2,1)S(1)}, bf16[4,5,32,128]{3,2,1,0:T(8,128)(2,1)S(1)}) custom-call(s32[1]{0:T(128)} %bitcast.1.refs_0_, s32[16,32]{1,0:T(8,128)S(1)} %bitcast.33, f32[16,32]{1,0:T(8,128)S(1)} %bitcast.39, ...), custom_call_target="tpu_custom_call" | custom-call | flops 536870912 | bytes 2228224 | tf_op jit(solution)/shard_map/pallas_call | solution.py:263
  12.4 0.0 copy-start.9
  12.5 1.3 %collective-permute-start.1 = (bf16[4,5,32,128]{3,2,1,0:T(8,128)(2,1)S(1)}, bf16[4,5,32,128]{3,2,1,0:T(8,128)(2,1)S(1)}, u32[]{:S(2)}, u32[]{:S(2)}) collective-permute-start(bf16[4,5,32,128]{3,2,1,0:T(8,128)(2,1)S(1)} %get-tuple-element.33), channel_id=1, source_target_pairs={{0,1},{1,0},{2,3},{3,2},{4,5},{5,4},{6,7},{7,6},{8,9},{9,8},{10,11... | collective-permute-start | bytes 491528 | tf_op jit(solution)/shard_map/ppermute | solution.py:75
  13.7 1.2 %collective-permute-start.2 = (bf16[4,5,32,128]{3,2,1,0:T(8,128)(2,1)S(1)}, bf16[4,5,32,128]{3,2,1,0:T(8,128)(2,1)S(1)}, u32[]{:S(2)}, u32[]{:S(2)}) collective-permute-start(bf16[4,5,32,128]{3,2,1,0:T(8,128)(2,1)S(1)} %get-tuple-element.34), channel_id=1, source_target_pairs={{0,2},{1,3},{2,0},{3,1},{4,6},{5,7},{6,4},{7,5},{8,10},{9,11},{10,... | collective-permute-start | bytes 491528 | tf_op jit(solution)/shard_map/ppermute | solution.py:75
  15.0 0.0 collective-permute-done.7.refs_5_
  15.0 1.1 %collective-permute-start.3 = (bf16[4,5,32,128]{3,2,1,0:T(8,128)(2,1)S(1)}, bf16[4,5,32,128]{3,2,1,0:T(8,128)(2,1)S(1)}, u32[]{:S(2)}, u32[]{:S(2)}) collective-permute-start(bf16[4,5,32,128]{3,2,1,0:T(8,128)(2,1)S(1)} %get-tuple-element.35), channel_id=1, source_target_pairs={{0,3},{1,2},{2,1},{3,0},{4,7},{5,6},{6,5},{7,4},{8,11},{9,10},{10,... | collective-permute-start | bytes 491528 | tf_op jit(solution)/shard_map/ppermute | solution.py:75
  16.1 2.1 %collective-permute-done.8.refs_6_ = bf16[4,5,32,128]{3,2,1,0:T(8,128)(2,1)S(1)} collective-permute-done((bf16[4,5,32,128]{3,2,1,0:T(8,128)(2,1)S(1)}, bf16[4,5,32,128]{3,2,1,0:T(8,128)(2,1)S(1)}, u32[]{:S(2)}, u32[]{:S(2)}) %collective-permute-start.8) | collective-permute-done | bytes 163872 | tf_op jit(solution)/shard_map/ppermute | solution.py:75
  18.2 6.9 %collective-permute-done.9.refs_7_ = bf16[4,5,32,128]{3,2,1,0:T(8,128)(2,1)S(1)} collective-permute-done((bf16[4,5,32,128]{3,2,1,0:T(8,128)(2,1)S(1)}, bf16[4,5,32,128]{3,2,1,0:T(8,128)(2,1)S(1)}, u32[]{:S(2)}, u32[]{:S(2)}) %collective-permute-start.9) | collective-permute-done | bytes 163872 | tf_op jit(solution)/shard_map/ppermute | solution.py:75
  25.1 1.3 %collective-permute-start.12 = (bf16[4,5,32,128]{3,2,1,0:T(8,128)(2,1)S(1)}, bf16[4,5,32,128]{3,2,1,0:T(8,128)(2,1)S(1)}, u32[]{:S(2)}, u32[]{:S(2)}) collective-permute-start(bf16[4,5,32,128]{3,2,1,0:T(8,128)(2,1)S(1)} %pad_maximum_fusion.5), channel_id=1, source_target_pairs={{0,1},{1,0},{2,3},{3,2},{4,5},{5,4},{6,7},{7,6},{8,9},{9,8},{10,11... | collective-permute-start | bytes 491528 | tf_op jit(solution)/shard_map/ppermute | solution.py:89
  26.4 1.3 %collective-permute-start.11 = (bf16[4,5,32,128]{3,2,1,0:T(8,128)(2,1)S(1)}, bf16[4,5,32,128]{3,2,1,0:T(8,128)(2,1)S(1)}, u32[]{:S(2)}, u32[]{:S(2)}) collective-permute-start(bf16[4,5,32,128]{3,2,1,0:T(8,128)(2,1)S(1)} %pad_maximum_fusion.4), channel_id=1, source_target_pairs={{0,2},{1,3},{2,0},{3,1},{4,6},{5,7},{6,4},{7,5},{8,10},{9,11},{10,... | collective-permute-start | bytes 491528 | tf_op jit(solution)/shard_map/ppermute | solution.py:89
  27.8 0.0 collective-permute-done.1.refs_5_
  27.8 0.3 collective-permute-start.10
  28.1 0.0 collective-permute-done.2.refs_6_
  28.1 0.0 collective-permute-done.3.refs_7_
  28.1 0.1 collective-permute-start.6
  28.3 2.5 %collective-permute-start.5 = (bf16[4,5,32,128]{3,2,1,0:T(8,128)(2,1)S(1)}, bf16[4,5,32,128]{3,2,1,0:T(8,128)(2,1)S(1)}, u32[]{:S(2)}, u32[]{:S(2)}) collective-permute-start(bf16[4,5,32,128]{3,2,1,0:T(8,128)(2,1)S(1)} %pad_maximum_fusion.1), channel_id=1, source_target_pairs={{0,8},{1,9},{2,10},{3,11},{4,12},{5,13},{6,14},{7,15},{8,0},{9,1},... | collective-permute-start | bytes 491528 | tf_op jit(solution)/shard_map/ppermute | solution.py:89
  30.8 0.0 collective-permute-done.12.refs_10_
  30.8 0.2 collective-permute-start.4
  31.1 0.0 collective-permute-done.11.refs_9_
  31.1 3.5 %collective-permute-done.10.refs_8_ = bf16[4,5,32,128]{3,2,1,0:T(8,128)(2,1)S(1)} collective-permute-done((bf16[4,5,32,128]{3,2,1,0:T(8,128)(2,1)S(1)}, bf16[4,5,32,128]{3,2,1,0:T(8,128)(2,1)S(1)}, u32[]{:S(2)}, u32[]{:S(2)}) %collective-permute-start.10) | collective-permute-done | bytes 163872 | tf_op jit(solution)/shard_map/ppermute | solution.py:89
  34.6 0.0 copy-done.9
  34.6 3.4 %shard_map.70 = (bf16[2,256,256]{2,1,0:T(8,128)(2,1)S(1)}, bf16[4,5,32,128]{3,2,1,0:T(8,128)(2,1)S(1)}, bf16[4,5,32,128]{3,2,1,0:T(8,128)(2,1)}, bf16[4,5,32,128]{3,2,1,0:T(8,128)(2,1)}, bf16[4,5,32,128]{3,2,1,0:T(8,128)(2,1)}) custom-call(s32[1]{0:T(128)} %bitcast.1.refs_0_, s32[16,32]{1,0:T(8,128)S(1)} %bitcast.34, f32[16,32]{1,0:T(8,128)S(1)} %bitcast.40, ...), custom_call_target="tpu_custom_call" | custom-call | flops 10737418240 | bytes 32440320 | tf_op jit(solution)/shard_map/pallas_call | solution.py:274
  38.0 0.7 copy-done.2
  38.7 0.0 collective-permute-start.13
  38.7 0.0 collective-permute-done.6.refs_10_
  38.7 0.0 collective-permute-done.5.refs_9_
  38.7 5.4 %collective-permute-done.4.refs_8_ = bf16[4,5,32,128]{3,2,1,0:T(8,128)(2,1)S(1)} collective-permute-done((bf16[4,5,32,128]{3,2,1,0:T(8,128)(2,1)S(1)}, bf16[4,5,32,128]{3,2,1,0:T(8,128)(2,1)S(1)}, u32[]{:S(2)}, u32[]{:S(2)}) %collective-permute-start.4) | collective-permute-done | bytes 163872 | tf_op jit(solution)/shard_map/ppermute | solution.py:89
  44.1 0.0 collective-permute-start.14
  44.1 2.1 %collective-permute-start.15 = (bf16[4,5,32,128]{3,2,1,0:T(8,128)(2,1)}, bf16[4,5,32,128]{3,2,1,0:T(8,128)(2,1)S(1)}, u32[]{:S(2)}, u32[]{:S(2)}) collective-permute-start(bf16[4,5,32,128]{3,2,1,0:T(8,128)(2,1)} %get-tuple-element.51), channel_id=1, source_target_pairs={{0,12},{1,13},{2,14},{3,15},{4,8},{5,9},{6,10},{7,11},{8,4},{9,5},... | collective-permute-start | bytes 491528 | tf_op jit(solution)/shard_map/ppermute | solution.py:75
  46.3 4.2 %shard_map.71 = (bf16[2,256,256]{2,1,0:T(8,128)(2,1)S(1)}, bf16[16,5,32,128]{3,2,1,0:T(8,128)(2,1)}) custom-call(s32[1]{0:T(128)} %bitcast.1.refs_0_, s32[16,32]{1,0:T(8,128)S(1)} %bitcast.35, f32[16,32]{1,0:T(8,128)S(1)} %bitcast.41, bf16[2,16,256,128]{3,2,1,0:T(8,128)(2,1)S(1)} %bitcast.43, bf16[4,5,32,128]{3,2,1,0:T(8,128)(2,1)S(1)} %get-tuple-element.40.refs_4_, ...), custom_call_target="tpu_custom_call" | custom-call | flops 10737418240 | bytes 32440320 | tf_op jit(solution)/shard_map/pallas_call | solution.py:274
  50.4 0.7 copy-done.4
  51.1 7.7 %all-to-all-start = ((bf16[16,5,32,128]{3,2,1,0:T(8,128)(2,1)}), bf16[16,5,32,128]{3,2,1,0:T(8,128)(2,1)S(1)}, u32[]{:S(2)}, u32[]{:S(2)}) async-start(bf16[16,5,32,128]{3,2,1,0:T(8,128)(2,1)} %get-tuple-element.49), calls=%async_computation | async-start | bytes 1310720 | tf_op jit(solution)/shard_map/all_to_all | solution.py:71
  58.9 0.0 collective-permute-done.14.refs_5_
  58.9 2.3 %collective-permute-done.15.refs_6_ = bf16[4,5,32,128]{3,2,1,0:T(8,128)(2,1)S(1)} collective-permute-done((bf16[4,5,32,128]{3,2,1,0:T(8,128)(2,1)}, bf16[4,5,32,128]{3,2,1,0:T(8,128)(2,1)S(1)}, u32[]{:S(2)}, u32[]{:S(2)}) %collective-permute-start.15) | collective-permute-done | bytes 163872 | tf_op jit(solution)/shard_map/ppermute | solution.py:75
  61.2 0.0 collective-permute-done.13.refs_4_
  61.3 0.0 copy-start.3
  61.3 0.0 copy-start.5
  61.3 1.2 %collective-permute-start.18 = (bf16[4,5,32,128]{3,2,1,0:T(8,128)(2,1)S(1)}, bf16[4,5,32,128]{3,2,1,0:T(8,128)(2,1)S(1)}, u32[]{:S(2)}, u32[]{:S(2)}) collective-permute-start(bf16[4,5,32,128]{3,2,1,0:T(8,128)(2,1)S(1)} %pad_maximum_fusion.8), channel_id=1, source_target_pairs={{0,1},{1,0},{2,3},{3,2},{4,5},{5,4},{6,7},{7,6},{8,9},{9,8},{10,11... | collective-permute-start | bytes 491528 | tf_op jit(solution)/shard_map/ppermute | solution.py:89
  62.5 1.2 %collective-permute-start.17 = (bf16[4,5,32,128]{3,2,1,0:T(8,128)(2,1)S(1)}, bf16[4,5,32,128]{3,2,1,0:T(8,128)(2,1)S(1)}, u32[]{:S(2)}, u32[]{:S(2)}) collective-permute-start(bf16[4,5,32,128]{3,2,1,0:T(8,128)(2,1)S(1)} %pad_maximum_fusion.7), channel_id=1, source_target_pairs={{0,2},{1,3},{2,0},{3,1},{4,6},{5,7},{6,4},{7,5},{8,10},{9,11},{10,... | collective-permute-start | bytes 491528 | tf_op jit(solution)/shard_map/ppermute | solution.py:89
  63.8 0.4 collective-permute-start.16
  64.2 4.9 %collective-permute-done.18.refs_9_ = bf16[4,5,32,128]{3,2,1,0:T(8,128)(2,1)S(1)} collective-permute-done((bf16[4,5,32,128]{3,2,1,0:T(8,128)(2,1)S(1)}, bf16[4,5,32,128]{3,2,1,0:T(8,128)(2,1)S(1)}, u32[]{:S(2)}, u32[]{:S(2)}) %collective-permute-start.18) | collective-permute-done | bytes 163872 | tf_op jit(solution)/shard_map/ppermute | solution.py:89
  69.1 1.6 %collective-permute-done.17.refs_8_ = bf16[4,5,32,128]{3,2,1,0:T(8,128)(2,1)S(1)} collective-permute-done((bf16[4,5,32,128]{3,2,1,0:T(8,128)(2,1)S(1)}, bf16[4,5,32,128]{3,2,1,0:T(8,128)(2,1)S(1)}, u32[]{:S(2)}, u32[]{:S(2)}) %collective-permute-start.17) | collective-permute-done | bytes 163872 | tf_op jit(solution)/shard_map/ppermute | solution.py:89
  70.7 5.2 %collective-permute-done.16.refs_7_ = bf16[4,5,32,128]{3,2,1,0:T(8,128)(2,1)S(1)} collective-permute-done((bf16[4,5,32,128]{3,2,1,0:T(8,128)(2,1)S(1)}, bf16[4,5,32,128]{3,2,1,0:T(8,128)(2,1)S(1)}, u32[]{:S(2)}, u32[]{:S(2)}) %collective-permute-start.16) | collective-permute-done | bytes 163872 | tf_op jit(solution)/shard_map/ppermute | solution.py:89
  75.8 0.0 copy-done.1
  75.8 2.0 %shard_map.74 = bf16[256,256]{1,0:T(8,128)(2,1)S(1)} custom-call(s32[1]{0:T(128)} %bitcast.1.refs_0_, s32[16,32]{1,0:T(8,128)S(1)} %bitcast.36, bf16[32,256,128]{2,1,0:T(8,128)(2,1)S(1)} %bitcast.26, bf16[4,5,32,128]{3,2,1,0:T(8,128)(2,1)S(1)} %get-tuple-element.36.refs_3_, bf16[4,5,32,128]{3,2,1,0:T(8,128)(2,1)S(1)} %collective-permute-done.13.refs_4_, ...), custom_call_target="tpu_custom_call" | custom-call | flops 536870912 | bytes 3244032 | tf_op jit(solution)/shard_map/pallas_call | solution.py:286
  77.9 2.4 %collective-permute-start.19 = (bf16[256,256]{1,0:T(8,128)(2,1)S(1)}, bf16[256,256]{1,0:T(8,128)(2,1)S(1)}, u32[]{:S(2)}, u32[]{:S(2)}) collective-permute-start(bf16[256,256]{1,0:T(8,128)(2,1)S(1)} %shard_map.74), channel_id=1, source_target_pairs={{0,16},{16,0},{1,17},{17,1},{2,18},{18,2},{3,19},{19,3},{4,20},{20... | collective-permute-start | bytes 393224 | tf_op jit(solution)/shard_map/ppermute | solution.py:323
  80.3 0.0 copy-done.5
  80.3 0.1 shard_map.72
  80.4 0.9 %reshape.38 = bf16[1,512,2,256]{3,2,1,0:T(2,128)(2,1)} reshape(bf16[512,512]{1,0:T(8,128)(2,1)S(1)} %shard_map.72) | data formatting | bytes 1048576 | tf_op jit(solution)/shard_map/reshape | solution.py:325
  81.3 0.0 all-to-all-done.refs_3_
  81.3 2.1 %shard_map.73.first_ref = bf16[256,256]{1,0:T(8,128)(2,1)S(1)} custom-call(s32[1]{0:T(128)} %bitcast.1.refs_0_, s32[16,32]{1,0:T(8,128)S(1)} %bitcast.37, bf16[32,256,128]{2,1,0:T(8,128)(2,1)S(1)} %bitcast.27, bf16[16,5,32,128]{3,2,1,0:T(8,128)(2,1)S(1)} %all-to-all-done.refs_3_), custom_call_target="tpu_custom_call" | custom-call | flops 536870912 | bytes 2752512 | tf_op jit(solution)/shard_map/pallas_call | solution.py:286
  83.4 0.0 collective-permute-done.19.second_ref
  83.4 0.8 reshape.39
  (32 shorter events, 0.4 us)
Async XLA Ops:
  1.8 1.7 %collective-permute-start = (bf16[256,2,128]{2,1,0:T(2,128)(2,1)S(1)}, bf16[256,2,128]{2,1,0:T(2,128)(2,1)S(1)}, u32[]{:S(2)}, u32[]{:S(2)}) collective-permute-start(bf16[256,2,128]{2,1,0:T(2,128)(2,1)S(1)} %get-tuple-element.52), channel_id=1, source_target_pairs={{0,16},{16,0},{1,17},{17,1},{2,18},{18,2},{3,19},{19,3},{4,20},{20... | collective-permute-start | bytes 393224 | tf_op jit(solution)/shard_map/ppermute | solution.py:307
  3.5 1.6 %copy-start = (bf16[1,32,1,256,128]{4,3,2,1,0:T(8,128)(2,1)S(1)}, bf16[1,32,1,256,128]{4,3,2,1,0:T(8,128)(2,1)}, u32[]{:S(2)}) copy-start(bf16[1,32,1,256,128]{4,3,2,1,0:T(8,128)(2,1)} %param.6) | copy-start | bytes 6291460
  5.1 0.7 copy-start.6
  5.8 0.7 copy-start.8
  8.1 6.9 %collective-permute-start.7 = (bf16[4,5,32,128]{3,2,1,0:T(8,128)(2,1)S(1)}, bf16[4,5,32,128]{3,2,1,0:T(8,128)(2,1)S(1)}, u32[]{:S(2)}, u32[]{:S(2)}) collective-permute-start(bf16[4,5,32,128]{3,2,1,0:T(8,128)(2,1)S(1)} %get-tuple-element.28), channel_id=1, source_target_pairs={{0,4},{1,5},{2,6},{3,7},{4,0},{5,1},{6,2},{7,3},{8,12},{9,13},{10,... | collective-permute-start | bytes 491528 | tf_op jit(solution)/shard_map/ppermute | solution.py:75
  8.2 10.0 %collective-permute-start.8 = (bf16[4,5,32,128]{3,2,1,0:T(8,128)(2,1)S(1)}, bf16[4,5,32,128]{3,2,1,0:T(8,128)(2,1)S(1)}, u32[]{:S(2)}, u32[]{:S(2)}) collective-permute-start(bf16[4,5,32,128]{3,2,1,0:T(8,128)(2,1)S(1)} %get-tuple-element.29), channel_id=1, source_target_pairs={{0,8},{1,9},{2,10},{3,11},{4,12},{5,13},{6,14},{7,15},{8,0},{9,1},... | collective-permute-start | bytes 491528 | tf_op jit(solution)/shard_map/ppermute | solution.py:75
  10.7 14.4 %collective-permute-start.9 = (bf16[4,5,32,128]{3,2,1,0:T(8,128)(2,1)S(1)}, bf16[4,5,32,128]{3,2,1,0:T(8,128)(2,1)S(1)}, u32[]{:S(2)}, u32[]{:S(2)}) collective-permute-start(bf16[4,5,32,128]{3,2,1,0:T(8,128)(2,1)S(1)} %get-tuple-element.30), channel_id=1, source_target_pairs={{0,12},{1,13},{2,14},{3,15},{4,8},{5,9},{6,10},{7,11},{8,4},{9,5},... | collective-permute-start | bytes 491528 | tf_op jit(solution)/shard_map/ppermute | solution.py:75
  12.4 22.2 %copy-start.9 = (bf16[1,2,16,256,128]{4,3,2,1,0:T(8,128)(2,1)S(1)}, bf16[1,2,16,256,128]{4,3,2,1,0:T(8,128)(2,1)}, u32[]{:S(2)}) copy-start(bf16[1,2,16,256,128]{4,3,2,1,0:T(8,128)(2,1)} %param.7) | copy-start | bytes 6291460
  12.5 15.3 %collective-permute-start.1 = (bf16[4,5,32,128]{3,2,1,0:T(8,128)(2,1)S(1)}, bf16[4,5,32,128]{3,2,1,0:T(8,128)(2,1)S(1)}, u32[]{:S(2)}, u32[]{:S(2)}) collective-permute-start(bf16[4,5,32,128]{3,2,1,0:T(8,128)(2,1)S(1)} %get-tuple-element.33), channel_id=1, source_target_pairs={{0,1},{1,0},{2,3},{3,2},{4,5},{5,4},{6,7},{7,6},{8,9},{9,8},{10,11... | collective-permute-start | bytes 491528 | tf_op jit(solution)/shard_map/ppermute | solution.py:75
  13.7 14.3 %collective-permute-start.2 = (bf16[4,5,32,128]{3,2,1,0:T(8,128)(2,1)S(1)}, bf16[4,5,32,128]{3,2,1,0:T(8,128)(2,1)S(1)}, u32[]{:S(2)}, u32[]{:S(2)}) collective-permute-start(bf16[4,5,32,128]{3,2,1,0:T(8,128)(2,1)S(1)} %get-tuple-element.34), channel_id=1, source_target_pairs={{0,2},{1,3},{2,0},{3,1},{4,6},{5,7},{6,4},{7,5},{8,10},{9,11},{10,... | collective-permute-start | bytes 491528 | tf_op jit(solution)/shard_map/ppermute | solution.py:75
  15.0 13.1 %collective-permute-start.3 = (bf16[4,5,32,128]{3,2,1,0:T(8,128)(2,1)S(1)}, bf16[4,5,32,128]{3,2,1,0:T(8,128)(2,1)S(1)}, u32[]{:S(2)}, u32[]{:S(2)}) collective-permute-start(bf16[4,5,32,128]{3,2,1,0:T(8,128)(2,1)S(1)} %get-tuple-element.35), channel_id=1, source_target_pairs={{0,3},{1,2},{2,1},{3,0},{4,7},{5,6},{6,5},{7,4},{8,11},{9,10},{10,... | collective-permute-start | bytes 491528 | tf_op jit(solution)/shard_map/ppermute | solution.py:75
  25.1 5.7 %collective-permute-start.12 = (bf16[4,5,32,128]{3,2,1,0:T(8,128)(2,1)S(1)}, bf16[4,5,32,128]{3,2,1,0:T(8,128)(2,1)S(1)}, u32[]{:S(2)}, u32[]{:S(2)}) collective-permute-start(bf16[4,5,32,128]{3,2,1,0:T(8,128)(2,1)S(1)} %pad_maximum_fusion.5), channel_id=1, source_target_pairs={{0,1},{1,0},{2,3},{3,2},{4,5},{5,4},{6,7},{7,6},{8,9},{9,8},{10,11... | collective-permute-start | bytes 491528 | tf_op jit(solution)/shard_map/ppermute | solution.py:89
  26.4 4.6 %collective-permute-start.11 = (bf16[4,5,32,128]{3,2,1,0:T(8,128)(2,1)S(1)}, bf16[4,5,32,128]{3,2,1,0:T(8,128)(2,1)S(1)}, u32[]{:S(2)}, u32[]{:S(2)}) collective-permute-start(bf16[4,5,32,128]{3,2,1,0:T(8,128)(2,1)S(1)} %pad_maximum_fusion.4), channel_id=1, source_target_pairs={{0,2},{1,3},{2,0},{3,1},{4,6},{5,7},{6,4},{7,5},{8,10},{9,11},{10,... | collective-permute-start | bytes 491528 | tf_op jit(solution)/shard_map/ppermute | solution.py:89
  27.8 6.8 %collective-permute-start.10 = (bf16[4,5,32,128]{3,2,1,0:T(8,128)(2,1)S(1)}, bf16[4,5,32,128]{3,2,1,0:T(8,128)(2,1)S(1)}, u32[]{:S(2)}, u32[]{:S(2)}) collective-permute-start(bf16[4,5,32,128]{3,2,1,0:T(8,128)(2,1)S(1)} %pad_maximum_fusion.3), channel_id=1, source_target_pairs={{0,3},{1,2},{2,1},{3,0},{4,7},{5,6},{6,5},{7,4},{8,11},{9,10},{10,... | collective-permute-start | bytes 491528 | tf_op jit(solution)/shard_map/ppermute | solution.py:89
  28.1 10.5 %collective-permute-start.6 = (bf16[4,5,32,128]{3,2,1,0:T(8,128)(2,1)S(1)}, bf16[4,5,32,128]{3,2,1,0:T(8,128)(2,1)S(1)}, u32[]{:S(2)}, u32[]{:S(2)}) collective-permute-start(bf16[4,5,32,128]{3,2,1,0:T(8,128)(2,1)S(1)} %pad_maximum_fusion.2), channel_id=1, source_target_pairs={{0,4},{1,5},{2,6},{3,7},{4,0},{5,1},{6,2},{7,3},{8,12},{9,13},{10,... | collective-permute-start | bytes 491528 | tf_op jit(solution)/shard_map/ppermute | solution.py:89
  28.3 10.4 %collective-permute-start.5 = (bf16[4,5,32,128]{3,2,1,0:T(8,128)(2,1)S(1)}, bf16[4,5,32,128]{3,2,1,0:T(8,128)(2,1)S(1)}, u32[]{:S(2)}, u32[]{:S(2)}) collective-permute-start(bf16[4,5,32,128]{3,2,1,0:T(8,128)(2,1)S(1)} %pad_maximum_fusion.1), channel_id=1, source_target_pairs={{0,8},{1,9},{2,10},{3,11},{4,12},{5,13},{6,14},{7,15},{8,0},{9,1},... | collective-permute-start | bytes 491528 | tf_op jit(solution)/shard_map/ppermute | solution.py:89
  30.8 13.3 %collective-permute-start.4 = (bf16[4,5,32,128]{3,2,1,0:T(8,128)(2,1)S(1)}, bf16[4,5,32,128]{3,2,1,0:T(8,128)(2,1)S(1)}, u32[]{:S(2)}, u32[]{:S(2)}) collective-permute-start(bf16[4,5,32,128]{3,2,1,0:T(8,128)(2,1)S(1)} %pad_maximum_fusion), channel_id=1, source_target_pairs={{0,12},{1,13},{2,14},{3,15},{4,8},{5,9},{6,10},{7,11},{8,4},{9,5},... | collective-permute-start | bytes 491528 | tf_op jit(solution)/shard_map/ppermute | solution.py:89
  38.0 0.7 copy-start.2
  38.7 22.5 %collective-permute-start.13 = (bf16[4,5,32,128]{3,2,1,0:T(8,128)(2,1)}, bf16[4,5,32,128]{3,2,1,0:T(8,128)(2,1)S(1)}, u32[]{:S(2)}, u32[]{:S(2)}) collective-permute-start(bf16[4,5,32,128]{3,2,1,0:T(8,128)(2,1)} %get-tuple-element.37), channel_id=1, source_target_pairs={{0,4},{1,5},{2,6},{3,7},{4,0},{5,1},{6,2},{7,3},{8,12},{9,13},{10,... | collective-permute-start | bytes 491528 | tf_op jit(solution)/shard_map/ppermute | solution.py:75
  44.1 14.7 %collective-permute-start.14 = (bf16[4,5,32,128]{3,2,1,0:T(8,128)(2,1)}, bf16[4,5,32,128]{3,2,1,0:T(8,128)(2,1)S(1)}, u32[]{:S(2)}, u32[]{:S(2)}) collective-permute-start(bf16[4,5,32,128]{3,2,1,0:T(8,128)(2,1)} %get-tuple-element.50), channel_id=1, source_target_pairs={{0,8},{1,9},{2,10},{3,11},{4,12},{5,13},{6,14},{7,15},{8,0},{9,1},... | collective-permute-start | bytes 491528 | tf_op jit(solution)/shard_map/ppermute | solution.py:75
  44.1 17.0 %collective-permute-start.15 = (bf16[4,5,32,128]{3,2,1,0:T(8,128)(2,1)}, bf16[4,5,32,128]{3,2,1,0:T(8,128)(2,1)S(1)}, u32[]{:S(2)}, u32[]{:S(2)}) collective-permute-start(bf16[4,5,32,128]{3,2,1,0:T(8,128)(2,1)} %get-tuple-element.51), channel_id=1, source_target_pairs={{0,12},{1,13},{2,14},{3,15},{4,8},{5,9},{6,10},{7,11},{8,4},{9,5},... | collective-permute-start | bytes 491528 | tf_op jit(solution)/shard_map/ppermute | solution.py:75
  50.4 0.7 copy-start.4
  51.1 24.7 %copy-start.1 = (bf16[1,32,1,256,128]{4,3,2,1,0:T(8,128)(2,1)S(1)}, bf16[1,32,1,256,128]{4,3,2,1,0:T(8,128)(2,1)}, u32[]{:S(2)}) copy-start(bf16[1,32,1,256,128]{4,3,2,1,0:T(8,128)(2,1)} %param.6) | copy-start | bytes 6291460
  51.1 24.7 %copy-start.7 = (s32[1,32,16]{1,2,0:T(8,128)S(1)}, s32[1,32,16]{1,2,0:T(8,128)}, u32[]{:S(2)}) copy-start(s32[1,32,16]{1,2,0:T(8,128)} %param.9) | copy-start | bytes 6148
  51.1 30.2 %all-to-all-start = ((bf16[16,5,32,128]{3,2,1,0:T(8,128)(2,1)}), bf16[16,5,32,128]{3,2,1,0:T(8,128)(2,1)S(1)}, u32[]{:S(2)}, u32[]{:S(2)}) async-start(bf16[16,5,32,128]{3,2,1,0:T(8,128)(2,1)} %get-tuple-element.49), calls=%async_computation | async-start | bytes 1310720 | tf_op jit(solution)/shard_map/all_to_all | solution.py:71
  61.3 19.0 %copy-start.3 = (bf16[2,256,256]{2,1,0:T(8,128)(2,1)S(1)}, bf16[2,256,256]{2,1,0:T(8,128)(2,1)}, u32[]{:S(2)}) copy-start(bf16[2,256,256]{2,1,0:T(8,128)(2,1)} %copy-done.2) | copy-start | bytes 786436
  61.3 19.0 %copy-start.5 = (bf16[2,256,256]{2,1,0:T(8,128)(2,1)S(1)}, bf16[2,256,256]{2,1,0:T(8,128)(2,1)}, u32[]{:S(2)}) copy-start(bf16[2,256,256]{2,1,0:T(8,128)(2,1)} %copy-done.4) | copy-start | bytes 786436
  61.3 7.8 %collective-permute-start.18 = (bf16[4,5,32,128]{3,2,1,0:T(8,128)(2,1)S(1)}, bf16[4,5,32,128]{3,2,1,0:T(8,128)(2,1)S(1)}, u32[]{:S(2)}, u32[]{:S(2)}) collective-permute-start(bf16[4,5,32,128]{3,2,1,0:T(8,128)(2,1)S(1)} %pad_maximum_fusion.8), channel_id=1, source_target_pairs={{0,1},{1,0},{2,3},{3,2},{4,5},{5,4},{6,7},{7,6},{8,9},{9,8},{10,11... | collective-permute-start | bytes 491528 | tf_op jit(solution)/shard_map/ppermute | solution.py:89
  62.5 8.1 %collective-permute-start.17 = (bf16[4,5,32,128]{3,2,1,0:T(8,128)(2,1)S(1)}, bf16[4,5,32,128]{3,2,1,0:T(8,128)(2,1)S(1)}, u32[]{:S(2)}, u32[]{:S(2)}) collective-permute-start(bf16[4,5,32,128]{3,2,1,0:T(8,128)(2,1)S(1)} %pad_maximum_fusion.7), channel_id=1, source_target_pairs={{0,2},{1,3},{2,0},{3,1},{4,6},{5,7},{6,4},{7,5},{8,10},{9,11},{10,... | collective-permute-start | bytes 491528 | tf_op jit(solution)/shard_map/ppermute | solution.py:89
  63.8 12.0 %collective-permute-start.16 = (bf16[4,5,32,128]{3,2,1,0:T(8,128)(2,1)S(1)}, bf16[4,5,32,128]{3,2,1,0:T(8,128)(2,1)S(1)}, u32[]{:S(2)}, u32[]{:S(2)}) collective-permute-start(bf16[4,5,32,128]{3,2,1,0:T(8,128)(2,1)S(1)} %pad_maximum_fusion.6), channel_id=1, source_target_pairs={{0,3},{1,2},{2,1},{3,0},{4,7},{5,6},{6,5},{7,4},{8,11},{9,10},{10,... | collective-permute-start | bytes 491528 | tf_op jit(solution)/shard_map/ppermute | solution.py:89
  77.9 5.5 %collective-permute-start.19 = (bf16[256,256]{1,0:T(8,128)(2,1)S(1)}, bf16[256,256]{1,0:T(8,128)(2,1)S(1)}, u32[]{:S(2)}, u32[]{:S(2)}) collective-permute-start(bf16[256,256]{1,0:T(8,128)(2,1)S(1)} %shard_map.74), channel_id=1, source_target_pairs={{0,16},{16,0},{1,17},{17,1},{2,18},{18,2},{3,19},{19,3},{4,20},{20... | collective-permute-start | bytes 393224 | tf_op jit(solution)/shard_map/ppermute | solution.py:323
